TPU v7x, 32 devices: a whole 2x2x4 slice. The times are simulated.
32 devices in a mesh: dp: 8 (over y, x, core), tensor: 4 (over z).
Axes of the slice: x: 2, y: 2, z: 4, core: 2. Of those that a mesh axis runs over, the one named last changes fastest.
Arguments:
- tokens: bfloat16 [8192, 2048], P(('dp', 'tensor')), may hold values from -6 to 6
- segments: int32 [8192], P('dp'), may hold values from 0 to 2, as said below
- positions: int32 [8192], P('dp'), may hold values from 0 to 2047, as said below
- attn_gain: bfloat16 [2048], P('dp'), may hold values from 0.099609375 to 1.8984375
- w_query: bfloat16 [2048, 2048], P('dp', 'tensor'), may hold values from -0.125 to 0.125
- w_key: bfloat16 [2048, 512], P('dp', 'tensor'), may hold values from -0.125 to 0.125
- w_value: bfloat16 [2048, 512], P('dp', 'tensor'), may hold values from -0.125 to 0.125
- w_out: bfloat16 [2048, 2048], P('tensor', 'dp'), may hold values from -1.5 to 1.5
- mlp_gain: bfloat16 [2048], P('dp'), may hold values from 0.099609375 to 1.8984375
- w_gate: bfloat16 [2048, 8192], P('dp', 'tensor'), may hold values from -0.125 to 0.125
- w_up: bfloat16 [2048, 8192], P('dp', 'tensor'), may hold values from -0.125 to 0.125
- w_down: bfloat16 [8192, 2048], P('tensor', 'dp'), may hold values from -0.0625 to 0.0625
- grad_out: bfloat16 [8192, 2048], P(('dp', 'tensor')), may hold values from -6 to 6
Outputs:
- block_out: bfloat16 [8192, 2048], P(('dp', 'tensor'))
- grad_tokens: float32 [8192, 2048], P(('dp', 'tensor'))
- grad_attn_gain: float32 [2048], P('dp')
- grad_query: float32 [2048, 2048], P('dp', 'tensor')
- grad_key: float32 [2048, 512], P('dp', 'tensor')
- grad_value: float32 [2048, 512], P('dp', 'tensor')
- grad_out_proj: float32 [2048, 2048], P('tensor', 'dp')
- grad_mlp_gain: float32 [2048], P('dp')
- grad_gate: float32 [2048, 8192], P('dp', 'tensor')
- grad_up: float32 [2048, 8192], P('dp', 'tensor')
- grad_down: float32 [8192, 2048], P('tensor', 'dp')
Inputs may be any that keep to these rules, and one draw needn't show every extreme that they name: `segments`: each sequence of 1024 tokens holds three documents numbered 0, 1, 2 in order: document 0 ends before token 256 and document 1 ends after token 768 and at least 64 tokens before the sequence's end. Within a document positions rise by one from token to token; each document's first position is below 2048.
All inputs are finite; a program needn't handle non-finite values.
Results may differ from a plain program's by a relative error of at most 0.013.
Values may be sent and summed in bfloat16 or wider, within the bound.
A program may use at most 256 MiB of HBM per device.

v0:
```python
from functools import partial
import math

import jax
import jax.numpy as jnp
from jax import lax
from jax.sharding import PartitionSpec as P

HD = 64


EPSILON = 1e-05
MASKED = -1e30


def frequencies(head_size):
    inverse = 1.0 / 500000.0 ** (jnp.arange(head_size // 2, dtype=jnp.float32) * 2.0 / head_size)
    wavelength = 2.0 * math.pi / inverse
    smooth = (8192.0 / wavelength - 1.0) / 3.0
    blended = (1.0 - smooth) * inverse / 32.0 + smooth * inverse
    return jnp.where(
        wavelength > 8192.0, inverse / 32.0, jnp.where(wavelength < 2048.0, inverse, blended)
    )


def tables(places, head_size):
    angles = places.astype(jnp.float32)[:, None] * frequencies(head_size)[None, :]
    cosine_table = jnp.cos(angles)
    sine_table = jnp.sin(angles)
    return (
        jnp.concatenate([cosine_table, cosine_table], -1),
        jnp.concatenate([sine_table, sine_table], -1),
    )


def rotate(values, cosine_table, sine_table, sign):
    middle = values.shape[-1] // 2
    turned = jnp.concatenate([-values[..., middle:], values[..., :middle]], axis=-1)
    return values * cosine_table + sign * turned * sine_table


def over_rows(left_side, right_side):
    return lax.dot_general(
        left_side, right_side, (((0,), (0,)), ((), ())), preferred_element_type=jnp.float32
    )


def against(left_side, right_side):
    return lax.dot_general(
        left_side, right_side, (((1,), (1,)), ((), ())), preferred_element_type=jnp.float32
    )


def block_scores(query_block, offset, key_rows, segments):
    length = query_block.shape[0]
    raw_scores = jnp.einsum(
        "qkgd,skd->kgqs", query_block, key_rows, preferred_element_type=jnp.float32
    )
    query_places = offset + lax.iota(jnp.int32, length)
    key_places = lax.iota(jnp.int32, key_rows.shape[0])
    query_segs = lax.dynamic_slice_in_dim(segments, offset, length)
    allowed = (key_places[None, :] <= query_places[:, None]) & (
        query_segs[:, None] == segments[None, :]
    )
    return jnp.where(allowed[None, None], 0.125 * raw_scores, MASKED)


def forward_block(element, key_rows, value_rows, segments):
    query_block, offset = element
    scaled = block_scores(query_block, offset, key_rows, segments)
    highest = jnp.max(scaled, -1, keepdims=True)
    exponents = jnp.exp(scaled - highest)
    totals = jnp.sum(exponents, -1, keepdims=True)
    rounded = (exponents / totals).astype(jnp.bfloat16)
    mixed_rows = jnp.einsum(
        "kgqs,skd->qkgd", rounded, value_rows, preferred_element_type=jnp.float32
    )
    return (mixed_rows.astype(jnp.bfloat16), (highest + jnp.log(totals))[..., 0])


def backward_step(running, element, key_rows, value_rows, segments):
    grad_keys, grad_values = running
    query_block, grad_block, log_totals, offset = element
    scaled = block_scores(query_block, offset, key_rows, segments)
    softmax_out = jnp.exp(scaled - log_totals[..., None])
    rounded = softmax_out.astype(jnp.bfloat16)
    grad_values = grad_values + jnp.einsum(
        "kgqs,qkgd->skd", rounded, grad_block, preferred_element_type=jnp.float32
    )
    grad_probs = jnp.einsum(
        "qkgd,skd->kgqs", grad_block, value_rows, preferred_element_type=jnp.float32
    )
    centre = jnp.sum(softmax_out * grad_probs, -1, keepdims=True)
    grad_scores = (0.125 * softmax_out * (grad_probs - centre)).astype(jnp.bfloat16)
    grad_query_block = jnp.einsum(
        "kgqs,skd->qkgd", grad_scores, key_rows, preferred_element_type=jnp.float32
    )
    grad_keys = grad_keys + jnp.einsum(
        "kgqs,qkgd->skd", grad_scores, query_block, preferred_element_type=jnp.float32
    )
    return ((grad_keys, grad_values), grad_query_block)


def body(
    tokens,
    segments,
    positions,
    attn_gain,
    w_query,
    w_key,
    w_value,
    w_out,
    mlp_gain,
    w_gate,
    w_up,
    w_down,
    grad_out,
):
    full_query, full_key, full_value, full_out, gain_one = (
        lax.all_gather(w_query, "dp", axis=0, tiled=True),
        lax.all_gather(w_key, "dp", axis=0, tiled=True),
        lax.all_gather(w_value, "dp", axis=0, tiled=True),
        lax.all_gather(w_out, "dp", axis=1, tiled=True),
        lax.all_gather(attn_gain, "dp", axis=0, tiled=True),
    )
    stream = tokens.astype(jnp.float32)
    scale_one = lax.rsqrt(jnp.mean(stream * stream, -1, keepdims=True) + EPSILON)
    unit_one = stream * scale_one
    gain_first = gain_one.astype(jnp.float32)
    normed_one = lax.all_gather(
        (unit_one * gain_first).astype(jnp.bfloat16), "tensor", axis=0, tiled=True
    )
    length = normed_one.shape[0]
    heads_here = full_query.shape[1] // HD
    groups_here = full_key.shape[1] // HD
    group_size = heads_here // groups_here
    cosine_table, sine_table = tables(positions, HD)
    cosine_table = cosine_table[:, None, :]
    sine_table = sine_table[:, None, :]
    query_lin = jnp.dot(normed_one, full_query, preferred_element_type=jnp.float32).reshape(
        length, heads_here, HD
    )
    queries = (
        rotate(query_lin, cosine_table, sine_table, 1.0)
        .astype(jnp.bfloat16)
        .reshape(length, groups_here, group_size, HD)
    )
    key_lin = jnp.dot(normed_one, full_key, preferred_element_type=jnp.float32).reshape(
        length, groups_here, HD
    )
    key_rows = rotate(key_lin, cosine_table, sine_table, 1.0).astype(jnp.bfloat16)
    value_rows = (
        jnp.dot(normed_one, full_value, preferred_element_type=jnp.float32)
        .astype(jnp.bfloat16)
        .reshape(length, groups_here, HD)
    )
    block_rows = min(512, length)
    blocks = length // block_rows
    offsets = lax.iota(jnp.int32, blocks) * block_rows
    query_blocks = queries.reshape(blocks, block_rows, groups_here, group_size, HD)
    mixed_blocks, log_totals = lax.map(
        partial(forward_block, key_rows=key_rows, value_rows=value_rows, segments=segments),
        (query_blocks, offsets),
    )
    attended = mixed_blocks.reshape(length, heads_here * HD)
    residual = stream + lax.psum_scatter(
        jnp.dot(attended, full_out, preferred_element_type=jnp.float32),
        "tensor",
        scatter_dimension=0,
        tiled=True,
    )
    full_gate, full_up, full_down, gain_two = (
        lax.all_gather(w_gate, "dp", axis=0, tiled=True),
        lax.all_gather(w_up, "dp", axis=0, tiled=True),
        lax.all_gather(w_down, "dp", axis=1, tiled=True),
        lax.all_gather(mlp_gain, "dp", axis=0, tiled=True),
    )
    scale_two = lax.rsqrt(jnp.mean(residual * residual, -1, keepdims=True) + EPSILON)
    unit_two = residual * scale_two
    gain_second = gain_two.astype(jnp.float32)
    normed_two = lax.all_gather(
        (unit_two * gain_second).astype(jnp.bfloat16), "tensor", axis=0, tiled=True
    )
    gate_values = jnp.dot(normed_two, full_gate, preferred_element_type=jnp.float32)
    up_values = jnp.dot(normed_two, full_up, preferred_element_type=jnp.float32)
    sigmoid_gate = jax.nn.sigmoid(gate_values)
    activated = gate_values * sigmoid_gate
    product = (activated * up_values).astype(jnp.bfloat16)
    block_out = (
        residual
        + lax.psum_scatter(
            jnp.dot(product, full_down, preferred_element_type=jnp.float32).astype(jnp.bfloat16),
            "tensor",
            scatter_dimension=0,
            tiled=True,
        ).astype(jnp.float32)
    ).astype(jnp.bfloat16)
    grad_rows = lax.all_gather(grad_out, "tensor", axis=0, tiled=True)
    grad_product = against(grad_rows, full_down)
    grad_down = over_rows(product, grad_rows)
    grad_gated = (
        grad_product * up_values * sigmoid_gate * (1.0 + gate_values * (1.0 - sigmoid_gate))
    ).astype(jnp.bfloat16)
    grad_lifted = (grad_product * activated).astype(jnp.bfloat16)
    grad_gate = over_rows(normed_two, grad_gated)
    grad_up = over_rows(normed_two, grad_lifted)
    grad_normed_two = lax.psum_scatter(
        against(grad_gated, full_gate) + against(grad_lifted, full_up),
        "tensor",
        scatter_dimension=0,
        tiled=True,
    )
    gain_two_part = jnp.sum(grad_normed_two * unit_two, 0)
    scaled_two = grad_normed_two * gain_second
    grad_residual = grad_out.astype(jnp.float32) + scale_two * (
        scaled_two - unit_two * jnp.mean(scaled_two * unit_two, -1, keepdims=True)
    )
    residual_rows = lax.all_gather(grad_residual.astype(jnp.bfloat16), "tensor", axis=0, tiled=True)
    grad_out_proj = over_rows(attended, residual_rows)
    grad_attended = against(residual_rows, full_out).astype(jnp.bfloat16)
    grad_blocks = grad_attended.reshape(blocks, block_rows, groups_here, group_size, HD)
    empty_rows = jnp.zeros((length, groups_here, HD), jnp.float32)
    (grad_keys, grad_values), grad_queries = lax.scan(
        partial(backward_step, key_rows=key_rows, value_rows=value_rows, segments=segments),
        (empty_rows, empty_rows),
        (query_blocks, grad_blocks, log_totals, offsets),
    )
    grad_queries = (
        rotate(grad_queries.reshape(length, heads_here, HD), cosine_table, sine_table, -1.0)
        .astype(jnp.bfloat16)
        .reshape(length, heads_here * HD)
    )
    grad_keys = (
        rotate(grad_keys, cosine_table, sine_table, -1.0)
        .astype(jnp.bfloat16)
        .reshape(length, groups_here * HD)
    )
    grad_values = grad_values.astype(jnp.bfloat16).reshape(length, groups_here * HD)
    grad_query = over_rows(normed_one, grad_queries)
    grad_key = over_rows(normed_one, grad_keys)
    grad_value = over_rows(normed_one, grad_values)
    grad_normed_one = lax.psum_scatter(
        against(grad_queries, full_query)
        + against(grad_keys, full_key)
        + against(grad_values, full_value),
        "tensor",
        scatter_dimension=0,
        tiled=True,
    )
    gain_one_part = jnp.sum(grad_normed_one * unit_one, 0)
    scaled_one = grad_normed_one * gain_first
    grad_tokens = grad_residual + scale_one * (
        scaled_one - unit_one * jnp.mean(scaled_one * unit_one, -1, keepdims=True)
    )
    gain_one_sum, gain_two_sum = lax.psum((gain_one_part, gain_two_part), "tensor")
    (
        grad_query,
        grad_key,
        grad_value,
        grad_out_proj,
        grad_attn_gain,
        grad_mlp_gain,
        grad_gate,
        grad_up,
        grad_down,
    ) = (
        lax.psum_scatter(grad_query, "dp", scatter_dimension=0, tiled=True),
        lax.psum_scatter(grad_key, "dp", scatter_dimension=0, tiled=True),
        lax.psum_scatter(grad_value, "dp", scatter_dimension=0, tiled=True),
        lax.psum_scatter(grad_out_proj, "dp", scatter_dimension=1, tiled=True),
        lax.psum_scatter(gain_one_sum, "dp", scatter_dimension=0, tiled=True),
        lax.psum_scatter(gain_two_sum, "dp", scatter_dimension=0, tiled=True),
        lax.psum_scatter(grad_gate, "dp", scatter_dimension=0, tiled=True),
        lax.psum_scatter(grad_up, "dp", scatter_dimension=0, tiled=True),
        lax.psum_scatter(grad_down, "dp", scatter_dimension=1, tiled=True),
    )
    return (
        block_out,
        grad_tokens,
        grad_attn_gain,
        grad_query,
        grad_key,
        grad_value,
        grad_out_proj,
        grad_mlp_gain,
        grad_gate,
        grad_up,
        grad_down,
    )


def solution(mesh):
    placed = (
        P(("dp", "tensor"), None),
        P("dp"),
        P("dp"),
        P("dp"),
        P("dp", "tensor"),
        P("dp", "tensor"),
        P("dp", "tensor"),
        P("tensor", "dp"),
        P("dp"),
        P("dp", "tensor"),
        P("dp", "tensor"),
        P("tensor", "dp"),
        P(("dp", "tensor"), None),
    )
    return jax.shard_map(
        body,
        mesh=mesh,
        in_specs=placed,
        out_specs=(
            P(("dp", "tensor"), None),
            P(("dp", "tensor"), None),
            P("dp"),
            P("dp", "tensor"),
            P("dp", "tensor"),
            P("dp", "tensor"),
            P("tensor", "dp"),
            P("dp"),
            P("dp", "tensor"),
            P("dp", "tensor"),
            P("tensor", "dp"),
        ),
        check_vma=False,
    )
```

profile of v0, /device:TPU:0, one launch (start us, length us, event | category | flops | bytes accessed | tf_op | source)
XLA Modules:
  0.0 1903.8 jit_solution(16582608316146147910)
XLA Ops:
  9.5 10.4 all-gather
  27.4 9.8 all_gather.42
  37.2 8.9 all_gather.43
  47.9 56.2 %all-gather.12.cloned.1.call-done = bf16[1024,2048]{1,0:T(8,128)(2,1)} async-done(((bf16[256,2048]{1,0:T(8,128)(2,1)}), bf16[1024,2048]{1,0:T(8,128)(2,1)}) %all-gather.12.cloned.1.call-update) | async-done | bytes 4194320 | tf_op jit(solution)/shard_map/all_gather | solution.py:130
  108.7 23.8 %all-gather.14.cloned.1.call-done = bf16[2048,512]{1,0:T(8,128)(2,1)} async-done(((bf16[256,512]{1,0:T(8,128)(2,1)}), bf16[2048,512]{1,0:T(8,128)(2,1)}) %all-gather.14.cloned.1.call-update) | async-done | bytes 2097168 | tf_op jit(solution)/shard_map/all_gather | solution.py:120
  155.1 34.9 %while.27 = (s32[]{:T(128)}, bf16[2,512,2,4,64]{1,4,3,2,0:T(8,128)(2,1)S(1)}, f32[2,2,4,512]{3,2,1,0:T(4,128)S(1)}, s32[2]{0:T(128)S(1)}, s32[1024]{0:T(1024)S(1...) while((s32[]{:T(128)}, ...), condition=%wide.region_4.5_spmd, body=%wide.region_1.4_spmd.sunk | while | flops 1125904896 | bytes 54147256 | solution.py:161
  191.4 7.6 fusion.72
  199.8 8.9 all-gather.1
  208.7 135.1 %reduce-scatter.12.cloned.1.call-done = f32[256,2048]{1,0:T(8,128)} async-done(((f32[1024,2048]{1,0:T(8,128)}), f32[256,2048]{1,0:T(8,128)}) %reduce-scatter.12.cloned.1.call-update) | async-done | bytes 2097168 | tf_op jit(solution)/shard_map/reduce_scatter | solution.py:166
  349.5 51.2 %all-gather.22.cloned.1.call-done = bf16[2048,2048]{1,0:T(8,128)(2,1)} async-done(((bf16[256,2048]{1,0:T(8,128)(2,1)}), bf16[2048,2048]{1,0:T(8,128)(2,1)}) %all-gather.22.cloned.1.call-update) | async-done | bytes 8388624 | tf_op jit(solution)/shard_map/all_gather | solution.py:174
  400.7 82.8 %all-gather.18.cloned.1.call-done = bf16[1024,2048]{1,0:T(8,128)(2,1)} async-done(((bf16[256,2048]{1,0:T(8,128)(2,1)}), bf16[1024,2048]{1,0:T(8,128)(2,1)}) %all-gather.18.cloned.1.call-update) | async-done | bytes 4194320 | tf_op jit(solution)/shard_map/all_gather | solution.py:181
  483.5 14.5 fusion.74
  497.9 40.4 %all-gather.20.cloned.1.call-done = bf16[2048,2048]{1,0:T(8,128)(2,1)} async-done(((bf16[256,2048]{1,0:T(8,128)(2,1)}), bf16[2048,2048]{1,0:T(8,128)(2,1)}) %all-gather.20.cloned.1.call-update) | async-done | bytes 8388624 | tf_op jit(solution)/shard_map/all_gather | solution.py:173
  538.3 14.4 fusion.73
  552.7 67.9 %all-gather.26.cloned.1.call-done = bf16[1024,2048]{1,0:T(8,128)(2,1)} async-done(((bf16[256,2048]{1,0:T(8,128)(2,1)}), bf16[1024,2048]{1,0:T(8,128)(2,1)}) %all-gather.26.cloned.1.call-update) | async-done | bytes 4194320 | tf_op jit(solution)/shard_map/all_gather | solution.py:198
  620.7 56.4 %all-gather.24.cloned.1.call-done = bf16[2048,2048]{1,0:T(8,128)(2,1)} async-done(((bf16[2048,256]{1,0:T(8,128)(2,1)}), bf16[2048,2048]{1,0:T(8,128)(2,1)}) %all-gather.24.cloned.1.call-update) | async-done | bytes 8388624 | tf_op jit(solution)/shard_map/all_gather | solution.py:175
  677.1 22.0 %multiply_convert_fusion = (bf16[1024,2048]{1,0:T(8,128)(2,1)}, bf16[1024,2048]{1,0:T(8,128)(2,1)}, bf16[1024,2048]{1,0:T(8,128)(2,1)}) fusion(f32[1024,2048]{1,0:T(8,128)} %fusion.73, f32[1024,2048]{1,0:T(8,128)} %fusion.74, bf16[1024,2048]{1,0:T(8,128)(2,1)} %all-gather.26.cloned.1.call-done, bf16[2048,2048]{1,0:T(8,128)(2,1)} %all-gather.24.cloned.1.call-done), kind=kOutput, calls=%fused_computation.61 | convolution fusion | flops 8621391872 | bytes 41943040 | tf_op jit(solution)/shard_map/dot_general | solution.py:49
  699.1 12.9 fusion.75
  712.0 13.5 convolution_add_fusion
  725.6 144.6 %reduce-scatter.16.cloned.1.call-done = f32[256,2048]{1,0:T(8,128)} async-done(((f32[1024,2048]{1,0:T(8,128)}), f32[256,2048]{1,0:T(8,128)}) %reduce-scatter.16.cloned.1.call-update) | async-done | bytes 2097168 | tf_op jit(solution)/shard_map/reduce_scatter | solution.py:207
  874.8 81.6 %all-gather.28.cloned.1.call-done = bf16[1024,2048]{1,0:T(8,128)(2,1)} async-done(((bf16[256,2048]{1,0:T(8,128)(2,1)}), bf16[1024,2048]{1,0:T(8,128)(2,1)}) %all-gather.28.cloned.1.call-update) | async-done | bytes 4194320 | tf_op jit(solution)/shard_map/all_gather | solution.py:218
  956.4 6.2 convolution_convert_fusion.1
  968.9 133.2 %while.28 = (s32[]{:T(128)}, f32[1024,2,64]{0,2,1:T(8,128)S(1)}, f32[1024,2,64]{0,2,1:T(8,128)}, f32[2,512,2,4,64]{1,0,4,3,2:T(2,128)}, bf16[2,512,2,4,64]{1,4,3...) while((s32[]{:T(128)}, f32[1024,2,64]{0,2,1:T(8,128)S(1)}, ...), condition=%wide.region_12.13_spmd.clone, body=%wide.region_10.12_spmd.clone.sunk | while | flops 2753556992 | bytes 176093504 | solution.py:223
  982.7 11.0 fusion.161
  993.8 8.5 fusion.162
  1008.3 6.1 convolution_bitcast_fusion.3
  1015.5 19.6 %dynamic_update_slice.20 = f32[2,512,2,4,64]{1,0,4,3,2:T(2,128)} dynamic-update-slice(f32[2,512,2,4,64]{1,0,4,3,2:T(2,128)} %get-tuple-element.450, f32[1,512,2,4,64]{1,0,4,3,2:T(1,128)S(1)} %copy.61, s32[]{:T(128)S(6)} %copy.78, s32[]{:T(128)} %constant.45.clone.1..sunk.1, s32[]{:T(128)} %constant.45.clone.1..sunk.1, s32[]{:T(128)} %constant.45.clone.1..sunk.1, s32[]{:T(128)} %constant.45.clone.1..sunk.1) | dynamic-update-slice | bytes 2097156 | tf_op jit(solution)/shard_map/while/body/jit(dynamic_update_index_in_dim)/dynamic_update_slice | solution.py:223
  1043.2 6.4 fusion.164
  1049.6 11.0 fusion.161
  1060.6 8.5 fusion.162
  1082.4 19.6 %dynamic_update_slice.20 = f32[2,512,2,4,64]{1,0,4,3,2:T(2,128)} dynamic-update-slice(f32[2,512,2,4,64]{1,0,4,3,2:T(2,128)} %get-tuple-element.450, f32[1,512,2,4,64]{1,0,4,3,2:T(1,128)S(1)} %copy.61, s32[]{:T(128)S(6)} %copy.78, s32[]{:T(128)} %constant.45.clone.1..sunk.1, s32[]{:T(128)} %constant.45.clone.1..sunk.1, s32[]{:T(128)} %constant.45.clone.1..sunk.1, s32[]{:T(128)} %constant.45.clone.1..sunk.1) | dynamic-update-slice | bytes 2097156 | tf_op jit(solution)/shard_map/while/body/jit(dynamic_update_index_in_dim)/dynamic_update_slice | solution.py:223
  1120.9 13.9 convolution_convert_fusion
  1144.3 15.3 fusion.83
  1159.7 15.3 fusion.82
  1175.3 15.2 fusion.84
  1191.8 6.5 fusion.81
  1198.4 6.6 fusion.78
  1206.9 57.1 %reduce-scatter.18.cloned.1.call-done = f32[256,2048]{1,0:T(8,128)} async-done(((f32[1024,2048]{1,0:T(8,128)}), f32[256,2048]{1,0:T(8,128)}) %reduce-scatter.18.cloned.1.call-update) | async-done | bytes 2097168 | tf_op jit(solution)/shard_map/reduce_scatter | solution.py:242
  1266.3 24.0 %all-reduce.2 = (f32[2048]{0:T(1024)S(1)}, f32[2048]{0:T(1024)S(1)}) all-reduce(f32[2048]{0:T(1024)S(1)} %get-tuple-element.205, f32[2048]{0:T(1024)S(1)} %copy-done.38), channel_id=6, replica_groups=mesh['dp'=8,'tensor'=4] {'dp'}, use_global_device_ids=true, to_apply=%region_17.18.clone | all-reduce | flops 4096 | bytes 32768
  1290.4 12.8 all-reduce.3
  1303.2 40.9 %reduce-scatter.14.cloned.1.call-done = bf16[256,2048]{1,0:T(8,128)(2,1)} async-done(((bf16[1024,2048]{1,0:T(8,128)(2,1)}), bf16[256,2048]{1,0:T(8,128)(2,1)}) %reduce-scatter.14.cloned.1.call-update) | async-done | bytes 1048592 | tf_op jit(solution)/shard_map/reduce_scatter | solution.py:191
  1349.7 34.9 %reduce-scatter.22.cloned.1.call-done = f32[256,128]{1,0:T(8,128)} async-done(((f32[2048,128]{1,0:T(8,128)}), f32[256,128]{1,0:T(8,128)}) %reduce-scatter.22.cloned.1.call-update) | async-done | bytes 131088 | tf_op jit(solution)/shard_map/reduce_scatter | solution.py:268
  1384.6 40.0 %reduce-scatter.24.cloned.1.call-done = f32[256,128]{1,0:T(8,128)} async-done(((f32[2048,128]{1,0:T(8,128)}), f32[256,128]{1,0:T(8,128)}) %reduce-scatter.24.cloned.1.call-update) | async-done | bytes 131088 | tf_op jit(solution)/shard_map/reduce_scatter | solution.py:269
  1424.5 120.4 %reduce-scatter.30.cloned.1.call-done = f32[256,2048]{1,0:T(8,128)} async-done(((f32[2048,2048]{1,0:T(8,128)}), f32[256,2048]{1,0:T(8,128)}) %reduce-scatter.30.cloned.1.call-update) | async-done | bytes 2097168 | tf_op jit(solution)/shard_map/reduce_scatter | solution.py:274
  1545.0 120.4 %reduce-scatter.28.cloned.1.call-done = f32[256,2048]{1,0:T(8,128)} async-done(((f32[2048,2048]{1,0:T(8,128)}), f32[256,2048]{1,0:T(8,128)}) %reduce-scatter.28.cloned.1.call-update) | async-done | bytes 2097168 | tf_op jit(solution)/shard_map/reduce_scatter | solution.py:273
  1665.4 120.4 %reduce-scatter.32.cloned.1.call-done = f32[2048,256]{1,0:T(8,128)} async-done(((f32[2048,2048]{1,0:T(8,128)}), f32[2048,256]{1,0:T(8,128)}) %reduce-scatter.32.cloned.1.call-update) | async-done | bytes 2097168 | tf_op jit(solution)/shard_map/reduce_scatter | solution.py:275
  1785.8 55.6 %reduce-scatter.26.cloned.1.call-done = f32[512,256]{1,0:T(8,128)} async-done(((f32[512,2048]{1,0:T(8,128)}), f32[512,256]{1,0:T(8,128)}) %reduce-scatter.26.cloned.1.call-update) | async-done | bytes 524304 | tf_op jit(solution)/shard_map/reduce_scatter | solution.py:270
  1841.4 55.1 %reduce-scatter.20.cloned.1.call-done = f32[256,512]{1,0:T(8,128)} async-done(((f32[2048,512]{1,0:T(8,128)}), f32[256,512]{1,0:T(8,128)}) %reduce-scatter.20.cloned.1.call-update) | async-done | bytes 524304 | tf_op jit(solution)/shard_map/reduce_scatter | solution.py:267
  (242 shorter events, 164.5 us)
Async XLA Ops:
  7.2 17.4 copy-start.45
  7.2 20.2 %copy-start.36 = (bf16[256,128]{1,0:T(8,128)(2,1)S(1)}, bf16[256,128]{1,0:T(8,128)(2,1)}, u32[]{:S(2)}) copy-start(bf16[256,128]{1,0:T(8,128)(2,1)} %param.22) | copy-start | bytes 196612
  7.2 30.0 %copy-start.37 = (bf16[256,128]{1,0:T(8,128)(2,1)S(1)}, bf16[256,128]{1,0:T(8,128)(2,1)}, u32[]{:S(2)}) copy-start(bf16[256,128]{1,0:T(8,128)(2,1)} %param.23) | copy-start | bytes 196612
  7.2 97.0 %all-gather.12.cloned.1.call-start = ((), (), s32[]{:S(2)}) async-start(), calls=%async_computation.11 | async-start | bytes 5242880 | tf_op jit(solution)/shard_map/all_gather | solution.py:130
  9.5 10.4 copy-start.41
  23.0 109.6 %all-gather.14.cloned.1.call-start = ((), (), s32[]{:S(2)}) async-start(), calls=%async_computation.12 | async-start | bytes 2359296 | tf_op jit(solution)/shard_map/all_gather | solution.py:120
  23.7 167.7 %all-gather.16.cloned.1.call-start = ((), (), s32[]{:S(2)}) async-start(), calls=%async_computation.13 | async-start | bytes 2359296 | tf_op jit(solution)/shard_map/all_gather | solution.py:123
  24.4 319.3 %reduce-scatter.12.cloned.1.call-start = ((), (), s32[]{:S(2)}) async-start(), calls=%async_computation.14 | async-start | bytes 10485760 | tf_op jit(solution)/shard_map/reduce_scatter | solution.py:166
  25.1 127.6 %copy-start.17 = (f32[1024,64]{0,1:T(8,128)}, f32[1024,64]{0,1:T(8,128)S(1)}, u32[]{:S(2)}) copy-start(f32[1024,64]{0,1:T(8,128)S(1)} %pad_maximum_fusion.2) | copy-start | bytes 786436
  37.2 71.5 %copy-start.15 = (bf16[2048,128]{1,0:T(8,128)(2,1)}, bf16[2048,128]{1,0:T(8,128)(2,1)S(1)}, u32[]{:S(2)}) copy-start(bf16[2048,128]{1,0:T(8,128)(2,1)S(1)} %all_gather.42) | copy-start | bytes 1572868
  46.1 107.5 %copy-start.13 = (bf16[2048,128]{1,0:T(8,128)(2,1)}, bf16[2048,128]{1,0:T(8,128)(2,1)S(1)}, u32[]{:S(2)}) copy-start(bf16[2048,128]{1,0:T(8,128)(2,1)S(1)} %all_gather.43) | copy-start | bytes 1572868
  142.2 6.3 copy-start.12
  148.6 4.2 copy-start.27
  148.6 5.0 copy-start.1
  190.0 9.0 copy-start.8
  190.0 9.0 copy-start.31
  191.4 7.7 copy-start.23
  199.1 144.7 %copy-start.4 = (bf16[256,2048]{1,0:T(8,128)(2,1)S(1)}, bf16[256,2048]{1,0:T(8,128)(2,1)}, u32[]{:S(2)}) copy-start(bf16[256,2048]{1,0:T(8,128)(2,1)} %param.17) | copy-start | bytes 3145732
  199.1 201.5 %all-gather.22.cloned.1.call-start = ((), (), s32[]{:S(2)}) async-start(), calls=%async_computation.17 | async-start | bytes 9437184 | tf_op jit(solution)/shard_map/all_gather | solution.py:174
  199.7 283.7 %all-gather.18.cloned.1.call-start = ((), (), s32[]{:S(2)}) async-start(), calls=%async_computation.15 | async-start | bytes 5242880 | tf_op jit(solution)/shard_map/all_gather | solution.py:181
  208.7 664.4 %copy-start.32 = (f32[8,1,256]{2,1,0:T(1,128)}, f32[8,1,256]{2,1,0:T(1,128)S(1)}, u32[]{:S(2)}) copy-start(f32[8,1,256]{2,1,0:T(1,128)S(1)} %convert_element_type.102) | copy-start | bytes 24580
  345.7 527.3 %copy-start.2 = (f32[256,2048]{1,0:T(8,128)}, f32[256,2048]{1,0:T(8,128)S(1)}, u32[]{:S(2)}) copy-start(f32[256,2048]{1,0:T(8,128)S(1)} %get-tuple-element.250) | copy-start | bytes 6291460
  345.8 527.3 %copy-start.39 = (f32[256]{0:T(256)}, f32[256]{0:T(256)S(1)}, u32[]{:S(2)}) copy-start(f32[256]{0:T(256)S(1)} %add_rsqrt_fusion) | copy-start | bytes 3076
  347.2 191.1 %all-gather.20.cloned.1.call-start = ((), (), s32[]{:S(2)}) async-start(), calls=%async_computation.16 | async-start | bytes 9437184 | tf_op jit(solution)/shard_map/all_gather | solution.py:173
  347.9 272.7 %all-gather.26.cloned.1.call-start = ((), (), s32[]{:S(2)}) async-start(), calls=%async_computation.20 | async-start | bytes 5242880 | tf_op jit(solution)/shard_map/all_gather | solution.py:198
  348.7 328.4 %all-gather.24.cloned.1.call-start = ((), (), s32[]{:S(2)}) async-start(), calls=%async_computation.18 | async-start | bytes 9437184 | tf_op jit(solution)/shard_map/all_gather | solution.py:175
  349.4 520.7 %reduce-scatter.16.cloned.1.call-start = ((), (), s32[]{:S(2)}) async-start(), calls=%async_computation.21 | async-start | bytes 10485760 | tf_op jit(solution)/shard_map/reduce_scatter | solution.py:207
  699.1 12.9 copy-start.49
  725.5 147.5 %copy-start.9 = (bf16[256,2048]{1,0:T(8,128)(2,1)S(1)}, bf16[256,2048]{1,0:T(8,128)(2,1)}, u32[]{:S(2)}) copy-start(bf16[256,2048]{1,0:T(8,128)(2,1)} %param.29) | copy-start | bytes 3145732
  725.5 230.9 %all-gather.28.cloned.1.call-start = ((), (), s32[]{:S(2)}) async-start(), calls=%async_computation.22 | async-start | bytes 5242880 | tf_op jit(solution)/shard_map/all_gather | solution.py:218
  874.8 389.2 %reduce-scatter.18.cloned.1.call-start = ((), (), s32[]{:S(2)}) async-start(), calls=%async_computation.23 | async-start | bytes 10485760 | tf_op jit(solution)/shard_map/reduce_scatter | solution.py:242
  1102.1 6.8 copy-start.10
  1120.9 223.2 %reduce-scatter.14.cloned.1.call-start = ((), (), s32[]{:S(2)}) async-start(), calls=%async_computation.19 | async-start | bytes 5242880 | tf_op jit(solution)/shard_map/reduce_scatter | solution.py:191
  1134.8 249.8 %reduce-scatter.22.cloned.1.call-start = ((), (), s32[]{:S(2)}) async-start(), calls=%async_computation.25 | async-start | bytes 1179648 | tf_op jit(solution)/shard_map/reduce_scatter | solution.py:268
  1139.3 285.2 %reduce-scatter.24.cloned.1.call-start = ((), (), s32[]{:S(2)}) async-start(), calls=%async_computation.26 | async-start | bytes 1179648 | tf_op jit(solution)/shard_map/reduce_scatter | solution.py:269
  1144.2 400.7 %reduce-scatter.30.cloned.1.call-start = ((), (), s32[]{:S(2)}) async-start(), calls=%async_computation.29 | async-start | bytes 18874368 | tf_op jit(solution)/shard_map/reduce_scatter | solution.py:274
  1159.6 505.8 %reduce-scatter.28.cloned.1.call-start = ((), (), s32[]{:S(2)}) async-start(), calls=%async_computation.28 | async-start | bytes 18874368 | tf_op jit(solution)/shard_map/reduce_scatter | solution.py:273
  1175.0 610.8 %reduce-scatter.32.cloned.1.call-start = ((), (), s32[]{:S(2)}) async-start(), calls=%async_computation.30 | async-start | bytes 18874368 | tf_op jit(solution)/shard_map/reduce_scatter | solution.py:275
  1190.5 650.9 %reduce-scatter.26.cloned.1.call-start = ((), (), s32[]{:S(2)}) async-start(), calls=%async_computation.27 | async-start | bytes 4718592 | tf_op jit(solution)/shard_map/reduce_scatter | solution.py:270
  1198.3 698.2 %reduce-scatter.20.cloned.1.call-start = ((), (), s32[]{:S(2)}) async-start(), calls=%async_computation.24 | async-start | bytes 4718592 | tf_op jit(solution)/shard_map/reduce_scatter | solution.py:267
  1205.0 59.0 %copy-start.5 = (bf16[256,2048]{1,0:T(8,128)(2,1)S(1)}, bf16[256,2048]{1,0:T(8,128)(2,1)}, u32[]{:S(2)}) copy-start(bf16[256,2048]{1,0:T(8,128)(2,1)} %param.17) | copy-start | bytes 3145732
  1205.0 59.0 %copy-start.35 = (f32[8,1,256]{2,1,0:T(1,128)S(1)}, f32[8,1,256]{2,1,0:T(1,128)}, u32[]{:S(2)}) copy-start(f32[8,1,256]{2,1,0:T(1,128)} %copy-done.34) | copy-start | bytes 24580
  1205.0 59.0 %copy-start.42 = (f32[256]{0:T(256)S(1)}, f32[256]{0:T(256)}, u32[]{:S(2)}) copy-start(f32[256]{0:T(256)} %copy-done.41) | copy-start | bytes 3076
  1205.0 61.3 %copy-start.38 = (f32[2048]{0:T(1024)S(1)}, f32[2048]{0:T(1024)}, u32[]{:S(2)}) copy-start(f32[2048]{0:T(1024)} %get-tuple-element.203) | copy-start | bytes 24580
  1205.0 139.1 %copy-start.3 = (f32[256,2048]{1,0:T(8,128)S(1)}, f32[256,2048]{1,0:T(8,128)}, u32[]{:S(2)}) copy-start(f32[256,2048]{1,0:T(8,128)} %copy-done.2) | copy-start | bytes 6291460
  1205.0 139.1 %copy-start.33 = (f32[8,1,256]{2,1,0:T(1,128)S(1)}, f32[8,1,256]{2,1,0:T(1,128)}, u32[]{:S(2)}) copy-start(f32[8,1,256]{2,1,0:T(1,128)} %copy-done.32) | copy-start | bytes 24580
  1205.0 139.1 %copy-start.40 = (f32[256]{0:T(256)S(1)}, f32[256]{0:T(256)}, u32[]{:S(2)}) copy-start(f32[256]{0:T(256)} %copy-done.39) | copy-start | bytes 3076
  1205.1 139.1 %copy-start.44 = (f32[256]{0:T(256)S(1)}, f32[256]{0:T(256)}, u32[]{:S(2)}) copy-start(f32[256]{0:T(256)} %copy-done.43) | copy-start | bytes 3076
  (25 other events, 62.5 us)
Sparse Core Ops, SparseCore 0:
  23.1 81.0 all-gather.11
  106.1 26.4 all-gather.13
  134.4 28.1 all-gather.15
  199.2 144.4 reduce-scatter.11
  345.5 55.0 all-gather.21
  402.7 80.7 all-gather.17
  485.3 52.9 all-gather.19
  539.9 80.7 all-gather.25
  622.5 54.4 all-gather.23
  725.6 144.4 reduce-scatter.15
  874.9 81.4 all-gather.27
  1121.0 142.9 reduce-scatter.17
  1266.3 77.7 reduce-scatter.13
  1348.0 36.4 reduce-scatter.21
  1388.5 36.0 reduce-scatter.23
  1429.0 115.9 reduce-scatter.29
  1549.4 115.9 reduce-scatter.27
  1669.8 115.9 reduce-scatter.31
  1790.1 51.2 reduce-scatter.25
  1845.2 51.2 reduce-scatter.19
where the time goes:
time: 1910 us; the launch traced here: 1900 us
  waiting for transfers between devices  1390 us (73%)
  matrix products  268 us (14%)
  local copies, waits for them, and re-layouts  80.5 us (4%)
  blocking collectives  74.7 us (4%)
  other arithmetic  64.7 us (3%)
    reduce_scatter x1, waiting for transfers between devices, body(): lax.psum_scatter(against(grad_gated, full_gate) + against(grad_lifted, fu...  145 us
    reduce_scatter x1, waiting for transfers between devices, body(): lax.psum_scatter(jnp.dot(attended, full_out, preferred_element_type=jnp.f...  135 us
    reduce_scatter x1, waiting for transfers between devices, body(): lax.psum_scatter(grad_down, 'dp', scatter_dimension=1, tiled=True)  120 us
    reduce_scatter x1, waiting for transfers between devices, body(): lax.psum_scatter(grad_up, 'dp', scatter_dimension=0, tiled=True)  120 us
    reduce_scatter x1, waiting for transfers between devices, body(): lax.psum_scatter(grad_gate, 'dp', scatter_dimension=0, tiled=True)  120 us
    all_gather x1, waiting for transfers between devices, body(): lax.all_gather((unit_two * gain_second).astype(jnp.bfloat16), 'tensor', a...  82.8 us
    all_gather x1, waiting for transfers between devices, body(): lax.all_gather(grad_residual.astype(jnp.bfloat16), 'tensor', axis=0, tile...  81.6 us
    dot_general x7, matrix products, over_rows(): lax.dot_general(left_side, right_side, (((0,), (0,)), ((), ())), preferre...  68 us
  transfers between devices with their start and end apart: 20, of which 19 were waited for; matrix products, arithmetic and copies ran while one was open for 10% of the time, Pallas kernels for 0%

commit v1 on v0

v1 whole, which is shorter than its diff:
```python
import functools
import math

import jax
import jax.numpy as jnp
from jax import lax
from jax.experimental import pallas as pl
from jax.experimental.pallas import tpu as pltpu
from jax.sharding import PartitionSpec as P

HD = 64
EPSILON = 1e-05
MASKED = -1e30
F32 = jnp.float32
BF = jnp.bfloat16

def turn_t(values, cosine, sine, sign):
    half=values.shape[0]//2
    first, second = values[:half], values[half:]
    return jnp.concatenate([first*cosine - sign*second*sine, second*cosine + sign*first*sine],0)

def block_bias(segs_col, segs_row, start, block):
    keys=start+block
    key_places=lax.broadcasted_iota(jnp.int32,(keys,block),0)
    query_places=start+lax.broadcasted_iota(jnp.int32,(keys,block),1)
    allowed=(key_places<=query_places)&(segs_col[0:keys,:]==segs_row[0:1,start:start+block])
    return jnp.where(allowed,0.0,MASKED).astype(F32)

def attend_kernel(heads, groups, block, lin_ref, cos_ref, sin_ref, segc_ref, segr_ref,
                  mixed_ref, lse_ref, q_ref, kt_ref, k_ref, vt_ref, v_ref, bias_ref):
    length=lin_ref.shape[1]
    per=heads//groups
    cosine, sine = cos_ref[...], sin_ref[...]
    def rope(h,_):
        rows=pl.ds(pl.multiple_of(h*HD,HD),HD)
        q_ref[rows,:]=(turn_t(lin_ref[rows,:],cosine,sine,1.0).astype(BF)*jnp.asarray(0.125,BF))
        return 0
    lax.fori_loop(0,heads,rope,0)
    kv=groups*HD
    turned=[turn_t(lin_ref[(heads+g)*HD:(heads+g+1)*HD,:],cosine,sine,1.0) for g in range(groups)]
    keys_t=jnp.concatenate(turned,0)
    kt_ref[...]=keys_t.astype(BF)
    vals_t=lin_ref[(heads+groups)*HD:(heads+2*groups)*HD,:]
    vt_ref[...]=vals_t.astype(BF)
    keys_n=keys_t.T.astype(BF)
    vals_n=vals_t.T.astype(BF)
    for g in range(groups):
        k_ref[g]=keys_n[:,g*HD:(g+1)*HD]
        v_ref[g]=vals_n[:,g*HD:(g+1)*HD]
    for start in range(0,length,block):
        keys=start+block
        bias_ref[0:keys,:]=block_bias(segc_ref,segr_ref,start,block)
        def head(h,_):
            g=h//per
            rows=pl.ds(pl.multiple_of(h*HD,HD),HD)
            grows=pl.ds(pl.multiple_of(g*HD,HD),HD)
            scores=jnp.dot(k_ref[g,0:keys,:],q_ref[rows,start:start+block],preferred_element_type=F32)
            scores=scores+bias_ref[0:keys,:]
            top=jnp.max(scores,0,keepdims=True)
            weights=jnp.exp(scores-top)
            total=jnp.sum(weights,0,keepdims=True)
            out=jnp.dot(vt_ref[grows,0:keys],weights.astype(BF),preferred_element_type=F32)
            mixed_ref[rows,start:start+block]=(out/total).astype(BF)
            lse_ref[h,:,start:start+block]=top+jnp.log(total)
            return 0
        lax.fori_loop(0,heads,head,0)

def attend(lin, cosine, sine, segments, heads, groups):
    length=lin.shape[1]
    block=min(256,length)
    sds=jax.ShapeDtypeStruct
    vm=pl.BlockSpec(memory_space=pltpu.VMEM)
    return pl.pallas_call(functools.partial(attend_kernel,heads,groups,block),
        out_shape=(sds((heads*HD,length),BF),sds((heads,1,length),F32),sds((heads*HD,length),BF),
            sds((groups*HD,length),BF),sds((groups,length,HD),BF),sds((groups*HD,length),BF),sds((groups,length,HD),BF)),
        in_specs=[vm]*5,out_specs=(vm,)*7,
        scratch_shapes=[pltpu.VMEM((length,block),F32)],
        cost_estimate=pl.CostEstimate(flops=30_000_000_000,bytes_accessed=10_000_000,transcendentals=8_000_000),
        compiler_params=pltpu.CompilerParams(vmem_limit_bytes=48*1024*1024),
    )(lin,cosine,sine,segments.reshape(length,1),segments.reshape(1,length))

def attend_back_kernel(heads, groups, block, q_ref, kt_ref, k_ref, v_ref, lse_ref, gm_ref, cos_ref, sin_ref, segc_ref, segr_ref,
                  out_ref, bias_ref, qn_ref, gn_ref, dq_ref, dk_ref, dv_ref):
    length=q_ref.shape[1]
    per=heads//groups
    cosine, sine = cos_ref[...], sin_ref[...]
    def flip(p,_):
        rows=pl.ds(pl.multiple_of(p*2*HD,2*HD),2*HD)
        qn=q_ref[rows,:].astype(F32).T.astype(BF)
        gn=gm_ref[rows,:].astype(F32).T.astype(BF)
        qn_ref[2*p]=qn[:,:HD]
        qn_ref[2*p+1]=qn[:,HD:]
        gn_ref[2*p]=gn[:,:HD]
        gn_ref[2*p+1]=gn[:,HD:]
        return 0
    lax.fori_loop(0,heads//2,flip,0)
    dk_ref[...]=jnp.zeros_like(dk_ref)
    dv_ref[...]=jnp.zeros_like(dv_ref)
    for start in range(0,length,block):
        keys=start+block
        cols=slice(start,start+block)
        bias_ref[0:keys,:]=block_bias(segc_ref,segr_ref,start,block)
        def head(h,_):
            g=h//per
            rows=pl.ds(pl.multiple_of(h*HD,HD),HD)
            grows=pl.ds(pl.multiple_of(g*HD,HD),HD)
            scores=jnp.dot(k_ref[g,0:keys,:],q_ref[rows,cols],preferred_element_type=F32)
            probs=jnp.exp(scores+bias_ref[0:keys,:]-lse_ref[h,:,cols])
            dv_ref[g,0:keys,:]+=jnp.dot(probs.astype(BF),gn_ref[h,cols,:],preferred_element_type=F32)
            gp=jnp.dot(v_ref[g,0:keys,:],gm_ref[rows,cols],preferred_element_type=F32)
            weighted=probs*gp
            centre=jnp.sum(weighted,0,keepdims=True)
            gs=(weighted-probs*centre).astype(BF)
            dk_ref[g,0:keys,:]+=jnp.dot(gs,qn_ref[h,cols,:],preferred_element_type=F32)
            dq_ref[rows,cols]=0.125*jnp.dot(kt_ref[grows,0:keys],gs,preferred_element_type=F32)
            return 0
        lax.fori_loop(0,heads,head,0)
    def back(h,_):
        rows=pl.ds(pl.multiple_of(h*HD,HD),HD)
        out_ref[rows,:]=turn_t(dq_ref[rows,:],cosine,sine,-1.0).astype(BF)
        return 0
    lax.fori_loop(0,heads,back,0)
    dk=jnp.concatenate([dk_ref[g] for g in range(groups)],1).T
    dv=jnp.concatenate([dv_ref[g] for g in range(groups)],1).T
    for g in range(groups):
        out_ref[(heads+g)*HD:(heads+g+1)*HD,:]=turn_t(dk[g*HD:(g+1)*HD],cosine,sine,-1.0).astype(BF)
    out_ref[(heads+groups)*HD:,:]=dv.astype(BF)

def attend_back(q,kt,k,v,lse,gm,cosine,sine,segments,heads,groups):
    length=q.shape[1]
    block=min(256,length)
    vm=pl.BlockSpec(memory_space=pltpu.VMEM)
    return pl.pallas_call(functools.partial(attend_back_kernel,heads,groups,block),
        out_shape=jax.ShapeDtypeStruct(((heads+2*groups)*HD,length),BF),
        in_specs=[vm]*10,out_specs=vm,
        scratch_shapes=[pltpu.VMEM((length,block),F32),pltpu.VMEM((heads,length,HD),BF),pltpu.VMEM((heads,length,HD),BF),
            pltpu.VMEM((heads*HD,length),F32),pltpu.VMEM((groups,length,HD),F32),pltpu.VMEM((groups,length,HD),F32)],
        cost_estimate=pl.CostEstimate(flops=60_000_000_000,bytes_accessed=10_000_000,transcendentals=8_000_000),
        compiler_params=pltpu.CompilerParams(vmem_limit_bytes=48*1024*1024),
    )(q,kt,k,v,lse,gm,cosine,sine,segments.reshape(length,1),segments.reshape(1,length))


AXIS="tensor"
MESH=pl.DeviceIdType.MESH

def greet(here, count):
    barrier=pltpu.get_barrier_semaphore()
    @pl.when(here>0)
    def _(): pl.semaphore_signal(barrier,inc=1,device_id={AXIS:here-1},device_id_type=MESH)
    @pl.when(here<count-1)
    def _(): pl.semaphore_signal(barrier,inc=1,device_id={AXIS:here+1},device_id_type=MESH)
    pl.semaphore_wait(barrier,jnp.where((here>0)&(here<count-1),2,1))

def remote(src,dst,send,recv,target):
    return pltpu.make_async_remote_copy(src_ref=src,dst_ref=dst,send_sem=send,recv_sem=recv,
        device_id={AXIS:target},device_id_type=MESH)

class Line:
    def __init__(self,count,pieces,rows,part=None,sums=None,sum_sems=None,held=None,held_sems=None):
        self.n,self.pieces,self.rows=count,pieces,rows
        self.sub=rows//pieces
        self.here=lax.axis_index(AXIS)
        self.part,self.sums,self.sum_sems=part,sums,sum_sems
        self.held,self.held_sems=held,held_sems
    def span(self,u): return pl.ds(pl.multiple_of(u*self.sub,self.sub),self.sub)
    def fits(self,u): return (u>=0)&(u<self.pieces)
    def _target(self,way):
        return lax.min(self.here+1,self.n-1) if way==0 else lax.max(self.here-1,0)
    def sum_copy(self,way,j,u,first):
        sends,recvs=self.sum_sems
        dst=self.sums.at[way,j,self.span(u)]
        src=self.part.at[j,self.span(u)] if first else dst
        return remote(src,dst,sends.at[way,j,u],recvs.at[way,j,u],self._target(way))
    def send_sums(self,t):
        here,n=self.here,self.n
        for k in range(n-1):
            for way,j in ((0,n-1-k),(1,k)):
                u=t-here if way==0 else t-(n-1-here)
                ok=self.fits(u)
                u=jnp.clip(u,0,self.pieces-1)
                begins=(here==0) if way==0 else (here==n-1)
                passes=((here>0)&(here<j)) if way==0 else ((here<n-1)&(here>j))
                @pl.when(ok&begins)
                def _(): self.sum_copy(way,j,u,True).start()
                @pl.when(ok&passes)
                def _():
                    copy=self.sum_copy(way,j,u,False)
                    copy.wait_recv()
                    ref=self.sums.at[way,j,self.span(u)]
                    ref[...]=(ref[...].astype(F32)+self.part[j,self.span(u)].astype(F32)).astype(BF)
                    copy.start()
    def own_sum(self,u,total):
        here,n=self.here,self.n
        total[...]=self.part[here,self.span(u)].astype(F32)
        for way in (0,1):
            @pl.when(here>0 if way==0 else here<n-1)
            def _():
                self.sum_copy(way,here,u,False).wait_recv()
                total[...]+=self.sums[way,here,self.span(u)].astype(F32)
    def end_sums(self):
        here,n=self.here,self.n
        def one(u,_):
            for k in range(n-1):
                for way,j in ((0,n-1-k),(1,k)):
                    @pl.when((here<j) if way==0 else (here>j))
                    def _(): self.sum_copy(way,j,u,False).wait_send()
            return 0
        lax.fori_loop(0,self.pieces,one,0)
    def piece_copy(self,way,c,u,src=None):
        sends,recvs=self.held_sems
        dst=self.held.at[c,self.span(u)]
        return remote(dst if src is None else src,dst,sends.at[way,c,u],recvs.at[way,c,u],self._target(way))
    def send_own(self,u,src=None):
        here,n=self.here,self.n
        for way in (0,1):
            @pl.when(here<n-1 if way==0 else here>0)
            def _(): self.piece_copy(way,here,u,src).start()
    def pass_pieces(self,t):
        here,n=self.here,self.n
        for k in range(1,n):
            u=t-k
            ok=self.fits(u)
            u=jnp.clip(u,0,self.pieces-1)
            for way in (0,1):
                c=here-k if way==0 else here+k
                there=ok&((c>=0) if way==0 else (c<n))
                c=jnp.clip(c,0,n-1)
                @pl.when(there)
                def _(): self.piece_copy(way,c,u).wait_recv()
                @pl.when(there&(here<n-1 if way==0 else here>0))
                def _(): self.piece_copy(way,c,u).start()
    def end_pieces(self):
        here,n=self.here,self.n
        def one(u,_):
            for k in range(n):
                for way in (0,1):
                    c=here-k if way==0 else here+k
                    there=(c>=0) if way==0 else (c<n)
                    c=jnp.clip(c,0,n-1)
                    @pl.when(there&(here<n-1 if way==0 else here>0))
                    def _(): self.piece_copy(way,c,u).wait_send()
            return 0
        lax.fori_loop(0,self.pieces,one,0)

def turn_over(finish, count, pieces, n_in, n_out, gather, *refs):
    part=refs[0]; ins=refs[1:1+n_in]; outs=refs[1+n_in:1+n_in+n_out]
    rest=refs[1+n_in+n_out:]
    if gather:
        whole,sums,total,ss,sr,held,hs,hr,ws=rest
    else:
        sums,total,ss,sr=rest; held=hs=hr=None
    rows=part.shape[1]
    line=Line(count,pieces,rows,part,sums,(ss,sr),held,(hs,hr))
    greet(line.here,count)
    far=count-1
    def step(t,_):
        line.send_sums(t)
        if gather: line.pass_pieces(t-far)
        u=t-far
        @pl.when(line.fits(u))
        def _():
            line.own_sum(u,total)
            low=finish(line.span(u),total,ins,outs)
            if gather:
                held[line.here,line.span(u)]=low
                line.send_own(u)
        return 0
    lax.fori_loop(0,pieces+(2*far if gather else far),step,0)
    if gather:
        copy=pltpu.make_async_copy(held,whole,ws); copy.start()
    line.end_sums()
    if gather:
        line.end_pieces()
        copy.wait()

def sum_and_finish(part,ins,out_shapes,finish,gather,cid,pieces,tensor):
    n=tensor; rows=part.shape[0]//n; D=part.shape[1]
    vm=pl.BlockSpec(memory_space=pltpu.VMEM)
    outs=list(out_shapes); out_specs=[vm]*len(outs)
    scratch=[pltpu.VMEM((2,n,rows,D),BF),pltpu.VMEM((rows//pieces,D),F32),
        pltpu.SemaphoreType.DMA((2,n,pieces)),pltpu.SemaphoreType.DMA((2,n,pieces))]
    if gather:
        outs.append(jax.ShapeDtypeStruct((n,rows,D),BF)); out_specs.append(pl.BlockSpec(memory_space=pl.ANY))
        scratch+=[pltpu.VMEM((n,rows,D),BF),pltpu.SemaphoreType.DMA((2,n,pieces)),pltpu.SemaphoreType.DMA((2,n,pieces)),pltpu.SemaphoreType.DMA]
    res=pl.pallas_call(functools.partial(turn_over,finish,n,pieces,len(ins),len(out_shapes),gather),
        out_shape=tuple(outs),in_specs=[vm]*(1+len(ins)),out_specs=tuple(out_specs),scratch_shapes=scratch,
        cost_estimate=pl.CostEstimate(flops=0,bytes_accessed=270_000_000,transcendentals=0),
        compiler_params=pltpu.CompilerParams(collective_id=cid,has_side_effects=True,vmem_limit_bytes=56*1024*1024),
    )(part.reshape(n,rows,D),*ins)
    return res


def frequencies(head_size):
    inverse = 1.0 / 500000.0 ** (jnp.arange(head_size // 2, dtype=jnp.float32) * 2.0 / head_size)
    wavelength = 2.0 * math.pi / inverse
    smooth = (8192.0 / wavelength - 1.0) / 3.0
    blended = (1.0 - smooth) * inverse / 32.0 + smooth * inverse
    return jnp.where(
        wavelength > 8192.0, inverse / 32.0, jnp.where(wavelength < 2048.0, inverse, blended)
    )


def dot(left_side, right_side, left_dim, right_dim):
    return lax.dot_general(
        left_side, right_side, (((left_dim,), (right_dim,)), ((), ())), preferred_element_type=F32
    )


def norm_kernel(count, pieces, tokens_ref, gain_ref, whole, held, hs, hr, ws):
    line = Line(count, pieces, tokens_ref.shape[0], held=held, held_sems=(hs, hr))
    greet(line.here, count)

    def step(t, _):
        line.pass_pieces(t)
        u = jnp.clip(t, 0, pieces - 1)

        @pl.when(t < pieces)
        def _():
            stream = tokens_ref[line.span(u), :].astype(F32)
            scale = lax.rsqrt(jnp.mean(stream * stream, -1, keepdims=True) + EPSILON)
            held[line.here, line.span(u)] = (stream * scale * gain_ref[...]).astype(BF)
            line.send_own(u)

        return 0

    lax.fori_loop(0, pieces + count - 1, step, 0)
    copy = pltpu.make_async_copy(held, whole, ws)
    copy.start()
    line.end_pieces()
    copy.wait()


def norm_and_gather(tokens, gain, cid, pieces, count):
    rows, width = tokens.shape
    vm = pl.BlockSpec(memory_space=pltpu.VMEM)
    return pl.pallas_call(
        functools.partial(norm_kernel, count, pieces),
        out_shape=jax.ShapeDtypeStruct((count, rows, width), BF),
        in_specs=[vm, vm],
        out_specs=pl.BlockSpec(memory_space=pl.ANY),
        scratch_shapes=[
            pltpu.VMEM((count, rows, width), BF),
            pltpu.SemaphoreType.DMA((2, count, pieces)),
            pltpu.SemaphoreType.DMA((2, count, pieces)),
            pltpu.SemaphoreType.DMA,
        ],
        cost_estimate=pl.CostEstimate(flops=0, bytes_accessed=270_000_000, transcendentals=0),
        compiler_params=pltpu.CompilerParams(
            collective_id=cid, has_side_effects=True, vmem_limit_bytes=40 * 1024 * 1024
        ),
    )(tokens, gain).reshape(count * rows, width)


def finish_attention(span, total, ins, outs):
    tokens, gain = ins
    residual = total[...] + tokens[span, :].astype(F32)
    outs[0][span, :] = residual
    scale = lax.rsqrt(jnp.mean(residual * residual, -1, keepdims=True) + EPSILON)
    return (residual * scale * gain[...]).astype(BF)


def finish_residual(span, total, ins, outs):
    residual_ref, grad_out, gain, start = ins
    residual = residual_ref[span, :]
    scale = lax.rsqrt(jnp.mean(residual * residual, -1, keepdims=True) + EPSILON)
    unit = residual * scale
    grads = total[...]
    outs[1][span, :] = grads * unit
    scaled = grads * gain[...]
    grad_residual = grad_out[span, :].astype(F32) + scale * (
        scaled - unit * jnp.mean(scaled * unit, -1, keepdims=True)
    )
    outs[0][span, :] = grad_residual
    return grad_residual.astype(BF)


def finish_tokens(span, total, ins, outs):
    tokens, grad_residual, gain = ins
    stream = tokens[span, :].astype(F32)
    scale = lax.rsqrt(jnp.mean(stream * stream, -1, keepdims=True) + EPSILON)
    unit = stream * scale
    grads = total[...]
    outs[1][span, :] = grads * unit
    scaled = grads * gain[...]
    outs[0][span, :] = grad_residual[span, :] + scale * (
        scaled - unit * jnp.mean(scaled * unit, -1, keepdims=True)
    )


def ring_gather(piece, count):
    rows, width = piece.shape
    half = rows // 2
    here = lax.axis_index(AXIS)
    right = [(k, (k + 1) % count) for k in range(count)]
    left = [(k, (k - 1) % count) for k in range(count)]
    one, two = piece[:half], piece[half:]
    whole = jnp.zeros((count, rows, width), piece.dtype)
    whole = lax.dynamic_update_slice(whole, piece[None], (here, 0, 0))
    for step in range(1, count):
        one = lax.ppermute(one, AXIS, right)
        two = lax.ppermute(two, AXIS, left)
        whole = lax.dynamic_update_slice(whole, one[None], ((here - step) % count, 0, 0))
        whole = lax.dynamic_update_slice(whole, two[None], ((here + step) % count, half, 0))
    return whole.reshape(count * rows, width)


def ring_sum(part, count):
    width = part.shape[1]
    half = part.shape[0] // count // 2
    here = lax.axis_index(AXIS)
    right = [(k, (k + 1) % count) for k in range(count)]
    left = [(k, (k - 1) % count) for k in range(count)]
    cut = part.reshape(count, 2, half, width)

    def term(owner, side):
        return lax.dynamic_slice(cut, (owner % count, side, 0, 0), (1, 1, half, width))[0, 0]

    one, two = term(here - 1, 0), term(here + 1, 1)
    for step in range(1, count):
        one = lax.ppermute(one, AXIS, right)
        two = lax.ppermute(two, AXIS, left)
        last = step == count - 1
        one = one.astype(F32) + term(here - step - 1, 0).astype(F32)
        two = two.astype(F32) + term(here + step + 1, 1).astype(F32)
        if not last:
            one, two = one.astype(BF), two.astype(BF)
    return jnp.concatenate([one, two], 0)


def body(
    count,
    tokens,
    segments,
    positions,
    attn_gain,
    w_query,
    w_key,
    w_value,
    w_out,
    mlp_gain,
    w_gate,
    w_up,
    w_down,
    grad_out,
):
    rows, width = tokens.shape
    heads = w_query.shape[1] // HD
    groups = w_key.shape[1] // HD
    gains = lax.all_gather(jnp.stack([attn_gain, mlp_gain]).astype(F32), "dp", axis=1, tiled=True)
    gain_one, gain_two = gains[0:1], gains[1:2]
    mix = lax.all_gather(jnp.concatenate([w_query, w_key, w_value], 1), "dp", axis=0, tiled=True)
    full_out = lax.all_gather(w_out, "dp", axis=1, tiled=True)
    full_gate = lax.all_gather(w_gate, "dp", axis=0, tiled=True)
    full_up = lax.all_gather(w_up, "dp", axis=0, tiled=True)
    full_down = lax.all_gather(w_down, "dp", axis=1, tiled=True)

    normed_one = norm_and_gather(tokens, gain_one, 1, 4, count)
    angles = frequencies(HD)[:, None] * positions.astype(F32)[None, :]
    cosine, sine = jnp.cos(angles), jnp.sin(angles)
    lin = dot(mix, normed_one, 0, 1)
    mixed, lse, q, kt, k, vt, v = attend(lin, cosine, sine, segments, heads, groups)
    grad_late, normed_late = lax.optimization_barrier((grad_out, normed_one))
    grad_rows = ring_gather(grad_late, count)

    part = dot(mixed, full_out, 0, 0).astype(BF)
    residual, normed_two = sum_and_finish(
        part, (tokens, gain_two), (jax.ShapeDtypeStruct((rows, width), F32),),
        finish_attention, True, 2, 16, count,
    )
    normed_two = normed_two.reshape(count * rows, width)
    gate_values = dot(normed_two, full_gate, 1, 0)
    up_values = dot(normed_two, full_up, 1, 0)
    sigmoid_gate = jax.nn.sigmoid(gate_values)
    activated = gate_values * sigmoid_gate
    product = (activated * up_values).astype(BF)
    down = ring_sum(dot(product, full_down, 1, 0).astype(BF), count)
    block_out = (residual + down).astype(BF)
    grad_product = dot(grad_rows, full_down, 1, 1)
    grad_gated = (
        grad_product * up_values * sigmoid_gate * (1.0 + gate_values * (1.0 - sigmoid_gate))
    ).astype(BF)
    grad_lifted = (grad_product * activated).astype(BF)
    part = (dot(grad_gated, full_gate, 1, 1) + dot(grad_lifted, full_up, 1, 1)).astype(BF)
    grad_down = lax.psum_scatter(dot(product, grad_rows, 0, 0).astype(BF), "dp", scatter_dimension=1, tiled=True)
    grad_gate = lax.psum_scatter(dot(normed_two, grad_gated, 0, 0).astype(BF), "dp", scatter_dimension=0, tiled=True)
    grad_up = lax.psum_scatter(dot(normed_two, grad_lifted, 0, 0).astype(BF), "dp", scatter_dimension=0, tiled=True)
    wide = jax.ShapeDtypeStruct((rows, width), F32)
    grad_residual, terms_two, grad_low = sum_and_finish(
        part, (residual, grad_out, gain_two, gain_two), (wide, wide), finish_residual, True, 3, 16, count
    )
    grad_low = grad_low.reshape(count * rows, width)
    grad_mixed = dot(full_out, grad_low, 1, 1).astype(BF)
    grad_out_proj = lax.psum_scatter(dot(mixed, grad_low, 1, 0).astype(BF), "dp", scatter_dimension=1, tiled=True)
    turned = attend_back(q, kt, k, v, lse, grad_mixed, cosine, sine, segments, heads, groups)
    part = dot(turned, mix, 0, 1).astype(BF)
    grad_mix = lax.psum_scatter(dot(normed_one, turned, 0, 1).astype(BF), "dp", scatter_dimension=0, tiled=True)
    grad_tokens, terms_one = sum_and_finish(
        part, (tokens, grad_residual, gain_one), (wide, wide), finish_tokens, False, 4, 4, count
    )
    sums = lax.psum(jnp.stack([jnp.sum(terms_one, 0), jnp.sum(terms_two, 0)]), ("dp", AXIS))
    place = lax.axis_index("dp") * attn_gain.shape[0]
    sums = lax.dynamic_slice(sums, (0, place), (2, attn_gain.shape[0]))
    edges = (heads * HD, (heads + groups) * HD)
    grad_query, grad_key, grad_value = jnp.split(grad_mix.astype(F32), edges, 1)
    return (
        block_out,
        grad_tokens,
        sums[0],
        grad_query,
        grad_key,
        grad_value,
        grad_out_proj.astype(F32),
        sums[1],
        grad_gate.astype(F32),
        grad_up.astype(F32),
        grad_down.astype(F32),
    )


def solution(mesh):
    placed = (
        P(("dp", "tensor"), None),
        P("dp"),
        P("dp"),
        P("dp"),
        P("dp", "tensor"),
        P("dp", "tensor"),
        P("dp", "tensor"),
        P("tensor", "dp"),
        P("dp"),
        P("dp", "tensor"),
        P("dp", "tensor"),
        P("tensor", "dp"),
        P(("dp", "tensor"), None),
    )
    return jax.shard_map(
        functools.partial(body, mesh.shape["tensor"]),
        mesh=mesh,
        in_specs=placed,
        out_specs=(
            P(("dp", "tensor"), None),
            P(("dp", "tensor"), None),
            P("dp"),
            P("dp", "tensor"),
            P("dp", "tensor"),
            P("dp", "tensor"),
            P("tensor", "dp"),
            P("dp"),
            P("dp", "tensor"),
            P("dp", "tensor"),
            P("tensor", "dp"),
        ),
        check_vma=False,
    )
```

time: 1910 us -> 866 us (0.45)
  waiting for transfers between devices: 1390 us -> 119 us
  Pallas kernels: 0 us -> 438 us
  matrix products: 268 us -> 172 us
  local copies, waits for them, and re-layouts: 80.5 us -> 18.9 us
  other arithmetic: 64.7 us -> 22.2 us
  blocking collectives: 74.7 us -> 47.9 us
  starting transfers between devices: 1.27 us -> 24 us
    reduce_scatter x11 -> x5, waiting for transfers between devices: 925 us -> 25 us  [the longest x1 25 us: body(): lax.psum_scatter(dot(product, grad_rows, 0, 0).astype(BF), 'dp', scatter_...]
    all_gather x9 -> x5, waiting for transfers between devices: 460 us -> 0.03 us  [the longest x1 0.02 us: body(): full_gate = lax.all_gather(w_gate, 'dp', axis=0, tiled=True)]
    pallas_call x0 -> x6, Pallas kernels: none -> 438 us  [the longest x3 314 us: sum_and_finish(): pl.pallas_call(functools.partial(turn_over, finish, n, pieces, len(ins),...]
    dot_general x35 -> x15, matrix products: 268 us -> 172 us  [dot(): lax.dot_general(left_side, right_side, (((left_dim,), (right_dim,)), ((),...]
    ppermute x0 -> x12, waiting for transfers between devices: none -> 91.8 us  [the longest x3 27.6 us: ring_gather(): one = lax.ppermute(one, AXIS, right)]
    dynamic_update_slice x4 -> x7, local copies, waits for them, and re-layouts: 41.4 us -> 6.16 us  [the longest x3 2.58 us: ring_gather(): lax.dynamic_update_slice(whole, two[None], ((here + step) % count, half, 0))]
    all_gather x4 -> x1, blocking collectives: 37.9 us -> 10.4 us  [body(): lax.all_gather(jnp.stack([attn_gain, mlp_gain]).astype(F32), 'dp', axis=1...]
    psum x1, blocking collectives: 12.8 us -> 37.6 us  [body(): lax.psum(jnp.stack([jnp.sum(terms_one, 0), jnp.sum(terms_two, 0)]), ('dp'...]
  transfers between devices with their start and end apart: 20 -> 22, of which waited for: 19 -> 11; matrix products, arithmetic and copies ran while one was open for 10% -> 17% of each run, Pallas kernels for 0% -> 37%
where the time goes in v1:
time: 866 us; the launch traced here: 857 us
  Pallas kernels  438 us (51%)
  matrix products  172 us (20%)
  waiting for transfers between devices  119 us (14%)
  blocking collectives  47.9 us (6%)
  starting transfers between devices  24 us (3%)
  other arithmetic  22.2 us (3%)
  local copies, waits for them, and re-layouts  18.9 us (2%)
  between operations  15.2 us (2%)
    pallas_call x3, Pallas kernels, sum_and_finish(): pl.pallas_call(functools.partial(turn_over, finish, n, pieces, len(ins),...  314 us
    dot_general x15, matrix products, dot(): lax.dot_general(left_side, right_side, (((left_dim,), (right_dim,)), ((),...  172 us
    pallas_call x1, Pallas kernels, norm_and_gather(): pl.pallas_call(functools.partial(norm_kernel, count, pieces), out_shape=j...  74.9 us
    psum x1, blocking collectives, body(): lax.psum(jnp.stack([jnp.sum(terms_one, 0), jnp.sum(terms_two, 0)]), ('dp'...  37.6 us
    pallas_call x1, Pallas kernels, attend_back(): pl.pallas_call(functools.partial(attend_back_kernel, heads, groups, block...  28.7 us
    ppermute x3, waiting for transfers between devices, ring_gather(): one = lax.ppermute(one, AXIS, right)  27.6 us
    reduce_scatter x1, waiting for transfers between devices, body(): lax.psum_scatter(dot(product, grad_rows, 0, 0).astype(BF), 'dp', scatter_...  25 us
    ppermute x3, waiting for transfers between devices, ring_sum(): one = lax.ppermute(one, AXIS, right)  24.9 us
  transfers between devices with their start and end apart: 22, of which 11 were waited for; matrix products, arithmetic and copies ran while one was open for 17% of the time, Pallas kernels for 37%

profile of v1, /device:TPU:0, one launch (start us, length us, event | category | flops | bytes accessed | tf_op | source)
XLA Modules:
  0.0 857.4 jit_solution(1484763418485833530)
XLA Ops:
  7.3 1.9 pad_maximum_fusion
  11.9 10.4 %all_gather.19 = f32[2,2048]{1,0:T(2,128)S(1)} all-gather(f32[2,256]{1,0:T(2,128)S(1)} %maximum_convert_fusion), channel_id=1, replica_groups=mesh['dp'=8,'tensor'=4] {'dp'}, dimensions={1}, use_global_device_ids=true | all-gather | bytes 18432 | tf_op jit(solution)/shard_map/all_gather | solution.py:449
  22.9 74.9 %shard_map.212 = bf16[4,256,2048]{2,1,0:T(8,128)(2,1)S(1)} custom-call(bf16[256,2048]{1,0:T(8,128)(2,1)S(1)} %copy-done, f32[1,2048]{1,0:T(1,128)S(1)} %get-tuple-element.57.gain_ref.refs_3_), custom_call_target="tpu_custom_call" | custom-call | bytes 270000000 | tf_op jit(solution)/shard_map/pallas_call | solution.py:336
  97.8 2.0 copy-done.1
  100.7 3.8 collective-permute-start.7
  105.5 2.5 broadcast_in_dim.26
  109.0 8.5 collective-permute-done.6
  117.6 7.1 collective-permute-done.7
  124.7 4.1 collective-permute-start.9
  130.5 9.6 %collective-permute-done.8 = bf16[128,2048]{1,0:T(8,128)(2,1)S(1)} collective-permute-done((bf16[128,2048]{1,0:T(8,128)(2,1)S(1)}, bf16[128,2048]{1,0:T(8,128)(2,1)S(1)}, u32[]{:S(2)}, u32[]{:S(2)}) %collective-permute-start.8) | collective-permute-done | bytes 524320 | tf_op jit(solution)/shard_map/ppermute | solution.py:400
  140.1 7.2 collective-permute-done.9
  147.3 4.1 collective-permute-start.11
  153.1 9.5 %collective-permute-done.10 = bf16[128,2048]{1,0:T(8,128)(2,1)S(1)} collective-permute-done((bf16[128,2048]{1,0:T(8,128)(2,1)S(1)}, bf16[128,2048]{1,0:T(8,128)(2,1)S(1)}, u32[]{:S(2)}, u32[]{:S(2)}) %collective-permute-start.10) | collective-permute-done | bytes 524320 | tf_op jit(solution)/shard_map/ppermute | solution.py:400
  163.4 6.1 collective-permute-done.11
  170.4 8.2 fusion.11.lin_ref
  178.6 20.8 %shard_map.213 = (bf16[512,1024]{1,0:T(8,128)(2,1)S(1)}, f32[8,1,1024]{2,1,0:T(1,128)S(1)}, bf16[512,1024]{1,0:T(8,128)(2,1)S(1)}, bf16[128,1024]{1,0:T(8,128)(2...) custom-call(f32[768,1024]{1,0:T(8,128)} %fusion.11.lin_ref, ...), custom_call_target="tpu_custom_call" | custom-call | flops 30000001024 | bytes 10000000 | tf_op jit(solution)/shard_map/pallas_call | solution.py:73
  200.4 6.3 convolution_convert_fusion.4
  206.6 121.8 %shard_map.214 = (f32[256,2048]{1,0:T(8,128)}, bf16[4,256,2048]{2,1,0:T(8,128)(2,1)}) custom-call(bf16[4,256,2048]{2,1,0:T(8,128)(2,1)} %bitcast.88, bf16[256,2048]{1,0:T(8,128)(2,1)} %refs_1_.3, f32[1,2048]{1,0:T(1,128)} %get-tuple-element.56.refs_2_.refs_3_.refs_4_), custom_call_target="tpu_custom_call" | custom-call | bytes 270000000 | tf_op jit(solution)/shard_map/pallas_call | solution.py:285
  328.5 14.6 %fusion.12 = f32[1024,2048]{1,0:T(8,128)} fusion(bf16[1024,2048]{1,0:T(8,128)(2,1)} %bitcast.98, bf16[2048,2048]{1,0:T(8,128)(2,1)} %all-gather.10.cloned.1.call-done), kind=kOutput, calls=%fused_computation.50 | convolution fusion | flops 8589934592 | bytes 20971520 | tf_op jit(solution)/shard_map/dot_general | solution.py:304
  343.1 14.6 %fusion.13 = f32[1024,2048]{1,0:T(8,128)} fusion(bf16[1024,2048]{1,0:T(8,128)(2,1)} %bitcast.99, bf16[2048,2048]{1,0:T(8,128)(2,1)} %all-gather.12.cloned.1.call-done), kind=kOutput, calls=%fused_computation.51 | convolution fusion | flops 8589934592 | bytes 20971520 | tf_op jit(solution)/shard_map/dot_general | solution.py:304
  357.6 22.2 %multiply_convert_fusion = (bf16[1024,2048]{1,0:T(8,128)(2,1)}, bf16[1024,2048]{1,0:T(8,128)(2,1)}, bf16[1024,2048]{1,0:T(8,128)(2,1)}) fusion(f32[1024,2048]{1,0:T(8,128)} %fusion.12, f32[1024,2048]{1,0:T(8,128)} %fusion.13, bf16[1024,2048]{1,0:T(8,128)(2,1)} %bitcast.21, bf16[2048,2048]{1,0:T(8,128)(2,1)} %all-gather.14.cloned.1.call-done), kind=kOutput, calls=%fused_computation.1 | convolution fusion | flops 8621391872 | bytes 41943040 | tf_op jit(solution)/shard_map/dot_general | solution.py:304
  379.9 14.8 %fusion.14 = f32[1024,2048]{1,0:T(8,128)} fusion(bf16[1024,2048]{1,0:T(8,128)(2,1)} %get-tuple-element.40, bf16[2048,2048]{1,0:T(8,128)(2,1)} %all-gather.10.cloned.1.call-done), kind=kOutput, calls=%fused_computation.52 | convolution fusion | flops 8589934592 | bytes 20971520 | tf_op jit(solution)/shard_map/dot_general | solution.py:304
  394.7 12.2 %add_convert_fusion = bf16[1024,2048]{1,0:T(8,128)(2,1)} fusion(f32[1024,2048]{1,0:T(8,128)} %fusion.14, bf16[1024,2048]{1,0:T(8,128)(2,1)S(1)} %copy-done.17, bf16[2048,2048]{1,0:T(8,128)(2,1)S(1)} %copy-done.14), kind=kOutput, calls=%fused_computation | convolution fusion | flops 8594128896 | bytes 25165824 | tf_op jit(solution)/shard_map/dot_general | solution.py:304
  406.8 118.3 %shard_map.215 = (f32[256,2048]{1,0:T(8,128)}, f32[256,2048]{1,0:T(8,128)}, bf16[4,256,2048]{2,1,0:T(8,128)(2,1)}) custom-call(bf16[4,256,2048]{2,1,0:T(8,128)(2,1)} %bitcast.87, f32[256,2048]{1,0:T(8,128)} %get-tuple-element.26.refs_1_, bf16[256,2048]{1,0:T(8,128)(2,1)} %refs_2_.1, f32[1,2048]{1,0:T(1,128)} %get-tuple-element.56.refs_2_.refs_3_.refs_4_, ...), custom_call_target="tpu_custom_call" | custom-call | bytes 270000000 | tf_op jit(solution)/shard_map/pallas_call | solution.py:285
  525.1 5.9 convolution_convert_fusion.7
  531.1 5.3 fusion.2.gm_ref
  536.5 28.7 %shard_map.216 = bf16[768,1024]{1,0:T(8,128)(2,1)S(1)} custom-call(bf16[512,1024]{1,0:T(8,128)(2,1)S(1)} %copy-done.6, bf16[128,1024]{1,0:T(8,128)(2,1)S(1)} %get-tuple-element.29.kt_ref, bf16[2,1024,64]{2,1,0:T(8,128)(2,1)S(1)} %get-tuple-element.30.k_ref, bf16[2,1024,64]{2,1,0:T(8,128)(2,1)S(1)} %copy-done.8, f32[8,1,1024]{2,1,0:T(1,128)S(1)} %get-tuple-element.32.lse_ref, ...), custom_call_target="tpu_custom_call" | custom-call | flops 60000002048 | bytes 10000000 | tf_op jit(solution)/shard_map/pallas_call | solution.py:133
  565.2 5.0 convolution_convert_fusion.6
  570.2 14.3 %convolution_convert_fusion.2 = bf16[2048,2048]{1,0:T(8,128)(2,1)} fusion(bf16[1024,2048]{1,0:T(8,128)(2,1)} %bitcast.100, bf16[1024,2048]{1,0:T(8,128)(2,1)} %get-tuple-element.40), kind=kOutput, calls=%fused_computation.8 | convolution fusion | flops 8594128896 | bytes 16777216 | tf_op jit(solution)/shard_map/dot_general | solution.py:304
  584.6 14.5 %convolution_convert_fusion.1 = bf16[2048,2048]{1,0:T(8,128)(2,1)} fusion(bf16[1024,2048]{1,0:T(8,128)(2,1)} %bitcast.101, bf16[1024,2048]{1,0:T(8,128)(2,1)} %get-tuple-element.39), kind=kOutput, calls=%fused_computation.7 | convolution fusion | flops 8594128896 | bytes 16777216 | tf_op jit(solution)/shard_map/dot_general | solution.py:304
  599.2 14.3 %convolution_convert_fusion = bf16[2048,2048]{1,0:T(8,128)(2,1)} fusion(bf16[1024,2048]{1,0:T(8,128)(2,1)} %get-tuple-element.41, bf16[1024,2048]{1,0:T(8,128)(2,1)} %bitcast.21), kind=kOutput, calls=%fused_computation.6 | convolution fusion | flops 8594128896 | bytes 16777216 | tf_op jit(solution)/shard_map/dot_general | solution.py:304
  613.5 12.5 %convolution_convert_fusion.3 = bf16[1024,2048]{1,0:T(8,128)(2,1)S(1)} fusion(bf16[1024,2048]{1,0:T(8,128)(2,1)} %get-tuple-element.41, bf16[2048,2048]{1,0:T(8,128)(2,1)} %all-gather.14.cloned.1.call-done), kind=kOutput, calls=%fused_computation.9 | convolution fusion | flops 8592031744 | bytes 16777216 | tf_op jit(solution)/shard_map/dot_general | solution.py:304
  626.2 3.8 collective-permute-start.3
  630.0 12.8 %collective-permute-done = bf16[128,2048]{1,0:T(8,128)(2,1)S(1)} collective-permute-done((bf16[128,2048]{1,0:T(8,128)(2,1)S(1)}, bf16[128,2048]{1,0:T(8,128)(2,1)S(1)}, u32[]{:S(2)}, u32[]{:S(2)}) %collective-permute-start) | collective-permute-done | bytes 524320 | tf_op jit(solution)/shard_map/ppermute | solution.py:420
  642.8 8.2 collective-permute-done.3
  652.7 2.6 collective-permute-start.4
  655.3 12.1 %collective-permute-done.1 = bf16[128,2048]{1,0:T(8,128)(2,1)S(1)} collective-permute-done((bf16[128,2048]{1,0:T(8,128)(2,1)S(1)}, bf16[128,2048]{1,0:T(8,128)(2,1)S(1)}, u32[]{:S(2)}, u32[]{:S(2)}) %collective-permute-start.1) | collective-permute-done | bytes 524320 | tf_op jit(solution)/shard_map/ppermute | solution.py:420
  667.4 10.7 %collective-permute-done.4 = bf16[128,2048]{1,0:T(8,128)(2,1)} collective-permute-done((bf16[128,2048]{1,0:T(8,128)(2,1)S(1)}, bf16[128,2048]{1,0:T(8,128)(2,1)}, u32[]{:S(2)}, u32[]{:S(2)}) %collective-permute-start.4) | collective-permute-done | bytes 524320 | tf_op jit(solution)/shard_map/ppermute | solution.py:421
  678.0 2.7 fusion.5
  681.5 3.1 collective-permute-start.5
  684.6 7.0 convolution_convert_fusion.5
  691.6 73.7 %shard_map.217 = (f32[256,2048]{1,0:T(8,128)}, f32[256,2048]{1,0:T(8,128)}) custom-call(bf16[4,256,2048]{2,1,0:T(8,128)(2,1)} %bitcast.93, bf16[256,2048]{1,0:T(8,128)(2,1)} %refs_1_.3, f32[256,2048]{1,0:T(8,128)} %get-tuple-element.35.refs_2_, f32[1,2048]{1,0:T(1,128)} %copy-done.3), custom_call_target="tpu_custom_call" | custom-call | bytes 270000000 | tf_op jit(solution)/shard_map/pallas_call | solution.py:285
  765.3 1.9 reduce_sum.19
  769.0 37.6 %psum.7 = f32[2,2048]{1,0:T(2,128)S(1)} all-reduce(f32[2,2048]{1,0:T(2,128)S(1)} %pad_maximum_fusion.1), channel_id=1, replica_groups=mesh['dp'=8,'tensor'=4] {'dp','tensor'}, use_global_device_ids=true, to_apply=%region_2.3 | all-reduce | flops 4096 | bytes 32768 | tf_op jit(solution)/shard_map/psum | solution.py:500
  815.2 2.9 convert_element_type.170
  818.2 2.8 convert_element_type.172
  821.0 25.0 %reduce-scatter.14.cloned.1.call-done = bf16[2048,256]{1,0:T(8,128)(2,1)} async-done(((bf16[2048,2048]{1,0:T(8,128)(2,1)}), bf16[2048,256]{1,0:T(8,128)(2,1)}) %reduce-scatter.14.cloned.1.call-update) | async-done | bytes 1048592 | tf_op jit(solution)/shard_map/reduce_scatter | solution.py:484
  846.0 2.7 convert_element_type.174
  (99 shorter events, 26.8 us)
Async XLA Ops:
  7.2 4.7 copy-start.15
  7.2 4.7 copy-start.16
  7.2 15.7 %copy-start = (bf16[256,2048]{1,0:T(8,128)(2,1)S(1)}, bf16[256,2048]{1,0:T(8,128)(2,1)}, u32[]{:S(2)}) copy-start(bf16[256,2048]{1,0:T(8,128)(2,1)} %refs_1_.3) | copy-start | bytes 3145732
  7.2 163.2 %all-gather.6.cloned.1.call-start = ((), (), s32[]{:S(2)}) async-start(), calls=%async_computation.5 | async-start | bytes 3538944 | tf_op jit(solution)/shard_map/all_gather | solution.py:451
  9.2 191.2 %all-gather.8.cloned.1.call-start = ((), (), s32[]{:S(2)}) async-start(), calls=%async_computation.6 | async-start | bytes 2359296 | tf_op jit(solution)/shard_map/all_gather | solution.py:452
  9.9 89.9 %copy-start.9 = (bf16[256,2048]{1,0:T(8,128)(2,1)S(1)}, bf16[256,2048]{1,0:T(8,128)(2,1)}, u32[]{:S(2)}) copy-start(bf16[256,2048]{1,0:T(8,128)(2,1)} %refs_2_.1) | copy-start | bytes 3145732
  9.9 318.6 %all-gather.10.cloned.1.call-start = ((), (), s32[]{:S(2)}) async-start(), calls=%async_computation.7 | async-start | bytes 9437184 | tf_op jit(solution)/shard_map/all_gather | solution.py:453
  10.7 332.4 %all-gather.12.cloned.1.call-start = ((), (), s32[]{:S(2)}) async-start(), calls=%async_computation.8 | async-start | bytes 9437184 | tf_op jit(solution)/shard_map/all_gather | solution.py:454
  11.2 93.3 %copy-start.13 = (s32[1024]{0:T(1024)S(1)}, s32[1024]{0:T(1024)}, u32[]{:S(2)}) copy-start(s32[1024]{0:T(1024)} %param.15) | copy-start | bytes 12292
  11.2 346.4 %all-gather.14.cloned.1.call-start = ((), (), s32[]{:S(2)}) async-start(), calls=%async_computation.9 | async-start | bytes 9437184 | tf_op jit(solution)/shard_map/all_gather | solution.py:455
  11.8 93.4 %copy-start.4 = (s32[1024]{0:T(1024)S(1)}, s32[1024]{0:T(1024)}, u32[]{:S(2)}) copy-start(s32[1024]{0:T(1024)} %param.14) | copy-start | bytes 12292
  11.8 798.2 %reduce-scatter.8.cloned.1.call-start = ((), (), s32[]{:S(2)}) async-start(), calls=%async_computation.11 | async-start | bytes 2359296 | tf_op jit(solution)/shard_map/reduce_scatter | solution.py:493
  22.9 81.6 %copy-start.3 = (f32[1,2048]{1,0:T(1,128)}, f32[1,2048]{1,0:T(1,128)S(1)}, u32[]{:S(2)}) copy-start(f32[1,2048]{1,0:T(1,128)S(1)} %get-tuple-element.57.gain_ref.refs_3_) | copy-start | bytes 24580
  97.8 2.0 copy-start.1
  100.7 16.9 %collective-permute-start.6 = (bf16[128,2048]{1,0:T(8,128)(2,1)}, bf16[128,2048]{1,0:T(8,128)(2,1)S(1)}, u32[]{:S(2)}, u32[]{:S(2)}) collective-permute-start(bf16[128,2048]{1,0:T(8,128)(2,1)} %get-tuple-element.51), channel_id=1, source_target_pairs={{0,1},{1,2},{2,3},{3,0},{4,5},{5,6},{6,7},{7,4},{8,9},{9,10},{10,1... | collective-permute-start | bytes 1572872 | tf_op jit(solution)/shard_map/ppermute | solution.py:400
  100.7 24.0 %collective-permute-start.7 = (bf16[128,2048]{1,0:T(8,128)(2,1)S(1)}, bf16[128,2048]{1,0:T(8,128)(2,1)S(1)}, u32[]{:S(2)}, u32[]{:S(2)}) collective-permute-start(bf16[128,2048]{1,0:T(8,128)(2,1)S(1)} %get-tuple-element.50), channel_id=1, source_target_pairs={{0,3},{1,0},{2,1},{3,2},{4,7},{5,4},{6,5},{7,6},{8,11},{9,8},{10,9... | collective-permute-start | bytes 1572872 | tf_op jit(solution)/shard_map/ppermute | solution.py:401
  117.6 22.5 %collective-permute-start.8 = (bf16[128,2048]{1,0:T(8,128)(2,1)S(1)}, bf16[128,2048]{1,0:T(8,128)(2,1)S(1)}, u32[]{:S(2)}, u32[]{:S(2)}) collective-permute-start(bf16[128,2048]{1,0:T(8,128)(2,1)S(1)} %collective-permute-done.6), channel_id=1, source_target_pairs={{0,1},{1,2},{2,3},{3,0},{4,5},{5,6},{6,7},{7,4},{8,9},{9,10},{10,1... | collective-permute-start | bytes 1572872 | tf_op jit(solution)/shard_map/ppermute | solution.py:400
  124.7 22.6 %collective-permute-start.9 = (bf16[128,2048]{1,0:T(8,128)(2,1)S(1)}, bf16[128,2048]{1,0:T(8,128)(2,1)S(1)}, u32[]{:S(2)}, u32[]{:S(2)}) collective-permute-start(bf16[128,2048]{1,0:T(8,128)(2,1)S(1)} %collective-permute-done.7), channel_id=1, source_target_pairs={{0,3},{1,0},{2,1},{3,2},{4,7},{5,4},{6,5},{7,6},{8,11},{9,8},{10,9... | collective-permute-start | bytes 1572872 | tf_op jit(solution)/shard_map/ppermute | solution.py:401
  140.1 22.5 %collective-permute-start.10 = (bf16[128,2048]{1,0:T(8,128)(2,1)S(1)}, bf16[128,2048]{1,0:T(8,128)(2,1)S(1)}, u32[]{:S(2)}, u32[]{:S(2)}) collective-permute-start(bf16[128,2048]{1,0:T(8,128)(2,1)S(1)} %collective-permute-done.8), channel_id=1, source_target_pairs={{0,1},{1,2},{2,3},{3,0},{4,5},{5,6},{6,7},{7,4},{8,9},{9,10},{10,1... | collective-permute-start | bytes 1572872 | tf_op jit(solution)/shard_map/ppermute | solution.py:400
  147.3 22.3 %collective-permute-start.11 = (bf16[128,2048]{1,0:T(8,128)(2,1)S(1)}, bf16[128,2048]{1,0:T(8,128)(2,1)S(1)}, u32[]{:S(2)}, u32[]{:S(2)}) collective-permute-start(bf16[128,2048]{1,0:T(8,128)(2,1)S(1)} %collective-permute-done.9), channel_id=1, source_target_pairs={{0,3},{1,0},{2,1},{3,2},{4,7},{5,4},{6,5},{7,6},{8,11},{9,8},{10,9... | collective-permute-start | bytes 1572872 | tf_op jit(solution)/shard_map/ppermute | solution.py:401
  199.4 1.0 copy-start.5
  200.4 6.3 copy-start.7
  379.9 14.8 %copy-start.14 = (bf16[2048,2048]{1,0:T(8,128)(2,1)S(1)}, bf16[2048,2048]{1,0:T(8,128)(2,1)}, u32[]{:S(2)}) copy-start(bf16[2048,2048]{1,0:T(8,128)(2,1)} %all-gather.12.cloned.1.call-done) | copy-start | bytes 25165828
  379.9 14.8 %copy-start.17 = (bf16[1024,2048]{1,0:T(8,128)(2,1)S(1)}, bf16[1024,2048]{1,0:T(8,128)(2,1)}, u32[]{:S(2)}) copy-start(bf16[1024,2048]{1,0:T(8,128)(2,1)} %get-tuple-element.39) | copy-start | bytes 12582916
  531.0 280.8 %reduce-scatter.6.cloned.1.call-start = ((), (), s32[]{:S(2)}) async-start(), calls=%async_computation.10 | async-start | bytes 3538944 | tf_op jit(solution)/shard_map/reduce_scatter | solution.py:496
  531.1 5.4 copy-start.6
  531.1 5.4 copy-start.8
  536.4 28.7 %copy-start.2 = (bf16[4,256,2048]{2,1,0:T(8,128)(2,1)S(1)}, bf16[4,256,2048]{2,1,0:T(8,128)(2,1)}, u32[]{:S(2)}) copy-start(bf16[4,256,2048]{2,1,0:T(8,128)(2,1)} %copy-done.1) | copy-start | bytes 12582916
  570.2 245.1 %reduce-scatter.10.cloned.1.call-start = ((), (), s32[]{:S(2)}) async-start(), calls=%async_computation.12 | async-start | bytes 9437184 | tf_op jit(solution)/shard_map/reduce_scatter | solution.py:485
  584.5 233.7 %reduce-scatter.12.cloned.1.call-start = ((), (), s32[]{:S(2)}) async-start(), calls=%async_computation.13 | async-start | bytes 9437184 | tf_op jit(solution)/shard_map/reduce_scatter | solution.py:486
  599.1 246.9 %reduce-scatter.14.cloned.1.call-start = ((), (), s32[]{:S(2)}) async-start(), calls=%async_computation.14 | async-start | bytes 9437184 | tf_op jit(solution)/shard_map/reduce_scatter | solution.py:484
  626.0 25.0 %copy-start.11 = (bf16[1024,2048]{1,0:T(8,128)(2,1)}, bf16[1024,2048]{1,0:T(8,128)(2,1)S(1)}, u32[]{:S(2)}) copy-start(bf16[1024,2048]{1,0:T(8,128)(2,1)S(1)} %convolution_convert_fusion.3) | copy-start | bytes 12582916
  626.1 16.7 %collective-permute-start = (bf16[128,2048]{1,0:T(8,128)(2,1)S(1)}, bf16[128,2048]{1,0:T(8,128)(2,1)S(1)}, u32[]{:S(2)}, u32[]{:S(2)}) collective-permute-start(bf16[128,2048]{1,0:T(8,128)(2,1)S(1)} %get-tuple-element.48), channel_id=1, source_target_pairs={{0,1},{1,2},{2,3},{3,0},{4,5},{5,6},{6,7},{7,4},{8,9},{9,10},{10,1... | collective-permute-start | bytes 1572872 | tf_op jit(solution)/shard_map/ppermute | solution.py:420
  626.2 24.9 %collective-permute-start.3 = (bf16[128,2048]{1,0:T(8,128)(2,1)S(1)}, bf16[128,2048]{1,0:T(8,128)(2,1)S(1)}, u32[]{:S(2)}, u32[]{:S(2)}) collective-permute-start(bf16[128,2048]{1,0:T(8,128)(2,1)S(1)} %get-tuple-element.49), channel_id=1, source_target_pairs={{0,3},{1,0},{2,1},{3,2},{4,7},{5,4},{6,5},{7,6},{8,11},{9,8},{10,9... | collective-permute-start | bytes 1572872 | tf_op jit(solution)/shard_map/ppermute | solution.py:421
  651.4 16.0 %collective-permute-start.1 = (bf16[128,2048]{1,0:T(8,128)(2,1)S(1)}, bf16[128,2048]{1,0:T(8,128)(2,1)S(1)}, u32[]{:S(2)}, u32[]{:S(2)}) collective-permute-start(bf16[128,2048]{1,0:T(8,128)(2,1)S(1)} %get-tuple-element.46), channel_id=1, source_target_pairs={{0,1},{1,2},{2,3},{3,0},{4,5},{5,6},{6,7},{7,4},{8,9},{9,10},{10,1... | collective-permute-start | bytes 1572872 | tf_op jit(solution)/shard_map/ppermute | solution.py:420
  652.7 25.4 %collective-permute-start.4 = (bf16[128,2048]{1,0:T(8,128)(2,1)S(1)}, bf16[128,2048]{1,0:T(8,128)(2,1)}, u32[]{:S(2)}, u32[]{:S(2)}) collective-permute-start(bf16[128,2048]{1,0:T(8,128)(2,1)S(1)} %get-tuple-element.47), channel_id=1, source_target_pairs={{0,3},{1,0},{2,1},{3,2},{4,7},{5,4},{6,5},{7,6},{8,11},{9,8},{10,9... | collective-permute-start | bytes 1572872 | tf_op jit(solution)/shard_map/ppermute | solution.py:421
  680.8 126.4 %collective-permute-start.2 = (bf16[128,2048]{1,0:T(8,128)(2,1)}, bf16[128,2048]{1,0:T(8,128)(2,1)S(1)}, u32[]{:S(2)}, u32[]{:S(2)}) collective-permute-start(bf16[128,2048]{1,0:T(8,128)(2,1)} %get-tuple-element.44), channel_id=1, source_target_pairs={{0,1},{1,2},{2,3},{3,0},{4,5},{5,6},{6,7},{7,4},{8,9},{9,10},{10,1... | collective-permute-start | bytes 1572872 | tf_op jit(solution)/shard_map/ppermute | solution.py:420
  681.5 125.7 %collective-permute-start.5 = (bf16[128,2048]{1,0:T(8,128)(2,1)}, bf16[128,2048]{1,0:T(8,128)(2,1)S(1)}, u32[]{:S(2)}, u32[]{:S(2)}) collective-permute-start(bf16[128,2048]{1,0:T(8,128)(2,1)} %get-tuple-element.45), channel_id=1, source_target_pairs={{0,3},{1,0},{2,1},{3,2},{4,7},{5,4},{6,5},{7,6},{8,11},{9,8},{10,9... | collective-permute-start | bytes 1572872 | tf_op jit(solution)/shard_map/ppermute | solution.py:421
  765.3 43.5 %copy-start.10 = (f32[256,2048]{1,0:T(8,128)S(1)}, f32[256,2048]{1,0:T(8,128)}, u32[]{:S(2)}) copy-start(f32[256,2048]{1,0:T(8,128)} %get-tuple-element.26.refs_1_) | copy-start | bytes 6291460
  815.2 33.5 %copy-start.12 = (f32[256,2048]{1,0:T(8,128)S(1)}, f32[256,2048]{1,0:T(8,128)}, u32[]{:S(2)}) copy-start(f32[256,2048]{1,0:T(8,128)} %get-tuple-element.72) | copy-start | bytes 6291460
Sparse Core Ops, SparseCore 0:
  10.5 35.0 all-gather.5
  47.4 28.2 all-gather.7
  77.6 54.3 all-gather.9
  133.8 54.4 all-gather.11
  190.0 55.9 all-gather.13
  531.1 39.7 reduce-scatter.7
  574.7 46.2 reduce-scatter.5
  624.4 71.2 reduce-scatter.9
  699.6 71.2 reduce-scatter.11
  774.2 71.7 reduce-scatter.13

commit v2 on v1

--- a/solution.py
+++ b/solution.py
@@ -141,15 +141,40 @@
 
 
 AXIS="tensor"
+DP="dp"
 MESH=pl.DeviceIdType.MESH
 
-def greet(here, count):
+def greet(here, count, plane=0):
     barrier=pltpu.get_barrier_semaphore()
-    @pl.when(here>0)
-    def _(): pl.semaphore_signal(barrier,inc=1,device_id={AXIS:here-1},device_id_type=MESH)
-    @pl.when(here<count-1)
-    def _(): pl.semaphore_signal(barrier,inc=1,device_id={AXIS:here+1},device_id_type=MESH)
-    pl.semaphore_wait(barrier,jnp.where((here>0)&(here<count-1),2,1))
+    if plane:
+        def call(k,_):
+            pl.semaphore_signal(barrier,inc=1,device_id={DP:lax.rem(lax.axis_index(DP)+k,plane)},device_id_type=MESH)
+            return 0
+        lax.fori_loop(1,plane,call,0)
+        for k in range(1,count):
+            pl.semaphore_signal(barrier,inc=1,device_id={AXIS:lax.rem(here+k,count)},device_id_type=MESH)
+        pl.semaphore_wait(barrier,plane+count-2)
+    else:
+        @pl.when(here>0)
+        def _(): pl.semaphore_signal(barrier,inc=1,device_id={AXIS:here-1},device_id_type=MESH)
+        @pl.when(here<count-1)
+        def _(): pl.semaphore_signal(barrier,inc=1,device_id={AXIS:here+1},device_id_type=MESH)
+        pl.semaphore_wait(barrier,jnp.where((here>0)&(here<count-1),2,1))
+
+def swap(axis, count, source, landing, sends, recvs):
+    me=lax.axis_index(axis)
+    def copy(peer, slot, k):
+        return pltpu.make_async_remote_copy(src_ref=source(peer),dst_ref=landing.at[slot],send_sem=sends.at[k],
+            recv_sem=recvs.at[slot],device_id={axis:peer},device_id_type=MESH)
+    def begin(k,_):
+        copy(lax.rem(me+k,count),me,k).start()
+        return 0
+    def end(k,_):
+        peer=lax.rem(me+k,count)
+        copy(peer,peer,k).wait_recv()
+        copy(peer,me,k).wait_send()
+        return 0
+    return (lambda: lax.fori_loop(1,count,begin,0)),(lambda: lax.fori_loop(1,count,end,0))
 
 def remote(src,dst,send,recv,target):
     return pltpu.make_async_remote_copy(src_ref=src,dst_ref=dst,send_sem=send,recv_sem=recv,
@@ -242,17 +267,33 @@
             return 0
         lax.fori_loop(0,self.pieces,one,0)
 
-def turn_over(finish, count, pieces, n_in, n_out, gather, *refs):
-    part=refs[0]; ins=refs[1:1+n_in]; outs=refs[1+n_in:1+n_in+n_out]
-    rest=refs[1+n_in+n_out:]
-    if gather:
-        whole,sums,total,ss,sr,held,hs,hr,ws=rest
-    else:
-        sums,total,ss,sr=rest; held=hs=hr=None
+def turn_over(finish, count, plane, pieces, n_in, n_out, gather, share, *refs):
+    part,other=refs[:2]; ins=refs[2:2+n_in]; outs=refs[2+n_in:2+n_in+n_out]
+    rest=list(refs[2+n_in+n_out:])
+    acc_out=rest.pop(0)
+    whole=rest.pop(0) if gather else None
+    sums,total,ss,sr,acc=rest[:5]; rest=rest[5:]
+    held=hs=hr=None
+    if gather: held,hs,hr,ws=rest[:4]; rest=rest[4:]
+    if share: cut,landed,level,stacked,ds,dr,zs,zr=rest
     rows=part.shape[1]
     line=Line(count,pieces,rows,part,sums,(ss,sr),held,(hs,hr))
-    greet(line.here,count)
+    greet(line.here,count,plane if share else 0)
     far=count-1
+    acc[...]=jnp.zeros_like(acc)
+    width=part.shape[2]
+    def terms(t):
+        def some(k,_):
+            span=pl.ds(pl.multiple_of(k*16,16),16)
+            both=part[t,span].astype(F32)*other[t,span].astype(F32)
+            acc[...]+=both[:8]+both[8:]
+            return 0
+        lax.fori_loop(0,rows//16,some,0)
+    if share:
+        me=lax.axis_index(DP)
+        piece=width//plane
+        begin_dp,end_dp=swap(DP,plane,lambda p: cut.at[p],landed,ds,dr)
+        begin_z,end_z=swap(AXIS,count,lambda p: level,stacked,zs,zr)
     def step(t,_):
         line.send_sums(t)
         if gather: line.pass_pieces(t-far)
@@ -264,29 +305,58 @@
             if gather:
                 held[line.here,line.span(u)]=low
                 line.send_own(u)
+        @pl.when(t<count)
+        def _(): terms(jnp.clip(t,0,count-1))
+        if share:
+            @pl.when(t==count-1)
+            def _():
+                for p in range(plane):
+                    cut[p,0:8,:]=acc[:,p*piece:(p+1)*piece]
+                    cut[p,8:16,:]=ins[-1][:,p*piece:(p+1)*piece]
+                landed[me]=cut[me]
+                begin_dp()
+            @pl.when(t==count)
+            def _():
+                end_dp()
+                level[...]=jnp.sum(landed[...],0)
+                stacked[line.here]=level[...]
+                begin_z()
         return 0
-    lax.fori_loop(0,pieces+(2*far if gather else far),step,0)
+    steps=pieces+(2*far if gather else far)
+    lax.fori_loop(0,steps,step,0)
     if gather:
         copy=pltpu.make_async_copy(held,whole,ws); copy.start()
+    if share:
+        end_z()
+        acc_out[...]=jnp.sum(stacked[...],0)
+    else:
+        acc_out[...]=acc[...]
     line.end_sums()
     if gather:
         line.end_pieces()
         copy.wait()
 
-def sum_and_finish(part,ins,out_shapes,finish,gather,cid,pieces,tensor):
+def sum_and_finish(part,other,ins,out_shapes,finish,gather,share,cid,pieces,tensor,plane):
     n=tensor; rows=part.shape[0]//n; D=part.shape[1]
+    assert pieces>=2
     vm=pl.BlockSpec(memory_space=pltpu.VMEM)
     outs=list(out_shapes); out_specs=[vm]*len(outs)
-    scratch=[pltpu.VMEM((2,n,rows,D),BF),pltpu.VMEM((rows//pieces,D),F32),
-        pltpu.SemaphoreType.DMA((2,n,pieces)),pltpu.SemaphoreType.DMA((2,n,pieces))]
+    sds=jax.ShapeDtypeStruct
+    outs.append(sds((16,D//plane) if share else (8,D),F32)); out_specs.append(vm)
+    sem=pltpu.SemaphoreType.DMA
+    scratch=[pltpu.VMEM((2,n,rows,D),BF),pltpu.VMEM((rows//pieces,D),F32),sem((2,n,pieces)),sem((2,n,pieces)),pltpu.VMEM((8,D),F32)]
     if gather:
-        outs.append(jax.ShapeDtypeStruct((n,rows,D),BF)); out_specs.append(pl.BlockSpec(memory_space=pl.ANY))
-        scratch+=[pltpu.VMEM((n,rows,D),BF),pltpu.SemaphoreType.DMA((2,n,pieces)),pltpu.SemaphoreType.DMA((2,n,pieces)),pltpu.SemaphoreType.DMA]
-    res=pl.pallas_call(functools.partial(turn_over,finish,n,pieces,len(ins),len(out_shapes),gather),
-        out_shape=tuple(outs),in_specs=[vm]*(1+len(ins)),out_specs=tuple(out_specs),scratch_shapes=scratch,
+        outs.append(sds((n,rows,D),BF)); out_specs.append(pl.BlockSpec(memory_space=pl.ANY))
+        scratch+=[pltpu.VMEM((n,rows,D),BF),sem((2,n,pieces)),sem((2,n,pieces)),sem]
+    if share:
+        w=D//plane
+        scratch+=[pltpu.VMEM((plane,16,w),F32),pltpu.VMEM((plane,16,w),F32),pltpu.VMEM((16,w),F32),pltpu.VMEM((n,16,w),F32),
+            sem((plane,)),sem((plane,)),sem((n,)),sem((n,))]
+    res=pl.pallas_call(functools.partial(turn_over,finish,n,plane,pieces,len(ins),len(out_shapes),gather,share),
+        out_shape=tuple(outs),in_specs=[vm]*(2+len(ins)),out_specs=tuple(out_specs),scratch_shapes=scratch,
         cost_estimate=pl.CostEstimate(flops=0,bytes_accessed=270_000_000,transcendentals=0),
         compiler_params=pltpu.CompilerParams(collective_id=cid,has_side_effects=True,vmem_limit_bytes=56*1024*1024),
-    )(part.reshape(n,rows,D),*ins)
+    )(part.reshape(n,rows,D),other.reshape(n,rows,D),*ins)
     return res
 
 
@@ -306,9 +376,17 @@
     )
 
 
-def norm_kernel(count, pieces, tokens_ref, gain_ref, whole, held, hs, hr, ws):
+def norm_kernel(count, plane, pieces, tokens_ref, gains_ref, whole, gains_out, held, landed, hs, hr, ws, ds, dr):
     line = Line(count, pieces, tokens_ref.shape[0], held=held, held_sems=(hs, hr))
-    greet(line.here, count)
+    greet(line.here, count, plane)
+    me = lax.axis_index(DP)
+    landed[me] = gains_ref[...]
+    begin, end = swap(DP, plane, lambda p: gains_ref, landed, ds, dr)
+    begin()
+    end()
+    piece = gains_ref.shape[1]
+    for p in range(plane):
+        gains_out[:, p * piece : (p + 1) * piece] = landed[p]
 
     def step(t, _):
         line.pass_pieces(t)
@@ -318,7 +396,7 @@
         def _():
             stream = tokens_ref[line.span(u), :].astype(F32)
             scale = lax.rsqrt(jnp.mean(stream * stream, -1, keepdims=True) + EPSILON)
-            held[line.here, line.span(u)] = (stream * scale * gain_ref[...]).astype(BF)
+            held[line.here, line.span(u)] = (stream * scale * gains_out[0:1, :]).astype(BF)
             line.send_own(u)
 
         return 0
@@ -330,25 +408,30 @@
     copy.wait()
 
 
-def norm_and_gather(tokens, gain, cid, pieces, count):
+def norm_and_gather(tokens, gains, cid, pieces, count, plane):
     rows, width = tokens.shape
     vm = pl.BlockSpec(memory_space=pltpu.VMEM)
-    return pl.pallas_call(
-        functools.partial(norm_kernel, count, pieces),
-        out_shape=jax.ShapeDtypeStruct((count, rows, width), BF),
+    sem = pltpu.SemaphoreType.DMA
+    normed, gains = pl.pallas_call(
+        functools.partial(norm_kernel, count, plane, pieces),
+        out_shape=(jax.ShapeDtypeStruct((count, rows, width), BF), jax.ShapeDtypeStruct((8, width), F32)),
         in_specs=[vm, vm],
-        out_specs=pl.BlockSpec(memory_space=pl.ANY),
+        out_specs=(pl.BlockSpec(memory_space=pl.ANY), vm),
         scratch_shapes=[
             pltpu.VMEM((count, rows, width), BF),
-            pltpu.SemaphoreType.DMA((2, count, pieces)),
-            pltpu.SemaphoreType.DMA((2, count, pieces)),
-            pltpu.SemaphoreType.DMA,
+            pltpu.VMEM((plane, 8, width // plane), F32),
+            sem((2, count, pieces)),
+            sem((2, count, pieces)),
+            sem,
+            sem((plane,)),
+            sem((plane,)),
         ],
         cost_estimate=pl.CostEstimate(flops=0, bytes_accessed=270_000_000, transcendentals=0),
         compiler_params=pltpu.CompilerParams(
             collective_id=cid, has_side_effects=True, vmem_limit_bytes=40 * 1024 * 1024
         ),
-    )(tokens, gain).reshape(count * rows, width)
+    )(tokens, gains)
+    return normed.reshape(count * rows, width), gains
 
 
 def finish_attention(span, total, ins, outs):
@@ -360,12 +443,11 @@
 
 
 def finish_residual(span, total, ins, outs):
-    residual_ref, grad_out, gain, start = ins
+    residual_ref, grad_out, gain = ins
     residual = residual_ref[span, :]
     scale = lax.rsqrt(jnp.mean(residual * residual, -1, keepdims=True) + EPSILON)
     unit = residual * scale
     grads = total[...]
-    outs[1][span, :] = grads * unit
     scaled = grads * gain[...]
     grad_residual = grad_out[span, :].astype(F32) + scale * (
         scaled - unit * jnp.mean(scaled * unit, -1, keepdims=True)
@@ -375,60 +457,29 @@
 
 
 def finish_tokens(span, total, ins, outs):
-    tokens, grad_residual, gain = ins
+    tokens, grad_residual, gain, _ = ins
     stream = tokens[span, :].astype(F32)
     scale = lax.rsqrt(jnp.mean(stream * stream, -1, keepdims=True) + EPSILON)
     unit = stream * scale
     grads = total[...]
-    outs[1][span, :] = grads * unit
     scaled = grads * gain[...]
     outs[0][span, :] = grad_residual[span, :] + scale * (
         scaled - unit * jnp.mean(scaled * unit, -1, keepdims=True)
     )
 
 
-def ring_gather(piece, count):
-    rows, width = piece.shape
-    half = rows // 2
-    here = lax.axis_index(AXIS)
-    right = [(k, (k + 1) % count) for k in range(count)]
-    left = [(k, (k - 1) % count) for k in range(count)]
-    one, two = piece[:half], piece[half:]
-    whole = jnp.zeros((count, rows, width), piece.dtype)
-    whole = lax.dynamic_update_slice(whole, piece[None], (here, 0, 0))
-    for step in range(1, count):
-        one = lax.ppermute(one, AXIS, right)
-        two = lax.ppermute(two, AXIS, left)
-        whole = lax.dynamic_update_slice(whole, one[None], ((here - step) % count, 0, 0))
-        whole = lax.dynamic_update_slice(whole, two[None], ((here + step) % count, half, 0))
-    return whole.reshape(count * rows, width)
-
-
-def ring_sum(part, count):
-    width = part.shape[1]
-    half = part.shape[0] // count // 2
-    here = lax.axis_index(AXIS)
-    right = [(k, (k + 1) % count) for k in range(count)]
-    left = [(k, (k - 1) % count) for k in range(count)]
-    cut = part.reshape(count, 2, half, width)
-
-    def term(owner, side):
-        return lax.dynamic_slice(cut, (owner % count, side, 0, 0), (1, 1, half, width))[0, 0]
-
-    one, two = term(here - 1, 0), term(here + 1, 1)
-    for step in range(1, count):
-        one = lax.ppermute(one, AXIS, right)
-        two = lax.ppermute(two, AXIS, left)
-        last = step == count - 1
-        one = one.astype(F32) + term(here - step - 1, 0).astype(F32)
-        two = two.astype(F32) + term(here + step + 1, 1).astype(F32)
-        if not last:
-            one, two = one.astype(BF), two.astype(BF)
-    return jnp.concatenate([one, two], 0)
+def ways(count):
+    return [(k, (k + 1) % count) for k in range(count)], [(k, (k - 1) % count) for k in range(count)]
+
+
+def both_ways(one, two, count):
+    right, left = ways(count)
+    return lax.ppermute(one, AXIS, right), lax.ppermute(two, AXIS, left)
 
 
 def body(
     count,
+    plane,
     tokens,
     segments,
     positions,
@@ -444,73 +495,119 @@
     grad_out,
 ):
     rows, width = tokens.shape
+    half = rows // 2
+    here = lax.axis_index(AXIS)
     heads = w_query.shape[1] // HD
     groups = w_key.shape[1] // HD
-    gains = lax.all_gather(jnp.stack([attn_gain, mlp_gain]).astype(F32), "dp", axis=1, tiled=True)
+    after = lax.optimization_barrier
+    mix = lax.all_gather(jnp.concatenate([w_query, w_key, w_value], 1), DP, axis=0, tiled=True)
+    full_out = lax.all_gather(w_out, DP, axis=1, tiled=True)
+    full_gate = lax.all_gather(w_gate, DP, axis=0, tiled=True)
+    full_up = lax.all_gather(w_up, DP, axis=0, tiled=True)
+    full_down = lax.all_gather(w_down, DP, axis=1, tiled=True)
+    gains = jnp.concatenate([jnp.stack([attn_gain, mlp_gain]).astype(F32), jnp.zeros((6, attn_gain.shape[0]), F32)])
+
+    normed_one, gains = norm_and_gather(tokens, gains, 1, 4, count, plane)
     gain_one, gain_two = gains[0:1], gains[1:2]
-    mix = lax.all_gather(jnp.concatenate([w_query, w_key, w_value], 1), "dp", axis=0, tiled=True)
-    full_out = lax.all_gather(w_out, "dp", axis=1, tiled=True)
-    full_gate = lax.all_gather(w_gate, "dp", axis=0, tiled=True)
-    full_up = lax.all_gather(w_up, "dp", axis=0, tiled=True)
-    full_down = lax.all_gather(w_down, "dp", axis=1, tiled=True)
-
-    normed_one = norm_and_gather(tokens, gain_one, 1, 4, count)
     angles = frequencies(HD)[:, None] * positions.astype(F32)[None, :]
     cosine, sine = jnp.cos(angles), jnp.sin(angles)
+
+    grad_rows = jnp.zeros((count, rows, width), BF)
+    grad_rows = lax.dynamic_update_slice(grad_rows, grad_out[None], (here, 0, 0))
+
+    def place(whole, one, two, step):
+        whole = lax.dynamic_update_slice(whole, one[None], ((here - step) % count, 0, 0))
+        return lax.dynamic_update_slice(whole, two[None], ((here + step) % count, half, 0))
+
+    one, two, normed_one = after((grad_out[:half], grad_out[half:], normed_one))
+    one, two = both_ways(one, two, count)
     lin = dot(mix, normed_one, 0, 1)
     mixed, lse, q, kt, k, vt, v = attend(lin, cosine, sine, segments, heads, groups)
-    grad_late, normed_late = lax.optimization_barrier((grad_out, normed_one))
-    grad_rows = ring_gather(grad_late, count)
-
+    one, two, mixed = after((one, two, mixed))
     part = dot(mixed, full_out, 0, 0).astype(BF)
-    residual, normed_two = sum_and_finish(
-        part, (tokens, gain_two), (jax.ShapeDtypeStruct((rows, width), F32),),
-        finish_attention, True, 2, 16, count,
+    residual, _, normed_two = sum_and_finish(
+        part, part, (tokens, gain_two), (jax.ShapeDtypeStruct((rows, width), F32),),
+        finish_attention, True, False, 2, 16, count, plane,
     )
     normed_two = normed_two.reshape(count * rows, width)
-    gate_values = dot(normed_two, full_gate, 1, 0)
-    up_values = dot(normed_two, full_up, 1, 0)
+    for step in range(1, count - 1):
+        grad_rows = place(grad_rows, one, two, step)
+        one, two, normed_two = after((one, two, normed_two))
+        one, two = both_ways(one, two, count)
+        if step == 1:
+            gate_values = dot(normed_two, full_gate, 1, 0)
+            up_values = dot(normed_two, full_up, 1, 0)
+            one, two, gate_values, up_values = after((one, two, gate_values, up_values))
     sigmoid_gate = jax.nn.sigmoid(gate_values)
     activated = gate_values * sigmoid_gate
     product = (activated * up_values).astype(BF)
-    down = ring_sum(dot(product, full_down, 1, 0).astype(BF), count)
-    block_out = (residual + down).astype(BF)
+    down = dot(product, full_down, 1, 0).astype(BF)
+    one, two, down = after((one, two, down))
+    grad_rows = place(grad_rows, one, two, count - 1).reshape(count * rows, width)
+
+    cut = down.reshape(count, 2, half, width)
+
+    def term(owner, side):
+        return lax.dynamic_slice(cut, (owner % count, side, 0, 0), (1, 1, half, width))[0, 0].astype(F32)
+
+    def add_terms(one, two, step):
+        return one.astype(F32) + term(here - step - 1, 0), two.astype(F32) + term(here + step + 1, 1)
+
+    one, two = both_ways(term(here - 1, 0).astype(BF), term(here + 1, 1).astype(BF), count)
     grad_product = dot(grad_rows, full_down, 1, 1)
     grad_gated = (
         grad_product * up_values * sigmoid_gate * (1.0 + gate_values * (1.0 - sigmoid_gate))
     ).astype(BF)
     grad_lifted = (grad_product * activated).astype(BF)
+    one, two, grad_gated, grad_lifted = after((one, two, grad_gated, grad_lifted))
+    one, two = add_terms(one, two, 1)
+    one, two = both_ways(one.astype(BF), two.astype(BF), count)
+    grad_down = dot(product, grad_rows, 0, 0).astype(BF)
+    grad_down, grad_gated, grad_lifted = after((grad_down, grad_gated, grad_lifted))
+    grad_down = lax.psum_scatter(grad_down, DP, scatter_dimension=1, tiled=True)
+    grad_gate = dot(normed_two, grad_gated, 0, 0).astype(BF)
+    grad_up = dot(normed_two, grad_lifted, 0, 0).astype(BF)
+    grad_gate, grad_up, grad_gated, grad_lifted = after((grad_gate, grad_up, grad_gated, grad_lifted))
+    grad_gate = lax.psum_scatter(grad_gate, DP, scatter_dimension=0, tiled=True)
+    grad_up = lax.psum_scatter(grad_up, DP, scatter_dimension=0, tiled=True)
     part = (dot(grad_gated, full_gate, 1, 1) + dot(grad_lifted, full_up, 1, 1)).astype(BF)
-    grad_down = lax.psum_scatter(dot(product, grad_rows, 0, 0).astype(BF), "dp", scatter_dimension=1, tiled=True)
-    grad_gate = lax.psum_scatter(dot(normed_two, grad_gated, 0, 0).astype(BF), "dp", scatter_dimension=0, tiled=True)
-    grad_up = lax.psum_scatter(dot(normed_two, grad_lifted, 0, 0).astype(BF), "dp", scatter_dimension=0, tiled=True)
+    one, two, part = after((one, two, part))
+    one, two = add_terms(one, two, 2)
     wide = jax.ShapeDtypeStruct((rows, width), F32)
     grad_residual, terms_two, grad_low = sum_and_finish(
-        part, (residual, grad_out, gain_two, gain_two), (wide, wide), finish_residual, True, 3, 16, count
-    )
+        part, normed_two, (residual, grad_out, gain_two), (wide,), finish_residual, True, False, 3, 16, count, plane
+    )
+    for step in range(3, count - 1):
+        one, two = both_ways(one.astype(BF), two.astype(BF), count)
+        one, two = add_terms(one, two, step)
     grad_low = grad_low.reshape(count * rows, width)
+    one, two, grad_low, grad_down, grad_gate = after((one.astype(BF), two.astype(BF), grad_low, grad_down, grad_gate))
+    one, two = both_ways(one, two, count)
     grad_mixed = dot(full_out, grad_low, 1, 1).astype(BF)
-    grad_out_proj = lax.psum_scatter(dot(mixed, grad_low, 1, 0).astype(BF), "dp", scatter_dimension=1, tiled=True)
+    grad_out_proj = lax.psum_scatter(dot(mixed, grad_low, 1, 0).astype(BF), DP, scatter_dimension=1, tiled=True)
     turned = attend_back(q, kt, k, v, lse, grad_mixed, cosine, sine, segments, heads, groups)
+    grad_mix = dot(normed_one, turned, 0, 1).astype(BF)
+    one, two, turned, grad_mix = after((one, two, turned, grad_mix))
+    grad_mix = lax.psum_scatter(grad_mix, DP, scatter_dimension=0, tiled=True)
+    one, two = add_terms(one, two, count - 1)
+    block_out = (residual + jnp.concatenate([one, two], 0)).astype(BF)
     part = dot(turned, mix, 0, 1).astype(BF)
-    grad_mix = lax.psum_scatter(dot(normed_one, turned, 0, 1).astype(BF), "dp", scatter_dimension=0, tiled=True)
-    grad_tokens, terms_one = sum_and_finish(
-        part, (tokens, grad_residual, gain_one), (wide, wide), finish_tokens, False, 4, 4, count
-    )
-    sums = lax.psum(jnp.stack([jnp.sum(terms_one, 0), jnp.sum(terms_two, 0)]), ("dp", AXIS))
-    place = lax.axis_index("dp") * attn_gain.shape[0]
-    sums = lax.dynamic_slice(sums, (0, place), (2, attn_gain.shape[0]))
+    part, grad_up = after((part, grad_up))
+    grad_tokens, sums = sum_and_finish(
+        part, normed_one, (tokens, grad_residual, gain_one, terms_two), (wide,), finish_tokens, False, True, 4, 4, count, plane
+    )
+    sums = jnp.sum(sums.reshape(2, 8, -1), 1)
     edges = (heads * HD, (heads + groups) * HD)
     grad_query, grad_key, grad_value = jnp.split(grad_mix.astype(F32), edges, 1)
     return (
         block_out,
         grad_tokens,
-        sums[0],
+        sums[0] / attn_gain.astype(F32),
         grad_query,
         grad_key,
         grad_value,
         grad_out_proj.astype(F32),
-        sums[1],
+        sums[1] / mlp_gain.astype(F32),
         grad_gate.astype(F32),
         grad_up.astype(F32),
         grad_down.astype(F32),
@@ -534,7 +631,7 @@
         P(("dp", "tensor"), None),
     )
     return jax.shard_map(
-        functools.partial(body, mesh.shape["tensor"]),
+        functools.partial(body, mesh.shape["tensor"], mesh.shape["dp"]),
         mesh=mesh,
         in_specs=placed,
         out_specs=(

time: 866 us -> 718 us (0.83)
  waiting for transfers between devices: 119 us -> 3.28 us
  blocking collectives: 47.9 us -> 0 us
  Pallas kernels: 438 us -> 457 us
    ppermute x12, waiting for transfers between devices: 91.8 us -> 0.03 us  [both_ways(): return (lax.ppermute(one, AXIS, right), lax.ppermute(two, AXIS, left))]
    psum x1 -> x0, blocking collectives: 37.6 us -> none  [body(): lax.psum(jnp.stack([jnp.sum(terms_one, 0), jnp.sum(terms_two, 0)]), ('dp'...]
    reduce_scatter x5, waiting for transfers between devices: 25 us -> 0.01 us  [the longest x1 0.01 us: body(): grad_down = lax.psum_scatter(grad_down, DP, scatter_dimension=1, tiled=True)]
    pallas_call x4, Pallas kernels: 389 us -> 407 us  [the longest x3 325 us: sum_and_finish(): pl.pallas_call(functools.partial(turn_over, finish, n, plane, pieces, len...]
    all_gather x1 -> x0, blocking collectives: 10.4 us -> none  [body(): lax.all_gather(jnp.stack([attn_gain, mlp_gain]).astype(F32), 'dp', axis=1...]
  transfers between devices with their start and end apart: 22 -> 22, of which waited for: 11 -> 0; matrix products, arithmetic and copies ran while one was open for 17% -> 29% of each run, Pallas kernels for 37% -> 64%
where the time goes in v2:
time: 718 us; the launch traced here: 710 us
  Pallas kernels  457 us (64%)
  matrix products  168 us (23%)
  local copies, waits for them, and re-layouts  23.1 us (3%)
  other arithmetic  22.8 us (3%)
  starting transfers between devices  21 us (3%)
  between operations  15.1 us (2%)
    pallas_call x3, Pallas kernels, sum_and_finish(): pl.pallas_call(functools.partial(turn_over, finish, n, plane, pieces, len...  325 us
    dot_general x15, matrix products, dot(): lax.dot_general(left_side, right_side, (((left_dim,), (right_dim,)), ((),...  168 us
    pallas_call x1, Pallas kernels, norm_and_gather(): pl.pallas_call(functools.partial(norm_kernel, count, plane, pieces), out_...  82.5 us
    pallas_call x1, Pallas kernels, attend_back(): pl.pallas_call(functools.partial(attend_back_kernel, heads, groups, block...  28.9 us
    pallas_call x1, Pallas kernels, attend(): pl.pallas_call(functools.partial(attend_kernel, heads, groups, block), ou...  20.8 us
    ppermute x12, starting transfers between devices, both_ways(): return (lax.ppermute(one, AXIS, right), lax.ppermute(two, AXIS, left))  20.5 us
  transfers between devices with their start and end apart: 22, of which 0 were waited for; matrix products, arithmetic and copies ran while one was open for 29% of the time, Pallas kernels for 64%

profile of v2, /device:TPU:0, one launch (start us, length us, event | category | flops | bytes accessed | tf_op | source)
XLA Modules:
  0.0 710.2 jit_solution(10427472702609947921)
XLA Ops:
  7.3 1.9 pad_maximum_fusion
  12.0 82.5 %shard_map.212 = (bf16[4,256,2048]{2,1,0:T(8,128)(2,1)S(1)}, f32[8,2048]{1,0:T(8,128)S(1)}) custom-call(bf16[256,2048]{1,0:T(8,128)(2,1)S(1)} %copy-done, f32[8,256]{1,0:T(8,128)S(1)} %fusion.10.gains_ref), custom_call_target="tpu_custom_call" | custom-call | bytes 270000000 | tf_op jit(solution)/shard_map/pallas_call | solution.py:415
  94.5 2.1 copy-done.1
  96.6 1.0 fusion.11
  97.6 3.8 collective-permute-start.1
  102.9 2.5 broadcast_in_dim.27
  105.3 1.1 bitcast_dynamic-update-slice_fusion
  106.4 8.3 %fusion.15.lin_ref = f32[768,1024]{1,0:T(8,128)} fusion(bf16[2048,768]{1,0:T(8,128)(2,1)} %all-gather.6.cloned.1.call-done, bf16[1024,2048]{1,0:T(8,128)(2,1)} %bitcast.84), kind=kOutput, calls=%fused_computation.54 | convolution fusion | flops 3221225472 | bytes 10485760 | tf_op jit(solution)/shard_map/dot_general | solution.py:374
  114.8 20.8 %shard_map.213 = (bf16[512,1024]{1,0:T(8,128)(2,1)S(1)}, f32[8,1,1024]{2,1,0:T(1,128)S(1)}, bf16[512,1024]{1,0:T(8,128)(2,1)S(1)}, bf16[128,1024]{1,0:T(8,128)(2...) custom-call(f32[768,1024]{1,0:T(8,128)} %fusion.15.lin_ref, ...), custom_call_target="tpu_custom_call" | custom-call | flops 30000001024 | bytes 10000000 | tf_op jit(solution)/shard_map/pallas_call | solution.py:73
  136.6 6.5 convolution_convert_fusion.4
  143.1 121.0 %shard_map.214 = (f32[256,2048]{1,0:T(8,128)}, f32[8,2048]{1,0:T(8,128)}, bf16[4,256,2048]{2,1,0:T(8,128)(2,1)}) custom-call(bf16[4,256,2048]{2,1,0:T(8,128)(2,1)} %bitcast.89, bf16[4,256,2048]{2,1,0:T(8,128)(2,1)} %bitcast.90, bf16[256,2048]{1,0:T(8,128)(2,1)} %refs_2_.3, f32[1,2048]{1,0:T(1,128)} %get-tuple-element.144.refs_3_.refs_4_), custom_call_target="tpu_custom_call" | custom-call | bytes 270000000 | tf_op jit(solution)/shard_map/pallas_call | solution.py:355
  264.2 3.8 collective-permute-start.3
  268.0 1.9 bitcast_dynamic-update-slice_fusion.6
  269.9 1.9 bitcast_dynamic-update-slice_fusion.5
  271.8 14.5 %fusion.17 = f32[1024,2048]{1,0:T(8,128)} fusion(bf16[1024,2048]{1,0:T(8,128)(2,1)} %bitcast.95, bf16[2048,2048]{1,0:T(8,128)(2,1)} %all-gather.12.cloned.1.call-done), kind=kOutput, calls=%fused_computation.56 | convolution fusion | flops 8589934592 | bytes 20971520 | tf_op jit(solution)/shard_map/dot_general | solution.py:374
  286.3 12.6 %fusion.16 = f32[1024,2048]{1,0:T(8,128)S(1)} fusion(bf16[1024,2048]{1,0:T(8,128)(2,1)} %bitcast.96, bf16[2048,2048]{1,0:T(8,128)(2,1)} %all-gather.10.cloned.1.call-done), kind=kOutput, calls=%fused_computation.55 | convolution fusion | flops 8589934592 | bytes 20971520 | tf_op jit(solution)/shard_map/dot_general | solution.py:374
  299.0 3.8 collective-permute-start.5
  302.9 3.9 multiply_convert_fusion.2
  306.8 12.5 %convolution_convert_fusion.3 = bf16[1024,2048]{1,0:T(8,128)(2,1)S(1)} fusion(bf16[1024,2048]{1,0:T(8,128)(2,1)} %multiply_convert_fusion.2, bf16[2048,2048]{1,0:T(8,128)(2,1)} %all-gather.14.cloned.1.call-done), kind=kOutput, calls=%fused_computation.9 | convolution fusion | flops 8592031744 | bytes 16777216 | tf_op jit(solution)/shard_map/dot_general | solution.py:374
  320.2 1.3 bitcast_dynamic-update-slice_fusion.3
  322.7 2.3 collective-permute-start.6
  325.8 1.9 bitcast_dynamic-update-slice_fusion.1
  327.7 20.5 %multiply_convert_fusion = (bf16[1024,2048]{1,0:T(8,128)(2,1)}, bf16[1024,2048]{1,0:T(8,128)(2,1)}) fusion(f32[1024,2048]{1,0:T(8,128)} %copy-done.13, f32[1024,2048]{1,0:T(8,128)} %fusion.17, bf16[1024,2048]{1,0:T(8,128)(2,1)} %bitcast.15, bf16[2048,2048]{1,0:T(8,128)(2,1)} %all-gather.14.cloned.1.call-done), kind=kOutput, calls=%fused_computation.1 | convolution fusion | flops 8617197568 | bytes 37748736 | tf_op jit(solution)/shard_map/dot_general | solution.py:374
  348.2 14.0 %convolution_convert_fusion.2 = bf16[2048,2048]{1,0:T(8,128)(2,1)} fusion(bf16[1024,2048]{1,0:T(8,128)(2,1)} %multiply_convert_fusion.2, bf16[1024,2048]{1,0:T(8,128)(2,1)} %bitcast.15), kind=kOutput, calls=%fused_computation.8 | convolution fusion | flops 8594128896 | bytes 16777216 | tf_op jit(solution)/shard_map/dot_general | solution.py:374
  362.5 14.3 %convolution_convert_fusion.1 = bf16[2048,2048]{1,0:T(8,128)(2,1)} fusion(bf16[1024,2048]{1,0:T(8,128)(2,1)} %bitcast.97, bf16[1024,2048]{1,0:T(8,128)(2,1)} %get-tuple-element.100), kind=kOutput, calls=%fused_computation.7 | convolution fusion | flops 8594128896 | bytes 16777216 | tf_op jit(solution)/shard_map/dot_general | solution.py:374
  376.7 14.7 %convolution_convert_fusion = bf16[2048,2048]{1,0:T(8,128)(2,1)} fusion(bf16[1024,2048]{1,0:T(8,128)(2,1)} %bitcast.98, bf16[1024,2048]{1,0:T(8,128)(2,1)} %get-tuple-element.101), kind=kOutput, calls=%fused_computation.6 | convolution fusion | flops 8594128896 | bytes 16777216 | tf_op jit(solution)/shard_map/dot_general | solution.py:374
  392.3 1.6 fusion.5
  393.9 2.5 collective-permute-start.9
  396.5 15.0 %fusion.18 = f32[1024,2048]{1,0:T(8,128)} fusion(bf16[1024,2048]{1,0:T(8,128)(2,1)} %get-tuple-element.100, bf16[2048,2048]{1,0:T(8,128)(2,1)} %all-gather.10.cloned.1.call-done), kind=kOutput, calls=%fused_computation.57 | convolution fusion | flops 8589934592 | bytes 20971520 | tf_op jit(solution)/shard_map/dot_general | solution.py:374
  411.6 13.4 %add_convert_fusion = bf16[1024,2048]{1,0:T(8,128)(2,1)} fusion(f32[1024,2048]{1,0:T(8,128)} %fusion.18, bf16[1024,2048]{1,0:T(8,128)(2,1)} %get-tuple-element.101, bf16[2048,2048]{1,0:T(8,128)(2,1)S(1)} %bitcast.104), kind=kOutput, calls=%fused_computation | convolution fusion | flops 8594128896 | bytes 25165824 | tf_op jit(solution)/shard_map/dot_general | solution.py:374
  425.0 121.3 %shard_map.215 = (f32[256,2048]{1,0:T(8,128)}, f32[8,2048]{1,0:T(8,128)}, bf16[4,256,2048]{2,1,0:T(8,128)(2,1)}) custom-call(bf16[4,256,2048]{2,1,0:T(8,128)(2,1)} %bitcast.99, bf16[4,256,2048]{2,1,0:T(8,128)(2,1)} %get-tuple-element.80, f32[256,2048]{1,0:T(8,128)} %get-tuple-element.77.refs_2_, bf16[256,2048]{1,0:T(8,128)(2,1)} %refs_3_.1, ...), custom_call_target="tpu_custom_call" | custom-call | bytes 270000000 | tf_op jit(solution)/shard_map/pallas_call | solution.py:355
  546.3 2.6 fusion.3
  548.9 3.8 collective-permute-start.11
  552.7 6.0 convolution_convert_fusion.7
  558.9 5.3 fusion.2.gm_ref
  564.3 28.9 %shard_map.216 = bf16[768,1024]{1,0:T(8,128)(2,1)S(1)} custom-call(bf16[512,1024]{1,0:T(8,128)(2,1)S(1)} %copy-done.7, bf16[128,1024]{1,0:T(8,128)(2,1)S(1)} %get-tuple-element.111.kt_ref, bf16[2,1024,64]{2,1,0:T(8,128)(2,1)S(1)} %get-tuple-element.112.k_ref, bf16[2,1024,64]{2,1,0:T(8,128)(2,1)S(1)} %copy-done.9, ...), custom_call_target="tpu_custom_call" | custom-call | flops 60000002048 | bytes 10000000 | tf_op jit(solution)/shard_map/pallas_call | solution.py:133
  593.2 5.0 convolution_convert_fusion.6
  598.2 3.0 convert_element_type.181
  601.2 1.5 convert_element_type.183
  602.7 5.1 convolution_convert_fusion.5
  607.8 82.5 %shard_map.217 = (f32[256,2048]{1,0:T(8,128)}, f32[16,256]{1,0:T(8,128)}) custom-call(bf16[4,256,2048]{2,1,0:T(8,128)(2,1)} %bitcast.100, bf16[4,256,2048]{2,1,0:T(8,128)(2,1)} %copy-done.1, bf16[256,2048]{1,0:T(8,128)(2,1)} %refs_2_.3, f32[256,2048]{1,0:T(8,128)} %get-tuple-element.121.refs_3_, f32[1,2048]{1,0:T(1,128)} %get-tuple-element.143.refs_4_, ...), custom_call_target="tpu_custom_call" | custom-call | bytes 270000000 | tf_op jit(solution)/shard_map/pallas_call | solution.py:355
  690.4 1.6 convert_element_type.182
  693.3 1.9 convert_add_fusion.1
  695.2 1.2 fusion.1
  696.4 1.8 convert_element_type.179
  698.2 1.6 fusion.12
  699.8 1.8 split.12
  701.6 1.3 copy.37
  (114 shorter events, 10.9 us)
Async XLA Ops:
  7.2 4.8 copy-start.21
  7.2 4.8 copy-start.19
  7.2 4.8 copy-start
  7.2 89.3 %copy-start.10 = (bf16[256,2048]{1,0:T(8,128)(2,1)S(1)}, bf16[256,2048]{1,0:T(8,128)(2,1)}, u32[]{:S(2)}) copy-start(bf16[256,2048]{1,0:T(8,128)(2,1)} %refs_3_.1) | copy-start | bytes 3145732
  7.2 94.2 %copy-start.18 = (s32[1024]{0:T(1024)S(1)}, s32[1024]{0:T(1024)}, u32[]{:S(2)}) copy-start(s32[1024]{0:T(1024)} %param.15) | copy-start | bytes 12292
  7.2 94.2 %copy-start.3 = (s32[1024]{0:T(1024)S(1)}, s32[1024]{0:T(1024)}, u32[]{:S(2)}) copy-start(s32[1024]{0:T(1024)} %param.14) | copy-start | bytes 12292
  7.2 99.2 %all-gather.6.cloned.1.call-start = ((), (), s32[]{:S(2)}) async-start(), calls=%async_computation.5 | async-start | bytes 3538944 | tf_op jit(solution)/shard_map/all_gather | solution.py:503
  9.2 127.3 %all-gather.8.cloned.1.call-start = ((), (), s32[]{:S(2)}) async-start(), calls=%async_computation.6 | async-start | bytes 2359296 | tf_op jit(solution)/shard_map/all_gather | solution.py:504
  10.0 261.8 %all-gather.12.cloned.1.call-start = ((), (), s32[]{:S(2)}) async-start(), calls=%async_computation.8 | async-start | bytes 9437184 | tf_op jit(solution)/shard_map/all_gather | solution.py:506
  10.7 275.6 %all-gather.10.cloned.1.call-start = ((), (), s32[]{:S(2)}) async-start(), calls=%async_computation.7 | async-start | bytes 9437184 | tf_op jit(solution)/shard_map/all_gather | solution.py:505
  11.3 295.4 %all-gather.14.cloned.1.call-start = ((), (), s32[]{:S(2)}) async-start(), calls=%async_computation.9 | async-start | bytes 9437184 | tf_op jit(solution)/shard_map/all_gather | solution.py:507
  11.9 537.0 %reduce-scatter.6.cloned.1.call-start = ((), (), s32[]{:S(2)}) async-start(), calls=%async_computation.10 | async-start | bytes 9437184 | tf_op jit(solution)/shard_map/reduce_scatter | solution.py:567
  94.5 2.1 copy-start.1
  97.6 38.9 %collective-permute-start = (bf16[128,2048]{1,0:T(8,128)(2,1)}, bf16[128,2048]{1,0:T(8,128)(2,1)}, u32[]{:S(2)}, u32[]{:S(2)}) collective-permute-start(bf16[128,2048]{1,0:T(8,128)(2,1)} %get-tuple-element.71), channel_id=1, source_target_pairs={{0,1},{1,2},{2,3},{3,0},{4,5},{5,6},{6,7},{7,4},{8,9},{9,10},{10,1... | collective-permute-start | bytes 1572872 | tf_op jit(solution)/shard_map/ppermute | solution.py:477
  97.6 38.9 %collective-permute-start.1 = (bf16[128,2048]{1,0:T(8,128)(2,1)}, bf16[128,2048]{1,0:T(8,128)(2,1)}, u32[]{:S(2)}, u32[]{:S(2)}) collective-permute-start(bf16[128,2048]{1,0:T(8,128)(2,1)} %get-tuple-element.72), channel_id=1, source_target_pairs={{0,3},{1,0},{2,1},{3,2},{4,7},{5,4},{6,5},{7,6},{8,11},{9,8},{10,9... | collective-permute-start | bytes 1572872 | tf_op jit(solution)/shard_map/ppermute | solution.py:477
  135.5 1.0 copy-start.6
  136.5 6.6 copy-start.4
  136.5 6.6 copy-start.8
  264.1 34.9 %collective-permute-start.2 = (bf16[128,2048]{1,0:T(8,128)(2,1)}, bf16[128,2048]{1,0:T(8,128)(2,1)S(1)}, u32[]{:S(2)}, u32[]{:S(2)}) collective-permute-start(bf16[128,2048]{1,0:T(8,128)(2,1)} %collective-permute-done), channel_id=1, source_target_pairs={{0,1},{1,2},{2,3},{3,0},{4,5},{5,6},{6,7},{7,4},{8,9},{9,10},{10,1... | collective-permute-start | bytes 1572872 | tf_op jit(solution)/shard_map/ppermute | solution.py:477
  264.2 34.8 %collective-permute-start.3 = (bf16[128,2048]{1,0:T(8,128)(2,1)}, bf16[128,2048]{1,0:T(8,128)(2,1)S(1)}, u32[]{:S(2)}, u32[]{:S(2)}) collective-permute-start(bf16[128,2048]{1,0:T(8,128)(2,1)} %collective-permute-done.1), channel_id=1, source_target_pairs={{0,3},{1,0},{2,1},{3,2},{4,7},{5,4},{6,5},{7,6},{8,11},{9,8},{10,9... | collective-permute-start | bytes 1572872 | tf_op jit(solution)/shard_map/ppermute | solution.py:477
  286.3 16.5 %copy-start.12 = (f32[1024,2048]{1,0:T(8,128)S(1)}, f32[1024,2048]{1,0:T(8,128)}, u32[]{:S(2)}) copy-start(f32[1024,2048]{1,0:T(8,128)} %fusion.17) | copy-start | bytes 25165828
  298.9 3.9 copy-start.13
  299.0 22.5 %collective-permute-start.4 = (bf16[128,2048]{1,0:T(8,128)(2,1)S(1)}, bf16[128,2048]{1,0:T(8,128)(2,1)S(1)}, u32[]{:S(2)}, u32[]{:S(2)}) collective-permute-start(bf16[128,2048]{1,0:T(8,128)(2,1)S(1)} %collective-permute-done.2), channel_id=1, source_target_pairs={{0,1},{1,2},{2,3},{3,0},{4,5},{5,6},{6,7},{7,4},{8,9},{9,10},{10,1... | collective-permute-start | bytes 1572872 | tf_op jit(solution)/shard_map/ppermute | solution.py:477
  299.0 22.4 %collective-permute-start.5 = (bf16[128,2048]{1,0:T(8,128)(2,1)S(1)}, bf16[128,2048]{1,0:T(8,128)(2,1)}, u32[]{:S(2)}, u32[]{:S(2)}) collective-permute-start(bf16[128,2048]{1,0:T(8,128)(2,1)S(1)} %collective-permute-done.3), channel_id=1, source_target_pairs={{0,3},{1,0},{2,1},{3,2},{4,7},{5,4},{6,5},{7,6},{8,11},{9,8},{10,9... | collective-permute-start | bytes 1572872 | tf_op jit(solution)/shard_map/ppermute | solution.py:477
  319.2 2.3 copy-start.14
  322.5 39.7 %collective-permute-start.7 = (bf16[128,2048]{1,0:T(8,128)(2,1)}, bf16[128,2048]{1,0:T(8,128)(2,1)S(1)}, u32[]{:S(2)}, u32[]{:S(2)}) collective-permute-start(bf16[128,2048]{1,0:T(8,128)(2,1)} %get-tuple-element.137), channel_id=1, source_target_pairs={{0,3},{1,0},{2,1},{3,2},{4,7},{5,4},{6,5},{7,6},{8,11},{9,8},{10,9... | collective-permute-start | bytes 1572872 | tf_op jit(solution)/shard_map/ppermute | solution.py:477
  322.7 39.5 %collective-permute-start.6 = (bf16[128,2048]{1,0:T(8,128)(2,1)}, bf16[128,2048]{1,0:T(8,128)(2,1)S(1)}, u32[]{:S(2)}, u32[]{:S(2)}) collective-permute-start(bf16[128,2048]{1,0:T(8,128)(2,1)} %get-tuple-element.138), channel_id=1, source_target_pairs={{0,1},{1,2},{2,3},{3,0},{4,5},{5,6},{6,7},{7,4},{8,9},{9,10},{10,1... | collective-permute-start | bytes 1572872 | tf_op jit(solution)/shard_map/ppermute | solution.py:477
  362.2 186.7 %reduce-scatter.8.cloned.1.call-start = ((), (), s32[]{:S(2)}) async-start(), calls=%async_computation.11 | async-start | bytes 9437184 | tf_op jit(solution)/shard_map/reduce_scatter | solution.py:571
  391.5 216.3 %reduce-scatter.10.cloned.1.call-start = ((), (), s32[]{:S(2)}) async-start(), calls=%async_computation.12 | async-start | bytes 9437184 | tf_op jit(solution)/shard_map/reduce_scatter | solution.py:572
  392.2 304.2 %reduce-scatter.14.cloned.1.call-start = ((), (), s32[]{:S(2)}) async-start(), calls=%async_computation.14 | async-start | bytes 2359296 | tf_op jit(solution)/shard_map/reduce_scatter | solution.py:587
  393.9 31.1 %collective-permute-start.9 = (bf16[128,2048]{1,0:T(8,128)(2,1)S(1)}, bf16[128,2048]{1,0:T(8,128)(2,1)S(1)}, u32[]{:S(2)}, u32[]{:S(2)}) collective-permute-start(bf16[128,2048]{1,0:T(8,128)(2,1)S(1)} %get-tuple-element.135), channel_id=1, source_target_pairs={{0,3},{1,0},{2,1},{3,2},{4,7},{5,4},{6,5},{7,6},{8,11},{9,8},{10,9... | collective-permute-start | bytes 1572872 | tf_op jit(solution)/shard_map/ppermute | solution.py:477
  396.3 15.2 %slice-start = ((s8[8388608]{0:T(1024)(128)(4,1)}), s8[4194304]{0:T(1024)(128)(4,1)S(1)}, s32[]{:S(2)}) async-start(s8[8388608]{0:T(1024)(128)(4,1)} %bitcast.103), calls=%async_computation.15 | async-start | bytes 8388608
  396.3 15.2 %slice-start.1 = ((s8[8388608]{0:T(1024)(128)(4,1)}), s8[4194304]{0:T(1024)(128)(4,1)S(1)}, s32[]{:S(2)}) async-start(s8[8388608]{0:T(1024)(128)(4,1)} %bitcast.103), calls=%async_computation.16 | async-start | bytes 8388608
  396.3 28.7 %collective-permute-start.8 = (bf16[128,2048]{1,0:T(8,128)(2,1)S(1)}, bf16[128,2048]{1,0:T(8,128)(2,1)S(1)}, u32[]{:S(2)}, u32[]{:S(2)}) collective-permute-start(bf16[128,2048]{1,0:T(8,128)(2,1)S(1)} %get-tuple-element.136), channel_id=1, source_target_pairs={{0,1},{1,2},{2,3},{3,0},{4,5},{5,6},{6,7},{7,4},{8,9},{9,10},{10,1... | collective-permute-start | bytes 1572872 | tf_op jit(solution)/shard_map/ppermute | solution.py:477
  425.0 127.8 %copy-start.5 = (bf16[512,1024]{1,0:T(8,128)(2,1)S(1)}, bf16[512,1024]{1,0:T(8,128)(2,1)}, u32[]{:S(2)}) copy-start(bf16[512,1024]{1,0:T(8,128)(2,1)} %copy-done.4) | copy-start | bytes 3145732
  548.9 49.2 %collective-permute-start.10 = (bf16[128,2048]{1,0:T(8,128)(2,1)}, bf16[128,2048]{1,0:T(8,128)(2,1)}, u32[]{:S(2)}, u32[]{:S(2)}) collective-permute-start(bf16[128,2048]{1,0:T(8,128)(2,1)} %get-tuple-element.108), channel_id=1, source_target_pairs={{0,1},{1,2},{2,3},{3,0},{4,5},{5,6},{6,7},{7,4},{8,9},{9,10},{10,1... | collective-permute-start | bytes 1572872 | tf_op jit(solution)/shard_map/ppermute | solution.py:477
  548.9 49.2 %collective-permute-start.11 = (bf16[128,2048]{1,0:T(8,128)(2,1)}, bf16[128,2048]{1,0:T(8,128)(2,1)}, u32[]{:S(2)}, u32[]{:S(2)}) collective-permute-start(bf16[128,2048]{1,0:T(8,128)(2,1)} %get-tuple-element.109), channel_id=1, source_target_pairs={{0,3},{1,0},{2,1},{3,2},{4,7},{5,4},{6,5},{7,6},{8,11},{9,8},{10,9... | collective-permute-start | bytes 1572872 | tf_op jit(solution)/shard_map/ppermute | solution.py:477
  558.8 139.4 %reduce-scatter.12.cloned.1.call-start = ((), (), s32[]{:S(2)}) async-start(), calls=%async_computation.13 | async-start | bytes 3538944 | tf_op jit(solution)/shard_map/reduce_scatter | solution.py:591
  558.8 5.4 copy-start.7
  558.9 5.4 copy-start.9
  564.2 29.0 %copy-start.2 = (bf16[4,256,2048]{2,1,0:T(8,128)(2,1)S(1)}, bf16[4,256,2048]{2,1,0:T(8,128)(2,1)}, u32[]{:S(2)}) copy-start(bf16[4,256,2048]{2,1,0:T(8,128)(2,1)} %copy-done.1) | copy-start | bytes 12582916
  598.2 3.1 copy-start.16
  598.2 4.5 copy-start.23
  607.8 82.6 %copy-start.17 = (bf16[256,2048]{1,0:T(8,128)(2,1)S(1)}, bf16[256,2048]{1,0:T(8,128)(2,1)}, u32[]{:S(2)}) copy-start(bf16[256,2048]{1,0:T(8,128)(2,1)} %reduce-scatter.10.cloned.1.call-done) | copy-start | bytes 3145732
  607.8 84.9 %copy-start.20 = (bf16[256]{0:T(256)(128)(2,1)S(1)}, bf16[256]{0:T(256)(128)(2,1)}, u32[]{:S(2)}) copy-start(bf16[256]{0:T(256)(128)(2,1)} %param.21) | copy-start | bytes 1540
  607.8 84.9 %copy-start.22 = (bf16[256]{0:T(256)(128)(2,1)S(1)}, bf16[256]{0:T(256)(128)(2,1)}, u32[]{:S(2)}) copy-start(bf16[256]{0:T(256)(128)(2,1)} %param.16) | copy-start | bytes 1540
  690.3 4.8 copy-start.11
  695.1 6.4 copy-start.15
Sparse Core Ops, SparseCore 0:
  10.5 35.0 all-gather.5
  47.5 28.1 all-gather.7
  77.6 54.4 all-gather.11
  133.8 54.3 all-gather.9
  189.9 55.9 all-gather.13
  362.4 72.0 reduce-scatter.5
  438.3 71.3 reduce-scatter.7
  513.1 71.2 reduce-scatter.9
  588.6 41.2 reduce-scatter.13
  633.1 46.6 reduce-scatter.11

commit v3 on v2

--- a/solution.py
+++ b/solution.py
@@ -26,17 +26,29 @@
     allowed=(key_places<=query_places)&(segs_col[0:keys,:]==segs_row[0:1,start:start+block])
     return jnp.where(allowed,0.0,MASKED).astype(F32)
 
-def attend_kernel(heads, groups, block, lin_ref, cos_ref, sin_ref, segc_ref, segr_ref,
-                  mixed_ref, lse_ref, q_ref, kt_ref, k_ref, vt_ref, v_ref, bias_ref):
-    length=lin_ref.shape[1]
+def attend_kernel(heads, groups, block, count, pieces, mix_ref, normed_ref, cos_ref, sin_ref, segc_ref, segr_ref, wo_ref, grad_ref,
+                  mixed_ref, lse_ref, q_ref, kt_ref, k_ref, vt_ref, v_ref, part_ref, rows_hbm,
+                  lin_ref, bias_ref, held, hs, hr, cs):
+    length=normed_ref.shape[0]
     per=heads//groups
+    rows=grad_ref.shape[0]
+    line=Line(count,pieces,rows,held=held,held_sems=(hs,hr),sub=rows//(2*pieces))
+    greet(line.here,count)
+    for u in range(pieces):
+        line.send_own(u,grad_ref.at[line.span(u),:])
+    lines=mix_ref.shape[0]
+    cut=256 if lines%256==0 else lines
+    def project(c,_):
+        some=pl.ds(pl.multiple_of(c*cut,cut),cut)
+        lin_ref[some,:]=lax.dot_general(mix_ref[some,:],normed_ref[...],(((1,),(1,)),((),())),preferred_element_type=F32)
+        return 0
+    lax.fori_loop(0,lines//cut,project,0)
     cosine, sine = cos_ref[...], sin_ref[...]
     def rope(h,_):
         rows=pl.ds(pl.multiple_of(h*HD,HD),HD)
         q_ref[rows,:]=(turn_t(lin_ref[rows,:],cosine,sine,1.0).astype(BF)*jnp.asarray(0.125,BF))
         return 0
     lax.fori_loop(0,heads,rope,0)
-    kv=groups*HD
     turned=[turn_t(lin_ref[(heads+g)*HD:(heads+g+1)*HD,:],cosine,sine,1.0) for g in range(groups)]
     keys_t=jnp.concatenate(turned,0)
     kt_ref[...]=keys_t.astype(BF)
@@ -47,8 +59,13 @@
     for g in range(groups):
         k_ref[g]=keys_n[:,g*HD:(g+1)*HD]
         v_ref[g]=vals_n[:,g*HD:(g+1)*HD]
+    done=0
+    steps=pieces+count-1
     for start in range(0,length,block):
         keys=start+block
+        if done<steps-2:
+            done+=1
+            line.pass_pieces(done)
         bias_ref[0:keys,:]=block_bias(segc_ref,segr_ref,start,block)
         def head(h,_):
             g=h//per
@@ -64,20 +81,39 @@
             lse_ref[h,:,start:start+block]=top+jnp.log(total)
             return 0
         lax.fori_loop(0,heads,head,0)
-
-def attend(lin, cosine, sine, segments, heads, groups):
-    length=lin.shape[1]
+    width=wo_ref.shape[1]
+    wide=min(512,width)
+    def out(c,_):
+        cols=pl.ds(pl.multiple_of(c*wide,wide),wide)
+        part_ref[:,cols]=lax.dot_general(mixed_ref[...],wo_ref[:,cols],(((0,),(0,)),((),())),preferred_element_type=F32).astype(BF)
+        return 0
+    lax.fori_loop(0,width//wide,out,0)
+    for t in range(done+1,steps):
+        line.pass_pieces(t)
+    half=rows//2
+    held[line.here,0:half]=grad_ref[0:half,:]
+    copy=pltpu.make_async_copy(held,rows_hbm,cs)
+    copy.start()
+    line.end_pieces()
+    copy.wait()
+
+def attend(mix, normed, cosine, sine, segments, w_out, grad_out, heads, groups, cid, pieces, count):
+    length,width=normed.shape
+    rows=grad_out.shape[0]
     block=min(256,length)
     sds=jax.ShapeDtypeStruct
     vm=pl.BlockSpec(memory_space=pltpu.VMEM)
-    return pl.pallas_call(functools.partial(attend_kernel,heads,groups,block),
+    sem=pltpu.SemaphoreType.DMA
+    return pl.pallas_call(functools.partial(attend_kernel,heads,groups,block,count,pieces),
         out_shape=(sds((heads*HD,length),BF),sds((heads,1,length),F32),sds((heads*HD,length),BF),
-            sds((groups*HD,length),BF),sds((groups,length,HD),BF),sds((groups*HD,length),BF),sds((groups,length,HD),BF)),
-        in_specs=[vm]*5,out_specs=(vm,)*7,
-        scratch_shapes=[pltpu.VMEM((length,block),F32)],
-        cost_estimate=pl.CostEstimate(flops=30_000_000_000,bytes_accessed=10_000_000,transcendentals=8_000_000),
-        compiler_params=pltpu.CompilerParams(vmem_limit_bytes=48*1024*1024),
-    )(lin,cosine,sine,segments.reshape(length,1),segments.reshape(1,length))
+            sds((groups*HD,length),BF),sds((groups,length,HD),BF),sds((groups*HD,length),BF),sds((groups,length,HD),BF),
+            sds((length,width),BF),sds((count,rows//2,width),BF)),
+        in_specs=[vm]*8,out_specs=(vm,)*8+(pl.BlockSpec(memory_space=pl.ANY),),
+        scratch_shapes=[pltpu.VMEM((mix.shape[0],length),F32),pltpu.VMEM((length,block),F32),pltpu.VMEM((count,rows//2,width),BF),
+            sem((2,count,pieces)),sem((2,count,pieces)),sem],
+        cost_estimate=pl.CostEstimate(flops=30_000_000_000,bytes_accessed=130_000_000,transcendentals=8_000_000),
+        compiler_params=pltpu.CompilerParams(collective_id=cid,has_side_effects=True,vmem_limit_bytes=56*1024*1024),
+    )(mix,normed,cosine,sine,segments.reshape(length,1),segments.reshape(1,length),w_out,grad_out)
 
 def attend_back_kernel(heads, groups, block, q_ref, kt_ref, k_ref, v_ref, lse_ref, gm_ref, cos_ref, sin_ref, segc_ref, segr_ref,
                   out_ref, bias_ref, qn_ref, gn_ref, dq_ref, dk_ref, dv_ref):
@@ -181,21 +217,52 @@
         device_id={AXIS:target},device_id_type=MESH)
 
 class Line:
-    def __init__(self,count,pieces,rows,part=None,sums=None,sum_sems=None,held=None,held_sems=None):
+    def __init__(self,count,pieces,rows,part=None,sums=None,sum_sems=None,held=None,held_sems=None,base=0,sub=None):
         self.n,self.pieces,self.rows=count,pieces,rows
-        self.sub=rows//pieces
+        self.sub=rows//pieces if sub is None else sub
+        self.base=base
         self.here=lax.axis_index(AXIS)
         self.part,self.sums,self.sum_sems=part,sums,sum_sems
         self.held,self.held_sems=held,held_sems
-    def span(self,u): return pl.ds(pl.multiple_of(u*self.sub,self.sub),self.sub)
+    def span(self,u): return pl.ds(pl.multiple_of(self.base+u*self.sub,self.sub),self.sub)
     def fits(self,u): return (u>=0)&(u<self.pieces)
     def _target(self,way):
         return lax.min(self.here+1,self.n-1) if way==0 else lax.max(self.here-1,0)
+    def slot(self,way,j,device):
+        return j if way==0 else jnp.where(j==device,self.n,j)
     def sum_copy(self,way,j,u,first):
         sends,recvs=self.sum_sems
-        dst=self.sums.at[way,j,self.span(u)]
-        src=self.part.at[j,self.span(u)] if first else dst
+        dst=self.sums.at[self.slot(way,j,self._target(way)),self.span(u)]
+        src=self.part.at[j,self.span(u)] if first else self.sums.at[self.slot(way,j,self.here),self.span(u)]
         return remote(src,dst,sends.at[way,j,u],recvs.at[way,j,u],self._target(way))
+    def sum_arrival(self,way,j,u):
+        sends,recvs=self.sum_sems
+        ref=self.sums.at[self.slot(way,j,self.here),self.span(u)]
+        return remote(ref,ref,sends.at[way,j,u],recvs.at[way,j,u],self._target(way))
+    def relay(self,way,j,u,begins,passes):
+        @pl.when(begins)
+        def _(): self.sum_copy(way,j,u,True).start()
+        @pl.when(passes)
+        def _():
+            self.sum_arrival(way,j,u).wait_recv()
+            ref=self.sums.at[j,self.span(u)]
+            ref[...]=(ref[...].astype(F32)+self.part[j,self.span(u)].astype(F32)).astype(BF)
+            self.sum_copy(way,j,u,False).start()
+    def far_steps(self): return (self.n-1)*self.pieces+1
+    def far_step(self,t,total,finish):
+        here,n,S=self.here,self.n,self.pieces
+        for way in (0,1):
+            q=t-here if way==0 else t-(n-1-here)
+            ok=(q>=0)&(q<S*(n-1-here if way==0 else here))
+            q=jnp.clip(q,0,S*(n-1)-1)
+            j=n-1-q//S if way==0 else q//S
+            end=(here==0) if way==0 else (here==n-1)
+            self.relay(way,j,q%S,ok&end,ok&jnp.logical_not(end))
+        u=t-(n-2)*S-1
+        @pl.when(self.fits(u))
+        def _():
+            self.own_sum(u,total)
+            finish(self.span(u),total)
     def send_sums(self,t):
         here,n=self.here,self.n
         for k in range(n-1):
@@ -205,23 +272,15 @@
                 u=jnp.clip(u,0,self.pieces-1)
                 begins=(here==0) if way==0 else (here==n-1)
                 passes=((here>0)&(here<j)) if way==0 else ((here<n-1)&(here>j))
-                @pl.when(ok&begins)
-                def _(): self.sum_copy(way,j,u,True).start()
-                @pl.when(ok&passes)
-                def _():
-                    copy=self.sum_copy(way,j,u,False)
-                    copy.wait_recv()
-                    ref=self.sums.at[way,j,self.span(u)]
-                    ref[...]=(ref[...].astype(F32)+self.part[j,self.span(u)].astype(F32)).astype(BF)
-                    copy.start()
+                self.relay(way,j,u,ok&begins,ok&passes)
     def own_sum(self,u,total):
         here,n=self.here,self.n
         total[...]=self.part[here,self.span(u)].astype(F32)
         for way in (0,1):
             @pl.when(here>0 if way==0 else here<n-1)
             def _():
-                self.sum_copy(way,here,u,False).wait_recv()
-                total[...]+=self.sums[way,here,self.span(u)].astype(F32)
+                self.sum_arrival(way,here,u).wait_recv()
+                total[...]+=self.sums[self.slot(way,here,here),self.span(u)].astype(F32)
     def end_sums(self):
         here,n=self.here,self.n
         def one(u,_):
@@ -240,7 +299,7 @@
         for way in (0,1):
             @pl.when(here<n-1 if way==0 else here>0)
             def _(): self.piece_copy(way,here,u,src).start()
-    def pass_pieces(self,t):
+    def pass_pieces(self,t,use=None):
         here,n=self.here,self.n
         for k in range(1,n):
             u=t-k
@@ -254,6 +313,9 @@
                 def _(): self.piece_copy(way,c,u).wait_recv()
                 @pl.when(there&(here<n-1 if way==0 else here>0))
                 def _(): self.piece_copy(way,c,u).start()
+                if use is not None:
+                    @pl.when(there)
+                    def _(): use(c,u)
     def end_pieces(self):
         here,n=self.here,self.n
         def one(u,_):
@@ -295,16 +357,17 @@
         begin_dp,end_dp=swap(DP,plane,lambda p: cut.at[p],landed,ds,dr)
         begin_z,end_z=swap(AXIS,count,lambda p: level,stacked,zs,zr)
     def step(t,_):
-        line.send_sums(t)
-        if gather: line.pass_pieces(t-far)
-        u=t-far
-        @pl.when(line.fits(u))
-        def _():
-            line.own_sum(u,total)
-            low=finish(line.span(u),total,ins,outs)
-            if gather:
-                held[line.here,line.span(u)]=low
+        if gather:
+            line.send_sums(t)
+            line.pass_pieces(t-far)
+            u=t-far
+            @pl.when(line.fits(u))
+            def _():
+                line.own_sum(u,total)
+                held[line.here,line.span(u)]=finish(line.span(u),total,ins,outs)
                 line.send_own(u)
+        else:
+            line.far_step(t,total,lambda span,total: finish(span,total,ins,outs))
         @pl.when(t<count)
         def _(): terms(jnp.clip(t,0,count-1))
         if share:
@@ -322,7 +385,7 @@
                 stacked[line.here]=level[...]
                 begin_z()
         return 0
-    steps=pieces+(2*far if gather else far)
+    steps=pieces+2*far if gather else line.far_steps()
     lax.fori_loop(0,steps,step,0)
     if gather:
         copy=pltpu.make_async_copy(held,whole,ws); copy.start()
@@ -344,7 +407,7 @@
     sds=jax.ShapeDtypeStruct
     outs.append(sds((16,D//plane) if share else (8,D),F32)); out_specs.append(vm)
     sem=pltpu.SemaphoreType.DMA
-    scratch=[pltpu.VMEM((2,n,rows,D),BF),pltpu.VMEM((rows//pieces,D),F32),sem((2,n,pieces)),sem((2,n,pieces)),pltpu.VMEM((8,D),F32)]
+    scratch=[pltpu.VMEM((n+1,rows,D),BF),pltpu.VMEM((rows//pieces,D),F32),sem((2,n,pieces)),sem((2,n,pieces)),pltpu.VMEM((8,D),F32)]
     if gather:
         outs.append(sds((n,rows,D),BF)); out_specs.append(pl.BlockSpec(memory_space=pl.ANY))
         scratch+=[pltpu.VMEM((n,rows,D),BF),sem((2,n,pieces)),sem((2,n,pieces)),sem]
@@ -360,6 +423,178 @@
     return res
 
 
+def mlp_kernel(count,pieces,tile,x_ref,grad_ref,res_ref,early_hbm,wg_hbm,wu_hbm,wd_hbm,
+        part_ref,wide_ref,out_ref,gr,product,gated,lifted,down,ring,tall,sums,total,hs,hr,ss,sr,ws,ts,ls):
+    s=pl.program_id(0)
+    length,hidden=product.shape
+    width=x_ref.shape[1]
+    rows=grad_ref.shape[0]
+    half=rows//2
+    first,second=hidden//tile,width//tile
+    slots=ring.shape[0]
+    at_down=first; at_grad=first+second; at_part=2*first+second; at_weight=2*first+2*second
+    spread=pieces//2
+    get=Line(count,spread,rows,held=gr,held_sems=(hs,hr),base=half,sub=half//spread)
+    line=Line(count,pieces,rows,down,sums,(ss,sr))
+    def strip(k,size): return pl.ds(pl.multiple_of(jnp.clip(k,0,size-1)*tile,tile),tile)
+    def tall_load(k):
+        slot=lax.rem(k,slots)
+        @pl.when((k<2*first)&(lax.rem(k,2)==0))
+        def _(): pltpu.make_async_copy(wg_hbm.at[:,strip(k//2,first)],tall.at[slot],ts.at[slot]).start()
+        @pl.when((k<2*first)&(lax.rem(k,2)==1))
+        def _(): pltpu.make_async_copy(wu_hbm.at[:,strip(k//2,first)],tall.at[slot],ts.at[slot]).start()
+        @pl.when((k>=2*first)&(k<2*first+second))
+        def _(): pltpu.make_async_copy(wd_hbm.at[:,strip(k-2*first,second)],tall.at[slot],ts.at[slot]).start()
+    def tall_loaded(k):
+        slot=lax.rem(k,slots)
+        pltpu.make_async_copy(wg_hbm.at[:,pl.ds(0,tile)],tall.at[slot],ts.at[slot]).wait()
+        return slot
+    def load(k):
+        slot=lax.rem(k,slots)
+        late=strip((k-first)//2,second)
+        @pl.when(k<first)
+        def _(): pltpu.make_async_copy(wd_hbm.at[strip(k,first),:],ring.at[slot],ws.at[slot]).start()
+        @pl.when((k>=first)&(lax.rem(k-first,2)==0)&(k<first+2*second))
+        def _(): pltpu.make_async_copy(wg_hbm.at[late,:],ring.at[slot],ws.at[slot]).start()
+        @pl.when((k>=first)&(lax.rem(k-first,2)==1)&(k<first+2*second))
+        def _(): pltpu.make_async_copy(wu_hbm.at[late,:],ring.at[slot],ws.at[slot]).start()
+    def loaded(k):
+        slot=lax.rem(k,slots)
+        pltpu.make_async_copy(wd_hbm.at[pl.ds(0,tile),:],ring.at[slot],ws.at[slot]).wait()
+        return slot
+    def own(): return pltpu.make_async_copy(grad_ref,gr.at[get.here],ls.at[0])
+    def early(c): return pltpu.make_async_copy(early_hbm.at[c],gr.at[c,pl.ds(0,half)],ls.at[1+c])
+    @pl.when(s==0)
+    def _():
+        for k in range(slots): tall_load(k)
+        greet(get.here,count)
+        for u in range(spread):
+            get.send_own(u,grad_ref.at[get.span(u),:])
+        own().start()
+        for c in range(count):
+            @pl.when(c!=get.here)
+            def _(): early(c).start()
+    @pl.when(s==at_down-1)
+    def _():
+        for k in range(slots): load(k)
+    hops=spread+count-2
+    gap=max(1,at_grad//hops)
+    @pl.when((s>0)&(lax.rem(s,gap)==0)&(s<=gap*hops))
+    def _(): get.pass_pieces(s//gap)
+    @pl.when(s==at_grad)
+    def _():
+        own().wait()
+        for c in range(count):
+            @pl.when(c!=get.here)
+            def _(): early(c).wait()
+    def finish(span,total):
+        out_ref[span,:]=(res_ref[span,:]+total[...]).astype(BF)
+    r=s-at_grad
+    if first==4 and second==4 and line.far_steps()==13:
+        ok=(r>=0)&(r!=2)&((r<8)|(lax.rem(r,4)==0))
+        t=jnp.where(r<2,r,jnp.where(r<8,r-1,5+r//4))
+    else:
+        ok=(r>=0)&(r<line.far_steps())
+        t=r
+    @pl.when(ok)
+    def _(): line.far_step(t,total,finish)
+    @pl.when(s<at_down)
+    def _():
+        one=tall_loaded(2*s)
+        two=tall_loaded(2*s+1)
+        cols=strip(s,first)
+        for c in range(count):
+            span=slice(c*rows,(c+1)*rows)
+            gate=jnp.dot(x_ref[span,:],tall[one],preferred_element_type=F32)
+            up=jnp.dot(x_ref[span,:],tall[two],preferred_element_type=F32)
+            sigmoid=1.0/(1.0+jnp.exp(-gate))
+            active=gate*sigmoid
+            product[span,cols]=(active*up).astype(BF)
+            lifted[span,cols]=active.astype(BF)
+            gated[span,cols]=(up*(sigmoid+active*(1.0-sigmoid))).astype(BF)
+        tall_load(2*s+slots)
+        tall_load(2*s+1+slots)
+    @pl.when((s>=at_down)&(s<at_grad))
+    def _():
+        k=2*first+s-at_down
+        slot=tall_loaded(k)
+        sums_here=jnp.dot(product[...],tall[slot],preferred_element_type=F32).astype(BF)
+        cols=strip(s-at_down,second)
+        for c in range(count): down[c,:,cols]=sums_here[c*rows:(c+1)*rows]
+        tall_load(k+slots)
+    @pl.when((s>=at_grad)&(s<at_part))
+    def _():
+        k=s-at_grad
+        slot=loaded(k)
+        cols=strip(k,first)
+        for c in range(count):
+            span=slice(c*rows,(c+1)*rows)
+            grads=lax.dot_general(gr[c],ring[slot],(((1,),(1,)),((),())),preferred_element_type=F32)
+            gated[span,cols]=(grads*gated[span,cols].astype(F32)).astype(BF)
+            lifted[span,cols]=(grads*lifted[span,cols].astype(F32)).astype(BF)
+        load(k+slots)
+    @pl.when((s>=at_part)&(s<at_weight))
+    def _():
+        k=first+2*(s-at_part)
+        one=loaded(k)
+        both=lax.dot_general(gated[...],ring[one],(((1,),(1,)),((),())),preferred_element_type=F32)
+        load(k+slots)
+        two=loaded(k+1)
+        both=both+lax.dot_general(lifted[...],ring[two],(((1,),(1,)),((),())),preferred_element_type=F32)
+        part_ref[...]=both.astype(BF)
+        load(k+1+slots)
+    last=s-at_weight
+    cols=strip(last//6,second)
+    kind=lax.rem(last,6)
+    cut=hidden//2
+    def weight(left,right):
+        wide_ref[...]=lax.dot_general(left,right,(((0,),(0,)),((),())),preferred_element_type=F32).astype(BF)
+    for side in (0,1):
+        these=slice(side*cut,(side+1)*cut)
+        @pl.when((last>=0)&(kind==side))
+        def _(): weight(x_ref[:,cols],gated[:,these])
+        @pl.when((last>=0)&(kind==2+side))
+        def _(): weight(x_ref[:,cols],lifted[:,these])
+        @pl.when((last>=0)&(kind==4+side))
+        def _(): weight(gr[:,:,cols].reshape(length,tile),product[:,these])
+    @pl.when(s==at_weight+6*second-1)
+    def _():
+        get.end_pieces()
+        line.end_sums()
+
+def mlp(x,grad_out,residual,early,w_gate,w_up,w_down,cid,pieces,count):
+    length,width=x.shape
+    hidden=w_gate.shape[1]
+    rows=length//count
+    tile=min(512,hidden,width)
+    first,second=hidden//tile,width//tile
+    steps=2*first+8*second
+    assert first+7*second>=(count-1)*pieces+1
+    whole=lambda shape: pl.BlockSpec(shape,lambda s: (0,)*len(shape),pipeline_mode=pl.Buffered(1))
+    hbm=pl.BlockSpec(memory_space=pl.ANY)
+    sds=jax.ShapeDtypeStruct
+    sem=pltpu.SemaphoreType.DMA
+    at_part=2*first+second
+    def wide_map(s):
+        k=jnp.maximum(s-at_part-second,0)
+        return (k//6,k%6)
+    vmem=pltpu.VMEM
+    spread=pieces//2
+    return pl.pallas_call(functools.partial(mlp_kernel,count,pieces,tile),
+        grid=(steps,),
+        out_shape=(sds((length,width),BF),sds((width,3*hidden),BF),sds((rows,width),BF)),
+        in_specs=[whole((length,width)),whole((rows,width)),whole((rows,width)),hbm,hbm,hbm,hbm],
+        out_specs=(pl.BlockSpec((length,tile),lambda s: (0,jnp.clip(s-at_part,0,second-1))),
+            pl.BlockSpec((tile,hidden//2),wide_map),whole((rows,width))),
+        scratch_shapes=[vmem((count,rows,width),BF),vmem((length,hidden),BF),vmem((length,hidden),BF),vmem((length,hidden),BF),
+            vmem((count,rows,width),BF),vmem((4,tile,width),BF),vmem((4,width,tile),BF),vmem((count+1,rows,width),BF),vmem((rows//pieces,width),F32),
+            sem((2,count,spread)),sem((2,count,spread)),sem((2,count,pieces)),sem((2,count,pieces)),sem((4,)),sem((4,)),sem((count+1,))],
+        cost_estimate=pl.CostEstimate(flops=78_000_000_000,bytes_accessed=380_000_000,transcendentals=0),
+        compiler_params=pltpu.CompilerParams(collective_id=cid,has_side_effects=True,vmem_limit_bytes=60*1024*1024,
+            dimension_semantics=("arbitrary",)),
+    )(x,grad_out,residual,early,w_gate,w_up,w_down)
+
+
 def frequencies(head_size):
     inverse = 1.0 / 500000.0 ** (jnp.arange(head_size // 2, dtype=jnp.float32) * 2.0 / head_size)
     wavelength = 2.0 * math.pi / inverse
@@ -376,36 +611,37 @@
     )
 
 
-def norm_kernel(count, plane, pieces, tokens_ref, gains_ref, whole, gains_out, held, landed, hs, hr, ws, ds, dr):
+def norm_kernel(count, plane, pieces, tokens_ref, gains_ref, normed, gains_out, held, landed, hs, hr, ds, dr):
     line = Line(count, pieces, tokens_ref.shape[0], held=held, held_sems=(hs, hr))
     greet(line.here, count, plane)
     me = lax.axis_index(DP)
+    begin, end = swap(DP, plane, lambda p: gains_ref, landed, ds, dr)
+    for u in range(pieces):
+        line.send_own(u, tokens_ref.at[line.span(u), :])
+    begin()
     landed[me] = gains_ref[...]
-    begin, end = swap(DP, plane, lambda p: gains_ref, landed, ds, dr)
-    begin()
     end()
     piece = gains_ref.shape[1]
     for p in range(plane):
         gains_out[:, p * piece : (p + 1) * piece] = landed[p]
 
+    def norm(rows, c, u):
+        stream = rows.astype(F32)
+        scale = lax.rsqrt(jnp.mean(stream * stream, -1, keepdims=True) + EPSILON)
+        normed[c, line.span(u)] = (stream * scale * gains_out[0:1, :]).astype(BF)
+
     def step(t, _):
-        line.pass_pieces(t)
-        u = jnp.clip(t, 0, pieces - 1)
+        line.pass_pieces(t, lambda c, u: norm(held[c, line.span(u)], c, u))
 
         @pl.when(t < pieces)
         def _():
-            stream = tokens_ref[line.span(u), :].astype(F32)
-            scale = lax.rsqrt(jnp.mean(stream * stream, -1, keepdims=True) + EPSILON)
-            held[line.here, line.span(u)] = (stream * scale * gains_out[0:1, :]).astype(BF)
-            line.send_own(u)
+            u = jnp.clip(t, 0, pieces - 1)
+            norm(tokens_ref[line.span(u), :], line.here, u)
 
         return 0
 
     lax.fori_loop(0, pieces + count - 1, step, 0)
-    copy = pltpu.make_async_copy(held, whole, ws)
-    copy.start()
     line.end_pieces()
-    copy.wait()
 
 
 def norm_and_gather(tokens, gains, cid, pieces, count, plane):
@@ -416,13 +652,12 @@
         functools.partial(norm_kernel, count, plane, pieces),
         out_shape=(jax.ShapeDtypeStruct((count, rows, width), BF), jax.ShapeDtypeStruct((8, width), F32)),
         in_specs=[vm, vm],
-        out_specs=(pl.BlockSpec(memory_space=pl.ANY), vm),
+        out_specs=(vm, vm),
         scratch_shapes=[
             pltpu.VMEM((count, rows, width), BF),
             pltpu.VMEM((plane, 8, width // plane), F32),
             sem((2, count, pieces)),
             sem((2, count, pieces)),
-            sem,
             sem((plane,)),
             sem((plane,)),
         ],
@@ -466,15 +701,6 @@
     outs[0][span, :] = grad_residual[span, :] + scale * (
         scaled - unit * jnp.mean(scaled * unit, -1, keepdims=True)
     )
-
-
-def ways(count):
-    return [(k, (k + 1) % count) for k in range(count)], [(k, (k - 1) % count) for k in range(count)]
-
-
-def both_ways(one, two, count):
-    right, left = ways(count)
-    return lax.ppermute(one, AXIS, right), lax.ppermute(two, AXIS, left)
 
 
 def body(
@@ -495,12 +721,10 @@
     grad_out,
 ):
     rows, width = tokens.shape
-    half = rows // 2
-    here = lax.axis_index(AXIS)
     heads = w_query.shape[1] // HD
     groups = w_key.shape[1] // HD
     after = lax.optimization_barrier
-    mix = lax.all_gather(jnp.concatenate([w_query, w_key, w_value], 1), DP, axis=0, tiled=True)
+    mix = lax.all_gather(jnp.concatenate([w_query, w_key, w_value], 1).T, DP, axis=1, tiled=True)
     full_out = lax.all_gather(w_out, DP, axis=1, tiled=True)
     full_gate = lax.all_gather(w_gate, DP, axis=0, tiled=True)
     full_up = lax.all_gather(w_up, DP, axis=0, tiled=True)
@@ -512,93 +736,35 @@
     angles = frequencies(HD)[:, None] * positions.astype(F32)[None, :]
     cosine, sine = jnp.cos(angles), jnp.sin(angles)
 
-    grad_rows = jnp.zeros((count, rows, width), BF)
-    grad_rows = lax.dynamic_update_slice(grad_rows, grad_out[None], (here, 0, 0))
-
-    def place(whole, one, two, step):
-        whole = lax.dynamic_update_slice(whole, one[None], ((here - step) % count, 0, 0))
-        return lax.dynamic_update_slice(whole, two[None], ((here + step) % count, half, 0))
-
-    one, two, normed_one = after((grad_out[:half], grad_out[half:], normed_one))
-    one, two = both_ways(one, two, count)
-    lin = dot(mix, normed_one, 0, 1)
-    mixed, lse, q, kt, k, vt, v = attend(lin, cosine, sine, segments, heads, groups)
-    one, two, mixed = after((one, two, mixed))
-    part = dot(mixed, full_out, 0, 0).astype(BF)
+    mixed, lse, q, kt, k, vt, v, part, early = attend(
+        mix, normed_one, cosine, sine, segments, full_out, grad_out, heads, groups, 6, 2, count
+    )
     residual, _, normed_two = sum_and_finish(
         part, part, (tokens, gain_two), (jax.ShapeDtypeStruct((rows, width), F32),),
         finish_attention, True, False, 2, 16, count, plane,
     )
     normed_two = normed_two.reshape(count * rows, width)
-    for step in range(1, count - 1):
-        grad_rows = place(grad_rows, one, two, step)
-        one, two, normed_two = after((one, two, normed_two))
-        one, two = both_ways(one, two, count)
-        if step == 1:
-            gate_values = dot(normed_two, full_gate, 1, 0)
-            up_values = dot(normed_two, full_up, 1, 0)
-            one, two, gate_values, up_values = after((one, two, gate_values, up_values))
-    sigmoid_gate = jax.nn.sigmoid(gate_values)
-    activated = gate_values * sigmoid_gate
-    product = (activated * up_values).astype(BF)
-    down = dot(product, full_down, 1, 0).astype(BF)
-    one, two, down = after((one, two, down))
-    grad_rows = place(grad_rows, one, two, count - 1).reshape(count * rows, width)
-
-    cut = down.reshape(count, 2, half, width)
-
-    def term(owner, side):
-        return lax.dynamic_slice(cut, (owner % count, side, 0, 0), (1, 1, half, width))[0, 0].astype(F32)
-
-    def add_terms(one, two, step):
-        return one.astype(F32) + term(here - step - 1, 0), two.astype(F32) + term(here + step + 1, 1)
-
-    one, two = both_ways(term(here - 1, 0).astype(BF), term(here + 1, 1).astype(BF), count)
-    grad_product = dot(grad_rows, full_down, 1, 1)
-    grad_gated = (
-        grad_product * up_values * sigmoid_gate * (1.0 + gate_values * (1.0 - sigmoid_gate))
-    ).astype(BF)
-    grad_lifted = (grad_product * activated).astype(BF)
-    one, two, grad_gated, grad_lifted = after((one, two, grad_gated, grad_lifted))
-    one, two = add_terms(one, two, 1)
-    one, two = both_ways(one.astype(BF), two.astype(BF), count)
-    grad_down = dot(product, grad_rows, 0, 0).astype(BF)
-    grad_down, grad_gated, grad_lifted = after((grad_down, grad_gated, grad_lifted))
-    grad_down = lax.psum_scatter(grad_down, DP, scatter_dimension=1, tiled=True)
-    grad_gate = dot(normed_two, grad_gated, 0, 0).astype(BF)
-    grad_up = dot(normed_two, grad_lifted, 0, 0).astype(BF)
-    grad_gate, grad_up, grad_gated, grad_lifted = after((grad_gate, grad_up, grad_gated, grad_lifted))
-    grad_gate = lax.psum_scatter(grad_gate, DP, scatter_dimension=0, tiled=True)
-    grad_up = lax.psum_scatter(grad_up, DP, scatter_dimension=0, tiled=True)
-    part = (dot(grad_gated, full_gate, 1, 1) + dot(grad_lifted, full_up, 1, 1)).astype(BF)
-    one, two, part = after((one, two, part))
-    one, two = add_terms(one, two, 2)
+    part, grad_wide, block_out = mlp(normed_two, grad_out, residual, early, full_gate, full_up, full_down, 5, 4, count)
+    grad_wide = lax.psum_scatter(grad_wide, DP, scatter_dimension=0, tiled=True)
     wide = jax.ShapeDtypeStruct((rows, width), F32)
     grad_residual, terms_two, grad_low = sum_and_finish(
         part, normed_two, (residual, grad_out, gain_two), (wide,), finish_residual, True, False, 3, 16, count, plane
     )
-    for step in range(3, count - 1):
-        one, two = both_ways(one.astype(BF), two.astype(BF), count)
-        one, two = add_terms(one, two, step)
     grad_low = grad_low.reshape(count * rows, width)
-    one, two, grad_low, grad_down, grad_gate = after((one.astype(BF), two.astype(BF), grad_low, grad_down, grad_gate))
-    one, two = both_ways(one, two, count)
     grad_mixed = dot(full_out, grad_low, 1, 1).astype(BF)
-    grad_out_proj = lax.psum_scatter(dot(mixed, grad_low, 1, 0).astype(BF), DP, scatter_dimension=1, tiled=True)
+    grad_out_proj = dot(grad_low, mixed, 0, 1).astype(BF)
     turned = attend_back(q, kt, k, v, lse, grad_mixed, cosine, sine, segments, heads, groups)
-    grad_mix = dot(normed_one, turned, 0, 1).astype(BF)
-    one, two, turned, grad_mix = after((one, two, turned, grad_mix))
+    grad_mix = jnp.concatenate([dot(normed_one, turned, 0, 1).astype(BF), grad_out_proj], 1)
+    turned, grad_mix, grad_wide = after((turned, grad_mix, grad_wide))
     grad_mix = lax.psum_scatter(grad_mix, DP, scatter_dimension=0, tiled=True)
-    one, two = add_terms(one, two, count - 1)
-    block_out = (residual + jnp.concatenate([one, two], 0)).astype(BF)
-    part = dot(turned, mix, 0, 1).astype(BF)
-    part, grad_up = after((part, grad_up))
+    part = dot(turned, mix, 0, 0).astype(BF)
     grad_tokens, sums = sum_and_finish(
         part, normed_one, (tokens, grad_residual, gain_one, terms_two), (wide,), finish_tokens, False, True, 4, 4, count, plane
     )
     sums = jnp.sum(sums.reshape(2, 8, -1), 1)
-    edges = (heads * HD, (heads + groups) * HD)
-    grad_query, grad_key, grad_value = jnp.split(grad_mix.astype(F32), edges, 1)
+    edges = (heads * HD, (heads + groups) * HD, (heads + 2 * groups) * HD)
+    grad_query, grad_key, grad_value, grad_out_proj = jnp.split(grad_mix.astype(F32), edges, 1)
+    grad_gate, grad_up, grad_down = jnp.split(grad_wide.astype(F32), 3, 1)
     return (
         block_out,
         grad_tokens,
@@ -606,11 +772,11 @@
         grad_query,
         grad_key,
         grad_value,
-        grad_out_proj.astype(F32),
+        grad_out_proj.T,
         sums[1] / mlp_gain.astype(F32),
-        grad_gate.astype(F32),
-        grad_up.astype(F32),
-        grad_down.astype(F32),
+        grad_gate,
+        grad_up,
+        grad_down.T,
     )
 
 

time: 718 us -> 671 us (0.935)
  matrix products: 168 us -> 19.5 us
  Pallas kernels: 457 us -> 602 us
  starting transfers between devices: 21 us -> 0.27 us
  other arithmetic: 22.8 us -> 6.54 us
    pallas_call x1 -> x2, Pallas kernels: 20.8 us -> 172 us  [the longest x1 117 us: mlp(): pl.pallas_call(functools.partial(mlp_kernel, count, pieces, tile), grid=(...]
    dot_general x15 -> x4, matrix products: 168 us -> 19.5 us  [dot(): lax.dot_general(left_side, right_side, (((left_dim,), (right_dim,)), ((),...]
    ppermute x12 -> x0, starting transfers between devices: 20.5 us -> none  [both_ways(): return (lax.ppermute(one, AXIS, right), lax.ppermute(two, AXIS, left))]
    convert_element_type x8 -> x2, other arithmetic: 17.1 us -> 0.82 us  [the longest x1 0.73 us: body(): grad_gate, grad_up, grad_down = jnp.split(grad_wide.astype(F32), 3, 1)]
    dynamic_update_slice x7 -> x0, local copies, waits for them, and re-layouts: 9.85 us -> none  [the longest x3 5.11 us: place(): lax.dynamic_update_slice(whole, two[None], ((here + step) % count, half, 0))]
    unnamed x53 -> x63, local copies, waits for them, and re-layouts: 4.48 us -> 13.3 us
    pallas_call x1, Pallas kernels: 82.5 us -> 74.9 us  [norm_and_gather(): pl.pallas_call(functools.partial(norm_kernel, count, plane, pieces), out_...]
  transfers between devices with their start and end apart: 22 -> 7, of which waited for: 0 -> 0; matrix products, arithmetic and copies ran while one was open for 29% -> 6% of each run, Pallas kernels for 64% -> 73%
where the time goes in v3:
time: 671 us; the launch traced here: 668 us
  Pallas kernels  602 us (90%)
  local copies, waits for them, and re-layouts  21.8 us (3%)
  matrix products  19.5 us (3%)
  between operations  14.8 us (2%)
    pallas_call x3, Pallas kernels, sum_and_finish(): pl.pallas_call(functools.partial(turn_over, finish, n, plane, pieces, len...  327 us
    pallas_call x1, Pallas kernels, mlp(): pl.pallas_call(functools.partial(mlp_kernel, count, pieces, tile), grid=(...  117 us
    pallas_call x1, Pallas kernels, norm_and_gather(): pl.pallas_call(functools.partial(norm_kernel, count, plane, pieces), out_...  74.9 us
    pallas_call x1, Pallas kernels, attend(): pl.pallas_call(functools.partial(attend_kernel, heads, groups, block, cou...  54.7 us
    pallas_call x1, Pallas kernels, attend_back(): pl.pallas_call(functools.partial(attend_back_kernel, heads, groups, block...  28.5 us
    dot_general x4, matrix products, dot(): lax.dot_general(left_side, right_side, (((left_dim,), (right_dim,)), ((),...  19.5 us
  transfers between devices with their start and end apart: 7, of which 0 were waited for; matrix products, arithmetic and copies ran while one was open for 6% of the time, Pallas kernels for 73%

profile of v3, /device:TPU:0, one launch (start us, length us, event | category | flops | bytes accessed | tf_op | source)
XLA Modules:
  0.0 668.0 jit_solution(6559124220758708405)
XLA Ops:
  7.2 0.0 all-gather.8.cloned.1.call-start
  7.3 0.7 all-gather.8.cloned.1.call-update
  8.0 0.0 all-gather.6.cloned.1.call-start
  8.0 0.9 copy.33
  9.0 0.9 copy.34
  9.9 1.1 copy.32
  11.0 0.8 maximum_bitcast_fusion
  11.8 0.0 all-gather.10.cloned.1.call-start
  11.8 0.7 all-gather.10.cloned.1.call-update
  12.5 0.0 all-gather.12.cloned.1.call-start
  12.6 0.5 all-gather.12.cloned.1.call-update
  13.1 0.0 all-gather.14.cloned.1.call-start
  13.2 0.5 all-gather.14.cloned.1.call-update
  13.7 0.0 reduce-scatter.3.cloned.1.call-start
  13.8 1.0 copy.35.segc_ref
  14.9 74.9 %shard_map.212 = (bf16[4,256,2048]{2,1,0:T(8,128)(2,1)S(1)}, f32[8,2048]{1,0:T(8,128)S(1)}) custom-call(bf16[256,2048]{1,0:T(8,128)(2,1)S(1)} %copy-done, f32[8,256]{1,0:T(8,128)S(1)} %fusion.4.gains_ref), custom_call_target="tpu_custom_call" | custom-call | bytes 270000000 | tf_op jit(solution)/shard_map/pallas_call | solution.py:651
  89.8 2.1 copy-done.1
  91.9 1.2 multiply_sine_fusion
  93.1 0.6 fusion.7
  93.7 54.7 %shard_map.213 = (bf16[512,1024]{1,0:T(8,128)(2,1)}, f32[8,1,1024]{2,1,0:T(1,128)}, bf16[512,1024]{1,0:T(8,128)(2,1)}, bf16[128,1024]{1,0:T(8,128)(2,1)}, bf16[2...) custom-call(bf16[768,2048]{1,0:T(8,128)(2,1)} %all-gather.6.cloned.1, ...), custom_call_target="tpu_custom_call" | custom-call | flops 30000001024 | bytes 130000000 | tf_op jit(solution)/shard_map/pallas_call | solution.py:107
  148.5 121.1 %shard_map.214 = (f32[256,2048]{1,0:T(8,128)}, f32[8,2048]{1,0:T(8,128)}, bf16[4,256,2048]{2,1,0:T(8,128)(2,1)}) custom-call(bf16[4,256,2048]{2,1,0:T(8,128)(2,1)} %bitcast.33, bf16[4,256,2048]{2,1,0:T(8,128)(2,1)} %bitcast.34, bf16[256,2048]{1,0:T(8,128)(2,1)} %refs_2_.3, f32[1,2048]{1,0:T(1,128)} %get-tuple-element.84.refs_3_.refs_4_), custom_call_target="tpu_custom_call" | custom-call | bytes 270000000 | tf_op jit(solution)/shard_map/pallas_call | solution.py:418
  269.6 0.0 all-gather.10.cloned.1.call-done.wg_hbm
  269.6 0.0 all-gather.12.cloned.1.call-done.wu_hbm
  269.7 117.2 %shard_map.215 = (bf16[1024,2048]{1,0:T(8,128)(2,1)}, bf16[2048,6144]{1,0:T(8,128)(2,1)}, bf16[256,2048]{1,0:T(8,128)(2,1)}) custom-call(bf16[1024,2048]{1,0:T(8,128)(2,1)} %bitcast.35, bf16[256,2048]{1,0:T(8,128)(2,1)} %refs_3_.1, f32[256,2048]{1,0:T(8,128)} %get-tuple-element.38.res_ref.refs_2_, bf16[4,128,2048]{2,1,0:T(8,128)(2,1)} %get-tuple-element.39.early_hbm, ...), custom_call_target="tpu_custom_call" | custom-call | flops 77999996928 | bytes 380000000 | tf_op jit(solution)/shard_map/pallas_call | solution.py:583
  386.9 0.0 reduce-scatter.5.cloned.1.call-start
  387.0 127.4 %shard_map.216 = (f32[256,2048]{1,0:T(8,128)}, f32[8,2048]{1,0:T(8,128)}, bf16[4,256,2048]{2,1,0:T(8,128)(2,1)}) custom-call(bf16[4,256,2048]{2,1,0:T(8,128)(2,1)} %bitcast.36, bf16[4,256,2048]{2,1,0:T(8,128)(2,1)} %get-tuple-element.37.refs_1_, f32[256,2048]{1,0:T(8,128)} %get-tuple-element.38.res_ref.refs_2_, bf16[256,2048]{1,0:T(8,128)(2,1)} %refs_3_.1, ...), custom_call_target="tpu_custom_call" | custom-call | bytes 270000000 | tf_op jit(solution)/shard_map/pallas_call | solution.py:418
  514.4 6.3 convolution_convert_fusion.2
  520.8 2.4 fusion.gm_ref
  523.3 28.5 %shard_map.217 = bf16[768,1024]{1,0:T(8,128)(2,1)S(1)} custom-call(bf16[512,1024]{1,0:T(8,128)(2,1)S(1)} %copy-done.8, bf16[128,1024]{1,0:T(8,128)(2,1)S(1)} %copy-done.11, bf16[2,1024,64]{2,1,0:T(8,128)(2,1)S(1)} %copy-done.9, bf16[2,1024,64]{2,1,0:T(8,128)(2,1)S(1)} %copy-done.10, f32[8,1,1024]{2,1,0:T(1,128)S(1)} %copy-done.12, ...), custom_call_target="tpu_custom_call" | custom-call | flops 60000002048 | bytes 10000000 | tf_op jit(solution)/shard_map/pallas_call | solution.py:169
  551.8 3.7 convolution_convert_fusion.1
  555.5 3.1 pad_maximum_fusion
  558.6 7.1 %convolution_convert_fusion = bf16[1024,2048]{1,0:T(8,128)(2,1)} fusion(bf16[768,1024]{1,0:T(8,128)(2,1)S(1)} %shard_map.217, bf16[768,2048]{1,0:T(8,128)(2,1)} %all-gather.6.cloned.1.call-done.mix_ref), kind=kOutput, calls=%fused_computation.1 | convolution fusion | flops 3223322624 | bytes 8912896 | tf_op jit(solution)/shard_map/dot_general | solution.py:609
  565.8 78.6 %shard_map.218 = (f32[256,2048]{1,0:T(8,128)}, f32[16,256]{1,0:T(8,128)}) custom-call(bf16[4,256,2048]{2,1,0:T(8,128)(2,1)} %bitcast.37, bf16[4,256,2048]{2,1,0:T(8,128)(2,1)} %copy-done.1, bf16[256,2048]{1,0:T(8,128)(2,1)} %refs_2_.3, f32[256,2048]{1,0:T(8,128)} %get-tuple-element.51.refs_3_, f32[1,2048]{1,0:T(1,128)} %get-tuple-element.83.refs_4_, ...), custom_call_target="tpu_custom_call" | custom-call | bytes 270000000 | tf_op jit(solution)/shard_map/pallas_call | solution.py:418
  644.4 0.7 convert_element_type.39
  645.1 1.6 slice_bitcast_fusion
  646.7 2.9 copy.41
  649.6 0.6 convert_divide_fusion
  650.2 2.5 fusion.5
  652.8 1.0 fusion.6
  653.7 0.8 copy.40
  654.5 0.8 copy.39
  655.2 1.0 split.28
  656.2 1.0 copy.38
  657.2 0.1 convert_element_type.37
  657.3 0.8 slice_bitcast_fusion.1
  658.2 0.5 copy-done.17
  658.6 1.0 copy.45
  659.6 1.3 copy.46
  (67 shorter events, 0.3 us)
Async XLA Ops:
  7.2 6.6 copy-start.22
  7.2 6.6 copy-start.20
  7.2 6.6 copy-start.19
  7.2 6.6 copy-start.6
  7.2 7.6 %copy-start = (bf16[256,2048]{1,0:T(8,128)(2,1)S(1)}, bf16[256,2048]{1,0:T(8,128)(2,1)}, u32[]{:S(2)}) copy-start(bf16[256,2048]{1,0:T(8,128)(2,1)} %refs_2_.3) | copy-start | bytes 3145732
  7.2 86.5 %all-gather.8.cloned.1.call-start = ((), (), s32[]{:S(2)}) async-start(), calls=%async_computation.3 | async-start | bytes 2359296 | tf_op jit(solution)/shard_map/all_gather | solution.py:728
  8.0 85.8 %all-gather.6.cloned.1.call-start = ((), (), s32[]{:S(2)}) async-start(), calls=%async_computation.2 | async-start | bytes 3538944 | tf_op jit(solution)/shard_map/all_gather | solution.py:727
  11.8 257.8 %all-gather.10.cloned.1.call-start = ((), (), s32[]{:S(2)}) async-start(), calls=%async_computation.4 | async-start | bytes 9437184 | tf_op jit(solution)/shard_map/all_gather | solution.py:729
  12.5 257.1 %all-gather.12.cloned.1.call-start = ((), (), s32[]{:S(2)}) async-start(), calls=%async_computation.5 | async-start | bytes 9437184 | tf_op jit(solution)/shard_map/all_gather | solution.py:730
  13.1 256.6 %all-gather.14.cloned.1.call-start = ((), (), s32[]{:S(2)}) async-start(), calls=%async_computation.6 | async-start | bytes 9437184 | tf_op jit(solution)/shard_map/all_gather | solution.py:731
  13.7 544.9 %reduce-scatter.3.cloned.1.call-start = ((), (), s32[]{:S(2)}) async-start(), calls=%async_computation.7 | async-start | bytes 28311552 | tf_op jit(solution)/shard_map/reduce_scatter | solution.py:748
  89.8 2.1 copy-start.1
  386.9 265.8 %reduce-scatter.5.cloned.1.call-start = ((), (), s32[]{:S(2)}) async-start(), calls=%async_computation.8 | async-start | bytes 5898240 | tf_op jit(solution)/shard_map/reduce_scatter | solution.py:759
  387.0 127.4 %copy-start.26 = (bf16[512,1024]{1,0:T(8,128)(2,1)S(1)}, bf16[512,1024]{1,0:T(8,128)(2,1)}, u32[]{:S(2)}) copy-start(bf16[512,1024]{1,0:T(8,128)(2,1)} %get-tuple-element.48) | copy-start | bytes 3145732
  514.4 6.3 copy-start.24
  514.4 6.3 copy-start.25
  520.7 2.5 copy-start.3
  520.7 2.5 copy-start.4
  520.7 2.5 copy-start.5
  520.8 2.5 copy-start.7
  520.8 2.5 copy-start.8
  520.8 2.5 copy-start.9
  520.8 2.5 copy-start.10
  520.8 2.5 copy-start.11
  520.8 2.5 copy-start.12
  523.3 28.5 %copy-start.2 = (bf16[4,256,2048]{2,1,0:T(8,128)(2,1)S(1)}, bf16[4,256,2048]{2,1,0:T(8,128)(2,1)}, u32[]{:S(2)}) copy-start(bf16[4,256,2048]{2,1,0:T(8,128)(2,1)} %copy-done.1) | copy-start | bytes 12582916
  551.8 3.7 copy-start.15
  565.8 78.6 %copy-start.13 = (bf16[256,6144]{1,0:T(8,128)(2,1)S(1)}, bf16[256,6144]{1,0:T(8,128)(2,1)}, u32[]{:S(2)}) copy-start(bf16[256,6144]{1,0:T(8,128)(2,1)} %reduce-scatter.3.cloned.1.call-done) | copy-start | bytes 9437188
  646.7 2.9 copy-start.18
  646.7 3.0 copy-start.21
  646.7 3.0 copy-start.23
  652.8 4.5 copy-start.14
  656.2 3.4 copy-start.16
  657.2 1.4 copy-start.17
Sparse Core Ops, SparseCore 0:
  9.9 30.8 all-gather.7
  43.3 32.8 all-gather.5
  78.1 54.5 all-gather.9
  134.5 54.4 all-gather.11
  190.7 55.9 all-gather.13
  387.1 165.0 reduce-scatter.2
  558.8 55.0 reduce-scatter.4
